TPU v7x, 32 devices: a whole 2x2x4 slice. The times are simulated.
32 devices in a mesh: seq: 8 (over y, x, core), batch: 4 (over z).
Axes of the slice: x: 2, y: 2, z: 4, core: 2. Of those that a mesh axis runs over, the one named last changes fastest.
Arguments:
- tokens: bfloat16 [4, 4096, 768], P('batch', 'seq'), may hold values from -6 to 6
- norm1_gain: float32 [768], replicated, may hold values from 0.5 to 1.5
- norm1_bias: float32 [768], replicated, may hold values from -1.75 to 1.75
- query_weight: bfloat16 [768, 768], replicated, may hold values from -0.21875 to 0.21875
- key_weight: bfloat16 [768, 768], replicated, may hold values from -0.21875 to 0.21875
- value_weight: bfloat16 [768, 768], replicated, may hold values from -0.21875 to 0.21875
- shift_taps: float32 [4, 768], replicated, may hold values from -3 to 3
- ssm_coef: float32 [64, 768], replicated, may hold values from -0.0234375 to 0.0234375
- ssm_rate: float32 [64, 768], replicated, may hold values from 3e-05 to 0.04
- ssm_skip: float32 [768], replicated, may hold values from -6 to 6
- out_weight: bfloat16 [768, 768], replicated, may hold values from -0.21875 to 0.21875
- norm2_gain: float32 [768], replicated, may hold values from 0.5 to 1.5
- norm2_bias: float32 [768], replicated, may hold values from -1.75 to 1.75
- up_weight: bfloat16 [768, 3072], replicated, may hold values from -0.21875 to 0.21875
- down_weight: bfloat16 [3072, 768], replicated, may hold values from -0.109375 to 0.109375
- out_grad: bfloat16 [4, 4096, 768], P('batch', 'seq'), may hold values from -6 to 6
Outputs:
- mixed_out: bfloat16 [4, 4096, 768], P('batch', 'seq')
- tokens_grad: float32 [4, 4096, 768], P('batch', 'seq')
- norm1_gain_grad: float32 [768], replicated
- norm1_bias_grad: float32 [768], replicated
- query_weight_grad: float32 [768, 768], replicated
- key_weight_grad: float32 [768, 768], replicated
- value_weight_grad: float32 [768, 768], replicated
- shift_taps_grad: float32 [4, 768], replicated
- ssm_coef_grad: float32 [64, 768], replicated
- ssm_rate_grad: float32 [64, 768], replicated
- ssm_skip_grad: float32 [768], replicated
- out_weight_grad: float32 [768, 768], replicated
- norm2_gain_grad: float32 [768], replicated
- norm2_bias_grad: float32 [768], replicated
- up_weight_grad: float32 [768, 3072], replicated
- down_weight_grad: float32 [3072, 768], replicated
All inputs are finite; a program needn't handle non-finite values.
Results may differ from a plain program's by a relative error of at most 0.0077.
Values sent between devices are 32-bit elements; how exact they have to be, the bound alone decides.
A program may use at most 256 MiB of HBM per device.

v0:
```python
from functools import partial
import math

import jax
import jax.numpy as jnp
from jax import lax
from jax.sharding import PartitionSpec as P

epsilon = 1e-05
highest = lax.Precision.HIGHEST


def passed_along(value, axis, steps):
    count = lax.axis_size(axis)
    leading, last = (max(0, -steps), min(count, count - steps))
    return lax.ppermute(value, axis, [(source, source + steps) for source in range(leading, last)])


def layer_norm(values, norm_gain, norm_bias):
    row_mean = jnp.mean(values, axis=-1, keepdims=True)
    centered = values - row_mean
    spread = jnp.mean(centered * centered, axis=-1, keepdims=True)
    return centered * lax.rsqrt(spread + epsilon) * norm_gain + norm_bias


def kernel_table(state_coef, state_rate, positions):
    channels = state_coef.shape[1]
    coef_blocks = state_coef.reshape(-1, 8, channels)
    rate_blocks = state_rate.reshape(-1, 8, channels)

    def add_block(running, members):
        decays = jnp.exp(-members[1][None] * positions[:, None, None])
        return (running + jnp.sum(members[0][None] * decays, axis=1), None)

    initial = jnp.zeros((positions.shape[0], channels), state_coef.dtype)
    running, unused = lax.scan(jax.checkpoint(add_block), initial, (coef_blocks, rate_blocks))
    return running


def phase_table(row_index, col_index, modulus):
    product = row_index[:, None] * col_index[None, :] % modulus
    angles = 2.0 * math.pi / modulus * product.astype(jnp.float32)
    return (jnp.cos(angles), jnp.sin(angles))


def project(rows_low, weight):
    return jnp.einsum("bsd,de->bse", rows_low, weight, preferred_element_type=jnp.float32)


def project_back(grads_low, weight):
    return jnp.einsum("bse,de->bsd", grads_low, weight, preferred_element_type=jnp.float32)


def weight_grad(rows_low, grads_low):
    return jnp.einsum("bsd,bse->de", rows_low, grads_low, preferred_element_type=jnp.float32)


def to_spectrum(stacked):
    devices = lax.axis_size("seq")
    my_index = lax.axis_index("seq")
    row_count = stacked.shape[1]
    piece_rows = row_count // devices
    coarse = 2 * devices
    length = coarse * row_count
    spread = lax.all_to_all(stacked[:, None], "seq", split_axis=2, concat_axis=1, tiled=True)
    cos_one, sin_one = phase_table(jnp.arange(coarse), jnp.arange(devices), coarse)
    real_one = jnp.einsum("kc,bcfd->bkfd", cos_one, spread, precision=highest)
    imag_one = -jnp.einsum("kc,bcfd->bkfd", sin_one, spread, precision=highest)
    local_rows = my_index * piece_rows + jnp.arange(piece_rows)
    cos_turn, sin_turn = phase_table(jnp.arange(coarse), local_rows, length)
    cos_turn = cos_turn[None, :, :, None]
    sin_turn = sin_turn[None, :, :, None]
    real_two = real_one * cos_turn + imag_one * sin_turn
    imag_two = imag_one * cos_turn - real_one * sin_turn
    turned = lax.all_to_all(
        jnp.stack([real_two, imag_two], 1), "seq", split_axis=2, concat_axis=3, tiled=True
    )
    cos_row, sin_row = phase_table(jnp.arange(row_count), jnp.arange(row_count), row_count)
    real_in = turned[:, 0]
    imag_in = turned[:, 1]
    real_out = jnp.einsum("kf,bjfd->bjkd", cos_row, real_in, precision=highest) + jnp.einsum(
        "kf,bjfd->bjkd", sin_row, imag_in, precision=highest
    )
    imag_out = jnp.einsum("kf,bjfd->bjkd", cos_row, imag_in, precision=highest) - jnp.einsum(
        "kf,bjfd->bjkd", sin_row, real_in, precision=highest
    )
    return (real_out, imag_out)


def from_spectrum(real_in, imag_in):
    devices = lax.axis_size("seq")
    my_index = lax.axis_index("seq")
    row_count = real_in.shape[2]
    coarse = 2 * devices
    per_device = coarse // devices
    length = coarse * row_count
    cos_row, sin_row = phase_table(jnp.arange(row_count), jnp.arange(row_count), row_count)
    real_mid = jnp.einsum("fk,bjkd->bjfd", cos_row, real_in, precision=highest) - jnp.einsum(
        "fk,bjkd->bjfd", sin_row, imag_in, precision=highest
    )
    imag_mid = jnp.einsum("fk,bjkd->bjfd", cos_row, imag_in, precision=highest) + jnp.einsum(
        "fk,bjkd->bjfd", sin_row, real_in, precision=highest
    )
    local_freq = my_index * per_device + jnp.arange(per_device)
    cos_turn, sin_turn = phase_table(local_freq, jnp.arange(row_count), length)
    cos_turn = cos_turn[None, :, :, None]
    sin_turn = sin_turn[None, :, :, None]
    real_two = real_mid * cos_turn - imag_mid * sin_turn
    imag_two = real_mid * sin_turn + imag_mid * cos_turn
    merged = lax.all_to_all(
        jnp.stack([real_two, imag_two], 1), "seq", split_axis=3, concat_axis=2, tiled=True
    )
    cos_one, sin_one = phase_table(jnp.arange(devices), jnp.arange(coarse), coarse)
    time_rows = jnp.einsum("ck,bkfd->bcfd", cos_one, merged[:, 0], precision=highest) - jnp.einsum(
        "ck,bkfd->bcfd", sin_one, merged[:, 1], precision=highest
    )
    time_rows = time_rows * (1.0 / length)
    restored = lax.all_to_all(time_rows, "seq", split_axis=1, concat_axis=2, tiled=True)
    return restored[:, 0]


def on_device(
    tokens,
    norm1_gain,
    norm1_bias,
    query_weight,
    key_weight,
    value_weight,
    shift_taps,
    ssm_coef,
    ssm_rate,
    ssm_skip,
    out_weight,
    norm2_gain,
    norm2_bias,
    up_weight,
    down_weight,
    out_grad,
):
    seq_count = tokens.shape[0]
    row_count = tokens.shape[1]
    my_index = lax.axis_index("seq")
    inputs = tokens.astype(jnp.float32)
    normed_one, norm_one_pull = jax.vjp(layer_norm, inputs, norm1_gain, norm1_bias)
    normed_low = normed_one.astype(jnp.bfloat16)
    queries = project(normed_low, query_weight)
    key_rows = project(normed_low, key_weight)
    value_rows = project(normed_low, value_weight)
    tap_count = shift_taps.shape[0]
    prev_rows = passed_along(key_rows[:, row_count - tap_count + 1 :], "seq", 1)
    extended = jnp.concatenate([prev_rows, key_rows], 1)
    keys_mixed = jnp.zeros_like(key_rows)
    for offset in range(tap_count):
        lead_rows = tap_count - 1 - offset
        keys_mixed = (
            keys_mixed + shift_taps[offset] * extended[:, lead_rows : lead_rows + row_count]
        )
    product = keys_mixed * value_rows
    positions = (my_index * row_count + jnp.arange(row_count)).astype(jnp.float32)
    kernel, kernel_pull = jax.vjp(partial(kernel_table, positions=positions), ssm_coef, ssm_rate)
    spec_real, spec_imag = to_spectrum(jnp.concatenate([product, kernel[None]], 0))
    sig_real = spec_real[:seq_count]
    sig_imag = spec_imag[:seq_count]
    ker_real = spec_real[seq_count:]
    ker_imag = spec_imag[seq_count:]
    mixed_rows = (
        from_spectrum(
            sig_real * ker_real - sig_imag * ker_imag, sig_real * ker_imag + sig_imag * ker_real
        )
        + ssm_skip * product
    )
    gated_rows = (queries * mixed_rows).astype(jnp.bfloat16)
    attended = project(gated_rows, out_weight)
    middle = inputs + attended
    normed_two, norm_two_pull = jax.vjp(layer_norm, middle, norm2_gain, norm2_bias)
    normed_two_low = normed_two.astype(jnp.bfloat16)
    hidden_pre = project(normed_two_low, up_weight)
    activated, gelu_pull = jax.vjp(jax.nn.gelu, hidden_pre)
    activated_low = activated.astype(jnp.bfloat16)
    mixed_out = (middle + project(activated_low, down_weight)).astype(jnp.bfloat16)
    grad_down = weight_grad(activated_low, out_grad)
    grad_act = project_back(out_grad, down_weight)
    grad_hidden = gelu_pull(grad_act)[0].astype(jnp.bfloat16)
    grad_up = weight_grad(normed_two_low, grad_hidden)
    grad_normed_two = project_back(grad_hidden, up_weight)
    grad_middle, grad_gain_two, grad_bias_two = norm_two_pull(grad_normed_two)
    grad_middle = grad_middle + out_grad.astype(jnp.float32)
    grad_attended = grad_middle.astype(jnp.bfloat16)
    grad_out_weight = weight_grad(gated_rows, grad_attended)
    grad_gated = project_back(grad_attended, out_weight)
    grad_queries = (grad_gated * mixed_rows).astype(jnp.bfloat16)
    grad_mixed = grad_gated * queries
    all_real, all_imag = to_spectrum(jnp.concatenate([product, kernel[None], grad_mixed], 0))
    sig_real = all_real[:seq_count]
    sig_imag = all_imag[:seq_count]
    ker_real = all_real[seq_count : seq_count + 1]
    ker_imag = all_imag[seq_count : seq_count + 1]
    grd_real = all_real[seq_count + 1 :]
    grd_imag = all_imag[seq_count + 1 :]
    back_real = ker_real * grd_real + ker_imag * grd_imag
    back_imag = ker_real * grd_imag - ker_imag * grd_real
    kern_real = jnp.sum(sig_real * grd_real + sig_imag * grd_imag, axis=0, keepdims=True)
    kern_imag = jnp.sum(sig_real * grd_imag - sig_imag * grd_real, axis=0, keepdims=True)
    returned = from_spectrum(
        jnp.concatenate([back_real, kern_real], 0), jnp.concatenate([back_imag, kern_imag], 0)
    )
    grad_product = returned[:seq_count] + ssm_skip * grad_mixed
    grad_kernel = returned[seq_count]
    grad_skip = jnp.sum(grad_mixed * product, axis=(0, 1))
    grad_coef, grad_rate = kernel_pull(grad_kernel)
    grad_keys_mixed = grad_product * value_rows
    grad_values = (grad_product * keys_mixed).astype(jnp.bfloat16)
    next_rows = passed_along(grad_keys_mixed[:, : tap_count - 1], "seq", -1)
    grad_extended = jnp.concatenate([grad_keys_mixed, next_rows], 1)
    grad_keys = jnp.zeros_like(grad_keys_mixed)
    tap_terms = []
    for offset in range(tap_count):
        lead_rows = tap_count - 1 - offset
        grad_keys = grad_keys + shift_taps[offset] * grad_extended[:, offset : offset + row_count]
        tap_terms.append(
            jnp.sum(grad_keys_mixed * extended[:, lead_rows : lead_rows + row_count], axis=(0, 1))
        )
    grad_taps = jnp.stack(tap_terms)
    grad_keys = grad_keys.astype(jnp.bfloat16)
    grad_query_weight = weight_grad(normed_low, grad_queries)
    grad_key_weight = weight_grad(normed_low, grad_keys)
    grad_value_weight = weight_grad(normed_low, grad_values)
    grad_normed = (
        project_back(grad_queries, query_weight)
        + project_back(grad_keys, key_weight)
        + project_back(grad_values, value_weight)
    )
    grad_inputs, grad_gain_one, grad_bias_one = norm_one_pull(grad_normed)
    grad_inputs = grad_inputs + grad_middle
    (
        grad_gain_one,
        grad_bias_one,
        grad_query_weight,
        grad_key_weight,
        grad_value_weight,
        grad_taps,
        grad_coef,
        grad_rate,
        grad_skip,
        grad_out_weight,
        grad_gain_two,
        grad_bias_two,
        grad_up,
        grad_down,
    ) = lax.psum(
        (
            grad_gain_one,
            grad_bias_one,
            grad_query_weight,
            grad_key_weight,
            grad_value_weight,
            grad_taps,
            grad_coef,
            grad_rate,
            grad_skip,
            grad_out_weight,
            grad_gain_two,
            grad_bias_two,
            grad_up,
            grad_down,
        ),
        ("seq", "batch"),
    )
    return (
        mixed_out,
        grad_inputs,
        grad_gain_one,
        grad_bias_one,
        grad_query_weight,
        grad_key_weight,
        grad_value_weight,
        grad_taps,
        grad_coef,
        grad_rate,
        grad_skip,
        grad_out_weight,
        grad_gain_two,
        grad_bias_two,
        grad_up,
        grad_down,
    )


def solution(mesh):
    placed = (
        P("batch", "seq", None),
        P(),
        P(),
        P(),
        P(),
        P(),
        P(),
        P(),
        P(),
        P(),
        P(),
        P(),
        P(),
        P(),
        P(),
        P("batch", "seq", None),
    )
    return jax.shard_map(
        on_device,
        mesh=mesh,
        in_specs=placed,
        out_specs=(
            P("batch", "seq", None),
            P("batch", "seq", None),
            P(),
            P(),
            P(),
            P(),
            P(),
            P(),
            P(),
            P(),
            P(),
            P(),
            P(),
            P(),
            P(),
            P(),
        ),
        check_vma=False,
    )
```

profile of v0, /device:TPU:0, one launch (start us, length us, event | category | flops | bytes accessed | tf_op | source)
XLA Modules:
  0.0 2123.0 jit_solution(17001349043243714272)
XLA Ops:
  17.2 69.3 %while.31 = (s32[]{:T(128)}, f32[512,768]{1,0:T(8,128)S(1)}, f32[8,8,768]{2,1,0:T(8,128)}, f32[8,8,768]{2,1,0:T(8,128)}, s32[]{:T(128)}, /*index=5*/s32[]{:T(128)}, s32[]{:T(128)}) while((s32[]{:T(128)}, f32[512,768]{1,0:T(8,128)S(1)}, f32[8,8,768]{2,1,0:T(8,128)}, f32[8,8,768]{2,1,0:T(8,128)}, s32[]{:T(128)}, ...), condition=%wide.region_4.5_spmd.clone, body=%wide.region_2.4_spmd.clone.sunk | while | flops 9837571 | bytes 6443111 | solution.py:36
  104.6 37.1 %all-to-all-done = f32[2,1,512,768]{3,0,1,2:T(2,128)} async-done(((f32[2,1,512,768]{3,0,1,2:T(2,128)}), f32[2,1,512,768]{3,0,1,2:T(2,128)}, u32[]{:S(2)}, u32[]{:S(2)}) %all-to-all-start) | async-done | bytes 3145760 | tf_op jit(solution)/shard_map/all_to_all | solution.py:65
  150.9 10.8 fusion.22
  161.7 10.4 pad_maximum_fusion.1
  172.1 16.4 copy.134
  194.3 138.6 %all-to-all-done.1 = f32[2,2,16,64,768]{4,3,0,1,2:T(8,128)} async-done(((f32[2,2,16,64,768]{4,3,0,1,2:T(8,128)}), f32[2,2,16,64,768]{4,3,0,1,2:T(8,128)}, u32[]{:S(2)}, u32[]{:S(2)}) %all-to-all-start.1) | async-done | bytes 12582944 | tf_op jit(solution)/shard_map/all_to_all | solution.py:75
  332.9 10.6 copy.136
  343.5 27.7 %fusion.25 = f32[2,2,768,512]{3,2,1,0:T(8,128)S(1)} fusion(f32[2,2,2,512,768]{4,3,2,1,0:T(8,128)} %bitcast.417), kind=kOutput, calls=%fused_computation.65 | convolution fusion | flops 9667346432 | bytes 12582912 | tf_op jit(solution)/shard_map/kf,bjfd->bjkd/dot_general | solution.py:84
  371.2 25.2 %fusion.26 = f32[2,2,768,512]{3,2,1,0:T(8,128)S(1)} fusion(f32[2,2,2,512,768]{4,3,2,1,0:T(8,128)S(1)} %bitcast.418), kind=kOutput, calls=%fused_computation.66 | convolution fusion | flops 9667346432 | bytes 12582912 | tf_op jit(solution)/shard_map/kf,bjfd->bjkd/dot_general | solution.py:81
  396.4 27.0 %subtract_bitcast_fusion.2 = f32[2,2,512,768]{2,3,1,0:T(8,128)} fusion(f32[2,2,768,512]{3,2,1,0:T(8,128)S(1)} %fusion.25, f32[2,2,2,512,768]{4,3,2,1,0:T(8,128)S(1)} %bitcast.419), kind=kOutput, calls=%fused_computation.63 | convolution fusion | flops 9668919296 | bytes 18874368 | tf_op jit(solution)/shard_map/kf,bjfd->bjkd/dot_general | solution.py:84
  423.5 27.4 %add_bitcast_fusion.2 = f32[2,2,512,768]{2,3,1,0:T(8,128)} fusion(f32[2,2,768,512]{3,2,1,0:T(8,128)S(1)} %fusion.26, f32[2,2,2,512,768]{4,3,2,1,0:T(8,128)S(1)} %bitcast.420), kind=kOutput, calls=%fused_computation.64 | convolution fusion | flops 9668919296 | bytes 18874368 | tf_op jit(solution)/shard_map/kf,bjfd->bjkd/dot_general | solution.py:81
  455.3 11.3 fusion.45
  466.6 11.3 fusion.43
  477.9 11.5 fusion.59
  489.4 11.7 fusion.40
  504.6 10.3 copy.139
  514.9 75.6 %all_to_all.114 = f32[1,2,2,512,768]{4,2,1,0,3:T(2,128)S(1)} all-to-all(f32[1,2,2,512,768]{4,2,1,0,3:T(2,128)} %copy.139), channel_id=1, replica_groups=mesh['seq'=8,'batch'=4] {'seq'}, dimensions={3} | all-to-all | bytes 12582912 | tf_op jit(solution)/shard_map/all_to_all | solution.py:110
  594.3 10.3 copy.141
  604.7 8.6 all_to_all.93
  630.1 17.7 all-to-all-done.3
  677.8 9.4 copy.143
  687.1 58.7 %all_to_all.115 = f32[3,1,512,768]{3,1,0,2:T(1,128)S(1)} all-to-all(f32[3,1,512,768]{3,1,0,2:T(1,128)} %copy.143), channel_id=1, replica_groups=mesh['seq'=8,'batch'=4] {'seq'}, dimensions={2} | all-to-all | bytes 9437184 | tf_op jit(solution)/shard_map/all_to_all | solution.py:65
  746.3 10.6 fusion.33
  756.9 14.8 fusion.5
  771.7 7.5 pad_maximum_fusion
  779.2 21.3 %copy.147 = f32[3,2,16,64,768]{4,3,0,1,2:T(8,128)} copy(f32[3,2,16,64,768]{4,2,3,0,1:T(8,128)S(1)} %pad_maximum_fusion) | data formatting | bytes 37748736 | tf_op jit(solution)/shard_map/stack | solution.py:76
  800.5 214.3 %all_to_all.116 = f32[3,2,16,64,768]{4,3,0,1,2:T(8,128)} all-to-all(f32[3,2,16,64,768]{4,3,0,1,2:T(8,128)} %copy.147), channel_id=1, replica_groups=mesh['seq'=8,'batch'=4] {'seq'}, dimensions={2} | all-to-all | bytes 37748736 | tf_op jit(solution)/shard_map/all_to_all | solution.py:75
  1022.2 41.5 %fusion.8 = f32[3,2,768,512]{3,2,1,0:T(8,128)} fusion(f32[3,2,2,512,768]{4,3,2,1,0:T(8,128)S(1)} %bitcast.413), kind=kOutput, calls=%fused_computation.32 | convolution fusion | flops 14499184640 | bytes 18874368 | tf_op jit(solution)/shard_map/kf,bjfd->bjkd/dot_general | solution.py:84
  1063.7 54.5 %fusion.9 = f32[3,2,768,512]{3,2,1,0:T(8,128)} fusion(f32[3,2,2,512,768]{4,3,2,1,0:T(8,128)S(1)} %bitcast.414), kind=kOutput, calls=%fused_computation.33 | convolution fusion | flops 14499184640 | bytes 18874368 | tf_op jit(solution)/shard_map/kf,bjfd->bjkd/dot_general | solution.py:81
  1118.2 42.2 %subtract_bitcast_fusion = f32[3,2,512,768]{2,3,1,0:T(8,128)} fusion(f32[3,2,768,512]{3,2,1,0:T(8,128)} %fusion.8, f32[3,2,2,512,768]{4,3,2,1,0:T(8,128)S(1)} %bitcast.415), kind=kOutput, calls=%fused_computation.28 | convolution fusion | flops 14501543936 | bytes 28311552 | tf_op jit(solution)/shard_map/kf,bjfd->bjkd/dot_general | solution.py:84
  1160.4 42.2 %add_bitcast_fusion = f32[3,2,512,768]{2,3,1,0:T(8,128)} fusion(f32[3,2,768,512]{3,2,1,0:T(8,128)} %fusion.9, f32[3,2,2,512,768]{4,3,2,1,0:T(8,128)S(1)} %bitcast.416), kind=kOutput, calls=%fused_computation.29 | convolution fusion | flops 14501543936 | bytes 28311552 | tf_op jit(solution)/shard_map/kf,bjfd->bjkd/dot_general | solution.py:81
  1202.6 7.8 multiply_add_fusion.1
  1210.4 16.0 fusion.29
  1226.4 16.1 fusion.30
  1242.5 16.3 fusion.31
  1258.8 21.9 %subtract_bitcast_fusion.1 = (f32[2,1,2,512,768]{3,4,2,0,1:T(8,128)}, f32[2,1,2,512,768]{3,4,2,0,1:T(8,128)}) fusion(f32[2,512]{1,0:T(2,128)S(1)} %copy-done.43, f32[2,512]{1,0:T(2,128)S(1)} %copy-done.41, f32[2,2,768,512]{3,2,1,0:T(8,128)} %fusion.29, f32[2,2,768,512]{3,2,1,0:T(8,128)} %fusion.31, f32[2,2,768,512]{3,2,1,0:T(8,128)} %fusion.30, ...), kind=kOutput, calls=%fused_computation.61 | convolution fusion | flops 9681502208 | bytes 37756928 | tf_op jit(solution)/shard_map/fk,bjkd->bjfd/dot_general | solution.py:98
  1280.7 10.7 pad_maximum_fusion.2
  1291.3 19.5 copy.152
  1310.8 145.9 %all_to_all.117 = f32[2,2,2,512,768]{4,2,0,1,3:T(2,128)} all-to-all(f32[2,2,2,512,768]{4,2,0,1,3:T(2,128)} %copy.152), channel_id=1, replica_groups=mesh['seq'=8,'batch'=4] {'seq'}, dimensions={3} | all-to-all | bytes 25165824 | tf_op jit(solution)/shard_map/all_to_all | solution.py:110
  1456.7 13.2 copy.153
  1469.9 22.0 %copy.154 = f32[2,2,8,2,64,768]{5,3,2,4,0,1:T(2,128)} copy(f32[2,2,8,2,64,768]{5,4,2,3,1,0:T(8,128)} %bitcast.426) | data formatting | bytes 25165824 | tf_op jit(solution)/shard_map/all_to_all | solution.py:110
  1491.9 15.8 all_to_all.104
  1543.7 20.8 all-to-all-done.7
  1574.3 58.8 %while.30 = (s32[]{:T(128)}, f32[512,768]{1,0:T(8,128)}, f32[8,8,768]{2,1,0:T(8,128)}, f32[8,8,768]{2,1,0:T(8,128)}, f32[8,8,768]{2,1,0:T(8,128)}, /*index=5*/f3...) while((s32[]{:T(128)}, f32[512,768]{1,0:T(8,128)}, f32[8,8,768]{2,1,0:T(8,128)}, ...), condition=%wide.region_26.27_spmd.clone, body=%wide.region_23.26_spmd.clone.sunk | while | flops 22021124 | bytes 1921153 | solution.py:36
  1649.5 10.2 fusion.87
  1669.4 43.4 %all-reduce = (f32[768]{0:T(1024)}, f32[768]{0:T(1024)}, f32[4,768]{1,0:T(4,128)}, f32[768]{0:T(1024)}, f32[768]{0:T(1024)}, /*index=5*/f32[768]{0:T(1024)}) all-reduce(f32[768]{0:T(1024)} %get-tuple-element.246, f32[768]{0:T(1024)} %reduce_sum.216, ...), channel_id=1, replica_groups=mesh['seq'=8,'batch'=4] {'seq','batch'}, use_global_device_ids=true, to_apply=%region_12.13 | all-reduce | flops 6912 | bytes 55296 | tf_op jit(solution)/shard_map/psum | solution.py:250
  1717.0 375.8 %all-reduce.4.cloned.1.call-done = (f32[768,768]{1,0:T(8,128)}, f32[768,768]{1,0:T(8,128)}, f32[768,768]{1,0:T(8,128)}, f32[64,768]{1,0:T(8,128)}, f32[64,768]{1...) async-done(((f32[768,768]{1,0:T(8,128)}, f32[768,768]{1,0:T(8,128)}, f32[768,768]{1,0:T(8,128)}, f32[64,768]{1,0:T(8,128)}, ...) | async-done | bytes 28704784 | tf_op jit(solution)/shard_map/psum | solution.py:250
  2102.9 9.3 copy.217
  (356 shorter events, 325.9 us)
Async XLA Ops:
  7.2 80.3 %copy-start = (bf16[768,768]{1,0:T(8,128)(2,1)S(1)}, bf16[768,768]{1,0:T(8,128)(2,1)}, u32[]{:S(2)}) copy-start(bf16[768,768]{1,0:T(8,128)(2,1)} %param.25) | copy-start | bytes 3538948
  8.6 618.1 %copy-start.44 = (f32[512]{0:T(512)}, f32[512]{0:T(512)S(1)}, u32[]{:S(2)}) copy-start(f32[512]{0:T(512)S(1)} %broadcast_multiply_fusion.1) | copy-start | bytes 6148
  10.7 76.8 %copy-start.50 = (f32[512]{0:T(512)}, f32[512]{0:T(512)S(1)}, u32[]{:S(2)}) copy-start(f32[512]{0:T(512)S(1)} %fusion.193) | copy-start | bytes 6148
  14.3 73.2 %collective-permute-start = (f32[1,3,768]{2,1,0:T(4,128)}, f32[1,3,768]{2,1,0:T(4,128)}, u32[]{:S(2)}, u32[]{:S(2)}) collective-permute-start(f32[1,3,768]{2,1,0:T(4,128)} %slice.141), channel_id=1, source_target_pairs={{0,4},{4,8},{8,12},{12,16},{16,20},{20,24},{24,28},{1,5},{5,9},{9,... | collective-permute-start | bytes 27656 | tf_op jit(solution)/shard_map/ppermute | solution.py:16
  17.2 70.3 %copy-start.5 = (bf16[1,512,768]{2,1,0:T(8,128)(2,1)S(1)}, bf16[1,512,768]{2,1,0:T(8,128)(2,1)}, u32[]{:S(2)}) copy-start(bf16[1,512,768]{2,1,0:T(8,128)(2,1)} %param.20) | copy-start | bytes 2359300
  17.2 70.3 %copy-start.48 = (f32[768]{0:T(1024)S(1)}, f32[768]{0:T(1024)}, u32[]{:S(2)}) copy-start(f32[768]{0:T(1024)} %param.21) | copy-start | bytes 9220
  87.4 5.8 copy-start.58
  87.5 5.8 copy-start.60
  87.5 5.8 copy-start.62
  87.5 5.8 copy-start.64
  98.7 43.0 %all-to-all-start = ((f32[2,1,512,768]{3,0,1,2:T(2,128)}), f32[2,1,512,768]{3,0,1,2:T(2,128)}, u32[]{:S(2)}, u32[]{:S(2)}) async-start(f32[2,1,512,768]{3,0,1,2:T(2,128)} %copy.130), calls=%async_computation | async-start | bytes 6291456 | tf_op jit(solution)/shard_map/all_to_all | solution.py:65
  143.8 7.0 copy-start.34
  143.8 7.0 copy-start.36
  188.5 144.4 %all-to-all-start.1 = ((f32[2,2,16,64,768]{4,3,0,1,2:T(8,128)}), f32[2,2,16,64,768]{4,3,0,1,2:T(8,128)}, u32[]{:S(2)}, u32[]{:S(2)}) async-start(f32[2,2,16,64,768]{4,3,0,1,2:T(8,128)} %copy.134), calls=%async_computation.1 | async-start | bytes 25165824 | tf_op jit(solution)/shard_map/all_to_all | solution.py:75
  194.3 295.1 %copy-start.40 = (f32[2,512]{1,0:T(2,128)}, f32[2,512]{1,0:T(2,128)S(1)}, u32[]{:S(2)}) copy-start(f32[2,512]{1,0:T(2,128)S(1)} %get-tuple-element.321) | copy-start | bytes 12292
  194.3 295.1 %copy-start.42 = (f32[2,512]{1,0:T(2,128)}, f32[2,512]{1,0:T(2,128)S(1)}, u32[]{:S(2)}) copy-start(f32[2,512]{1,0:T(2,128)S(1)} %get-tuple-element.322) | copy-start | bytes 12292
  343.5 27.7 %copy-start.1 = (f32[2,2,2,8,64,768]{5,4,3,2,1,0:T(8,128)S(1)}, f32[2,2,2,8,64,768]{5,4,3,2,1,0:T(8,128)}, u32[]{:S(2)}) copy-start(f32[2,2,2,8,64,768]{5,4,3,2,1,0:T(8,128)} %copy.136) | copy-start | bytes 37748740
  423.5 27.4 %copy-start.4 = (f32[2,2,512,768]{2,3,1,0:T(8,128)S(1)}, f32[2,2,512,768]{2,3,1,0:T(8,128)}, u32[]{:S(2)}) copy-start(f32[2,2,512,768]{2,3,1,0:T(8,128)} %subtract_bitcast_fusion.2) | copy-start | bytes 18874372
  620.8 6.0 copy-start.51
  622.4 25.3 %all-to-all-start.3 = ((f32[1,8,64,768]{3,2,0,1:T(8,128)}), f32[1,8,64,768]{3,2,0,1:T(8,128)}, u32[]{:S(2)}, u32[]{:S(2)}) async-start(f32[1,8,64,768]{3,2,0,1:T(8,128)} %copy.142), calls=%async_computation.3 | async-start | bytes 3145728 | tf_op jit(solution)/shard_map/all_to_all | solution.py:118
  626.7 21.0 copy-start.46
  650.6 6.9 slice-start.5
  651.5 15.9 copy-start.15
  651.5 15.9 copy-start.55
  651.8 15.6 copy-start.70
  651.8 5.7 copy-start.21
  651.8 5.7 slice-start.6
  651.9 12.1 slice-start.3
  657.5 6.4 copy-start.80
  657.5 6.4 slice-start.4
  746.3 10.6 copy-start.35
  746.3 10.6 copy-start.37
  1242.5 16.3 copy-start.41
  1242.5 16.3 copy-start.43
  1522.0 42.5 %all-to-all-start.7 = ((f32[2,8,64,768]{3,2,0,1:T(8,128)}), f32[2,8,64,768]{3,2,0,1:T(8,128)}, u32[]{:S(2)}, u32[]{:S(2)}) async-start(f32[2,8,64,768]{3,2,0,1:T(8,128)} %copy.155), calls=%async_computation.7 | async-start | bytes 6291456 | tf_op jit(solution)/shard_map/all_to_all | solution.py:118
  1526.6 566.2 %all-reduce.4.cloned.1.call-start = ((), (), s32[]{:S(2)}) async-start(), calls=%async_computation.8 | async-start | bytes 57409536 | tf_op jit(solution)/shard_map/psum | solution.py:250
  1526.7 11.3 slice-start.7
  1538.0 29.9 %copy-start.47 = (f32[768]{0:T(1024)S(1)}, f32[768]{0:T(1024)}, u32[]{:S(2)}) copy-start(f32[768]{0:T(1024)} %param.29) | copy-start | bytes 9220
  1571.6 66.8 %collective-permute-start.1 = (f32[1,3,768]{2,1,0:T(4,128)}, f32[1,3,768]{2,1,0:T(4,128)}, u32[]{:S(2)}, u32[]{:S(2)}) collective-permute-start(f32[1,3,768]{2,1,0:T(4,128)} %slice.165), channel_id=1, source_target_pairs={{4,0},{8,4},{12,8},{16,12},{20,16},{24,20},{28,24},{5,1},{9,5},{13... | collective-permute-start | bytes 27656 | tf_op jit(solution)/shard_map/ppermute | solution.py:16
  1649.4 10.3 copy-start.66
  1649.4 10.9 copy-start.69
  1649.4 11.4 copy-start.68
  1649.4 12.0 copy-start.67
  1649.4 12.6 copy-start.33
  1649.5 12.6 copy-start.75
  2101.5 10.7 slice-start
  2102.9 9.3 slice-start.1
  2102.9 9.3 slice-start.2
  (51 other events, 130.6 us)
Sparse Core Ops, SparseCore 0:
  1644.9 447.8 all-reduce.3
where the time goes:
time: 2130 us; the launch traced here: 2120 us
  waiting for transfers between devices  590 us (28%)
  blocking collectives  538 us (25%)
  matrix products  530 us (25%)
  local copies, waits for them, and re-layouts  233 us (11%)
  other arithmetic  192 us (9%)
  starting transfers between devices  23.8 us (1%)
    psum x1, waiting for transfers between devices, on_device(): lax.psum((grad_gain_one, grad_bias_one, grad_query_weight, grad_key_weigh...  376 us
    all_to_all x2, blocking collectives, from_spectrum(): lax.all_to_all(jnp.stack([real_two, imag_two], 1), 'seq', split_axis=3, c...  222 us
    all_to_all x1, blocking collectives, to_spectrum(): lax.all_to_all(jnp.stack([real_two, imag_two], 1), 'seq', split_axis=2, c...  214 us
    all_to_all x1, waiting for transfers between devices, to_spectrum(): lax.all_to_all(jnp.stack([real_two, imag_two], 1), 'seq', split_axis=2, c...  139 us
    dot_general x2, matrix products, to_spectrum(): jnp.einsum('kf,bjfd->bjkd', cos_row, real_in, precision=highest)  79.7 us
    all_to_all x6, local copies, waits for them, and re-layouts, from_spectrum(): lax.all_to_all(jnp.stack([real_two, imag_two], 1), 'seq', split_axis=3, c...  73.8 us
    dot_general x2, matrix products, to_spectrum(): jnp.einsum('kf,bjfd->bjkd', sin_row, imag_in, precision=highest)  69.6 us
    dot_general x2, matrix products, to_spectrum(): jnp.einsum('kf,bjfd->bjkd', cos_row, imag_in, precision=highest)  69.2 us
  transfers between devices with their start and end apart: 7, of which 5 were waited for; matrix products, arithmetic and copies ran while one was open for 9% of the time, Pallas kernels for 0%

commit v1 on v0

v1 whole, which is shorter than its diff:
```python
import functools

import jax
import jax.numpy as jnp
from jax import lax
from jax.experimental import pallas as pl
from jax.experimental.pallas import tpu as pltpu
from jax.sharding import PartitionSpec as P

epsilon = 1e-05
CHUNKS = 16
GROUP = 8
LANES = 128


def passed_along(value, axis, steps):
    count = lax.axis_size(axis)
    leading, last = (max(0, -steps), min(count, count - steps))
    return lax.ppermute(value, axis, [(source, source + steps) for source in range(leading, last)])


def standardize(values):
    row_mean = jnp.mean(values, axis=-1, keepdims=True)
    centered = values - row_mean
    spread = jnp.mean(centered * centered, axis=-1, keepdims=True)
    factor = lax.rsqrt(spread + epsilon)
    return centered * factor, factor


def norm_back(grads, gain, standard, factor):
    scaled = grads * gain
    return factor * (
        scaled
        - jnp.mean(scaled, axis=-1, keepdims=True)
        - standard * jnp.mean(scaled * standard, axis=-1, keepdims=True)
    )


def project(rows_low, weight):
    return jnp.dot(rows_low, weight, preferred_element_type=jnp.float32)


def project_back(grads_low, weight):
    return lax.dot_general(
        grads_low, weight, (((1,), (1,)), ((), ())), preferred_element_type=jnp.float32
    )


def weight_grad(rows_low, grads_low):
    return lax.dot_general(
        rows_low, grads_low, (((0,), (0,)), ((), ())), preferred_element_type=jnp.float32
    )


def block(ref, place):
    return ref[place * CHUNKS : (place + 1) * CHUNKS, :]


def chunk_rows(chunk, states):
    return pl.ds(chunk, states, stride=CHUNKS)


def state_sums(width, rows_ref, decay_ref, out_ref, group, places, weight, lead):
    decay = decay_ref[pl.ds(group * GROUP, GROUP), :][:, None, :]
    running = jnp.zeros((GROUP, CHUNKS, LANES), jnp.float32)
    for place in places:
        rows = block(rows_ref, place)
        if weight is not None:
            rows = rows * weight(place)
        running = decay * (running + rows[None]) if lead else decay * running + rows[None]
    return running


def forward_states(width, rows_ref, rate_ref, sums_ref, last_ref, decay_ref):
    states = rate_ref.shape[0]
    decay_ref[...] = jnp.exp(-rate_ref[...])

    def body(group, unused):
        running = state_sums(width, rows_ref, decay_ref, None, group, range(width), None, False)
        sums_ref[pl.ds(group * GROUP * CHUNKS, GROUP * CHUNKS), :] = running.reshape(-1, LANES)
        return unused

    lax.fori_loop(0, states // GROUP, body, 0)
    hop = jnp.exp(-width * rate_ref[...])
    held = jnp.zeros((states, LANES), jnp.float32)
    for chunk in range(CHUNKS):
        held = hop * held + sums_ref[chunk_rows(chunk, states), :]
    last_ref[...] = held


def forward_mix(
    width,
    rows_ref,
    sums_ref,
    entering_ref,
    rate_ref,
    coef_ref,
    skip_ref,
    mixed_ref,
    held_ref,
    kernel_ref,
    decay_ref,
    taps_ref,
):
    states = rate_ref.shape[0]
    decay_ref[...] = jnp.exp(-rate_ref[...])
    hop = jnp.exp(-width * rate_ref[...])
    held = entering_ref[...]
    for chunk in range(CHUNKS):
        held_ref[chunk_rows(chunk, states), :] = held
        held = hop * held + sums_ref[chunk_rows(chunk, states), :]
    lags = lax.broadcasted_iota(jnp.int32, (8, LANES), 0).astype(jnp.float32)

    def add_state(state, totals):
        rate = rate_ref[pl.ds(state, 1), :]
        term = coef_ref[pl.ds(state, 1), :] * jnp.exp(-rate * lags)
        step = jnp.exp(-8.0 * rate)
        out = []
        for total in totals:
            out.append(total + term)
            term = term * step
        return tuple(out)

    totals = lax.fori_loop(
        0, states, add_state, tuple(jnp.zeros((8, LANES), jnp.float32) for _ in range(width // 8))
    )
    kernel_ref[...] = jnp.concatenate(totals, axis=0)
    for lag in range(width):
        taps_ref[lag * CHUNKS : (lag + 1) * CHUNKS, :] = jnp.broadcast_to(
            kernel_ref[lag : lag + 1, :], (CHUNKS, LANES)
        )
    for start in range(0, width, 4):
        sums = [skip_ref[...] * block(rows_ref, start + i) for i in range(4)]
        for place in range(start + 4):
            rows = block(rows_ref, place)
            for i in range(4):
                if start + i >= place:
                    sums[i] = sums[i] + block(taps_ref, start + i - place) * rows
        for i in range(4):
            mixed_ref[(start + i) * CHUNKS : (start + i + 1) * CHUNKS, :] = sums[i]

    def body(group, unused):
        decay = decay_ref[pl.ds(group * GROUP, GROUP), :][:, None, :]
        coef = coef_ref[pl.ds(group * GROUP, GROUP), :][:, None, :]
        term = held_ref[pl.ds(group * GROUP * CHUNKS, GROUP * CHUNKS), :].reshape(
            GROUP, CHUNKS, LANES
        )
        term = term * (coef * decay)
        for place in range(width):
            mixed_ref[place * CHUNKS : (place + 1) * CHUNKS, :] += jnp.sum(term, axis=0)
            if place < width - 1:
                term = term * decay
        return unused

    lax.fori_loop(0, states // GROUP, body, 0)


def backward_states(width, grads_ref, rate_ref, sums_ref, first_ref, decay_ref):
    states = rate_ref.shape[0]
    decay_ref[...] = jnp.exp(-rate_ref[...])

    def body(group, unused):
        running = state_sums(
            width, grads_ref, decay_ref, None, group, range(width - 1, -1, -1), None, True
        )
        sums_ref[pl.ds(group * GROUP * CHUNKS, GROUP * CHUNKS), :] = running.reshape(-1, LANES)
        return unused

    lax.fori_loop(0, states // GROUP, body, 0)
    hop = jnp.exp(-width * rate_ref[...])
    held = jnp.zeros((states, LANES), jnp.float32)
    for chunk in range(CHUNKS - 1, -1, -1):
        held = hop * held + sums_ref[chunk_rows(chunk, states), :]
    first_ref[...] = held


def backward_mix(
    width,
    grads_ref,
    rows_ref,
    sums_ref,
    held_ref,
    entering_ref,
    rate_ref,
    coef_ref,
    skip_ref,
    kernel_ref,
    back_ref,
    coef_grad_ref,
    rate_grad_ref,
    decay_ref,
    hop_ref,
    taps_ref,
    after_ref,
    lag_ref,
):
    states = rate_ref.shape[0]
    decay_ref[...] = jnp.exp(-rate_ref[...])
    hop = jnp.exp(-width * rate_ref[...])
    hop_ref[...] = hop
    held = entering_ref[...]
    for chunk in range(CHUNKS - 1, -1, -1):
        after_ref[chunk_rows(chunk, states), :] = held
        held = hop * held + sums_ref[chunk_rows(chunk, states), :]
    for lag in range(width):
        taps_ref[lag * CHUNKS : (lag + 1) * CHUNKS, :] = jnp.broadcast_to(
            kernel_ref[lag : lag + 1, :], (CHUNKS, LANES)
        )
    for start in range(0, width, 4):
        sums = [skip_ref[...] * block(grads_ref, start + i) for i in range(4)]
        for place in range(start, width):
            grads = block(grads_ref, place)
            for i in range(4):
                if place >= start + i:
                    sums[i] = sums[i] + block(taps_ref, place - start - i) * grads
        for i in range(4):
            back_ref[(start + i) * CHUNKS : (start + i + 1) * CHUNKS, :] = sums[i]
    for start in range(0, width, 4):
        sums = [jnp.zeros((CHUNKS, LANES), jnp.float32) for i in range(4)]
        for place in range(start, width):
            grads = block(grads_ref, place)
            for i in range(4):
                if place >= start + i:
                    sums[i] = sums[i] + block(rows_ref, place - start - i) * grads
        for i in range(4):
            lag_ref[start + i : start + i + 1, :] = jnp.sum(sums[i], axis=0, keepdims=True)
    decay_all = decay_ref[...]
    near_coef = jnp.zeros((states, LANES), jnp.float32)
    near_rate = jnp.zeros((states, LANES), jnp.float32)
    for lag in range(width - 1, -1, -1):
        near_coef = near_coef * decay_all + lag_ref[lag : lag + 1, :]
        near_rate = near_rate * decay_all + float(lag) * lag_ref[lag : lag + 1, :]
    coef_grad_ref[...] = near_coef
    rate_grad_ref[...] = near_rate

    def body(group, unused):
        members = pl.ds(group * GROUP, GROUP)
        cells = pl.ds(group * GROUP * CHUNKS, GROUP * CHUNKS)
        cube = (GROUP, CHUNKS, LANES)
        decay = decay_ref[members, :][:, None, :]
        coef = coef_ref[members, :][:, None, :]
        after = after_ref[cells, :].reshape(cube)
        term = after * coef
        for place in range(width - 1, -1, -1):
            back_ref[place * CHUNKS : (place + 1) * CHUNKS, :] += jnp.sum(term, axis=0)
            if place > 0:
                term = term * decay
        held = held_ref[cells, :].reshape(cube)
        coef_grad_ref[members, :] += jnp.sum(held * sums_ref[cells, :].reshape(cube), axis=1)
        slope = state_sums(
            width,
            rows_ref,
            decay_ref,
            None,
            group,
            range(width),
            lambda place: float(width - 1 - place),
            False,
        )
        total = after * (float(width) * hop_ref[members, :][:, None, :] * held + slope)
        slope = state_sums(
            width,
            grads_ref,
            decay_ref,
            None,
            group,
            range(width - 1, -1, -1),
            lambda place: float(place + 1),
            True,
        )
        total = total + held * slope
        rate_grad_ref[members, :] += jnp.sum(total, axis=1)
        return unused

    lax.fori_loop(0, states // GROUP, body, 0)
    rate_grad_ref[...] = -coef_ref[...] * rate_grad_ref[...]


def per_lanes(body, out_rows, scratch, *arrays):
    channels = arrays[0].shape[1]
    scratch = [pltpu.VMEM((rows, LANES), jnp.float32) for rows in scratch]
    return pl.pallas_call(
        body,
        grid=(channels // LANES,),
        in_specs=[pl.BlockSpec((array.shape[0], LANES), lambda i: (0, i)) for array in arrays],
        out_specs=[pl.BlockSpec((rows, LANES), lambda i: (0, i)) for rows in out_rows],
        out_shape=[jax.ShapeDtypeStruct((rows, channels), jnp.float32) for rows in out_rows],
        scratch_shapes=scratch,
        compiler_params=pltpu.CompilerParams(vmem_limit_bytes=40 * 2**20),
    )(*arrays)


def carried(own, rate, row_count, forward):
    count = lax.axis_size("seq")
    place = lax.axis_index("seq")
    every = lax.all_gather(own, "seq", axis=0)
    source = jnp.arange(count)
    hops = place - 1 - source if forward else source - 1 - place
    decays = jnp.exp(-rate[None] * (row_count * jnp.maximum(hops, 0)).astype(jnp.float32)[:, None, None])
    return jnp.sum(jnp.where(hops[:, None, None] >= 0, every * decays, 0.0), axis=0)


def on_device(
    tokens,
    norm1_gain,
    norm1_bias,
    query_weight,
    key_weight,
    value_weight,
    shift_taps,
    ssm_coef,
    ssm_rate,
    ssm_skip,
    out_weight,
    norm2_gain,
    norm2_bias,
    up_weight,
    down_weight,
    out_grad,
):
    unused, row_count, channels = tokens.shape
    width = row_count // CHUNKS
    states = ssm_rate.shape[0]
    tap_count = shift_taps.shape[0]
    halo = tap_count - 1

    def mixed_order(values):
        return values.reshape(CHUNKS, width, channels).swapaxes(0, 1).reshape(row_count, channels)

    def token_order(values):
        return values.reshape(width, CHUNKS, channels).swapaxes(0, 1).reshape(1, row_count, channels)

    low = jnp.bfloat16
    inputs = mixed_order(tokens).astype(jnp.float32)
    out_grad = mixed_order(out_grad)
    standard_one, factor_one = standardize(inputs)
    normed_low = (standard_one * norm1_gain + norm1_bias).astype(low)
    key_rows = project(normed_low, key_weight)
    key_blocks = key_rows.reshape(width, CHUNKS, channels)
    before = passed_along(key_blocks[width - halo :, CHUNKS - 1], "seq", 1)
    value_rows = project(normed_low, value_weight)
    queries = project(normed_low, query_weight)
    head = jnp.concatenate([before[:, None], key_blocks[width - halo :, : CHUNKS - 1]], axis=1)
    extended = jnp.concatenate([head.reshape(halo * CHUNKS, channels), key_rows], 0)

    def delayed(offset):
        start = (halo - offset) * CHUNKS
        return extended[start : start + row_count]

    keys_mixed = sum(shift_taps[offset] * delayed(offset) for offset in range(tap_count))
    product = keys_mixed * value_rows
    skip_row = ssm_skip[None]
    cells = states * CHUNKS
    sums, last = per_lanes(
        functools.partial(forward_states, width), [cells, states], [states], product, ssm_rate
    )
    entering = carried(last, ssm_rate, row_count, True)
    mixed_rows, held, kernel = per_lanes(
        functools.partial(forward_mix, width),
        [row_count, cells, width],
        [states, row_count],
        product,
        sums,
        entering,
        ssm_rate,
        ssm_coef,
        skip_row,
    )
    gated_rows = (queries * mixed_rows).astype(low)
    middle = inputs + project(gated_rows, out_weight)
    standard_two, factor_two = standardize(middle)
    normed_two_low = (standard_two * norm2_gain + norm2_bias).astype(low)
    hidden_pre = project(normed_two_low, up_weight)
    activated, gelu_pull = jax.vjp(jax.nn.gelu, hidden_pre)
    activated_low = activated.astype(low)
    mixed_out = (middle + project(activated_low, down_weight)).astype(low)
    grad_down = weight_grad(activated_low, out_grad)
    grad_hidden = gelu_pull(project_back(out_grad, down_weight))[0].astype(low)
    grad_up = weight_grad(normed_two_low, grad_hidden)
    grad_normed_two = project_back(grad_hidden, up_weight)
    grad_gain_two = jnp.sum(grad_normed_two * standard_two, axis=0)
    grad_bias_two = jnp.sum(grad_normed_two, axis=0)
    grad_middle = out_grad.astype(jnp.float32) + norm_back(
        grad_normed_two, norm2_gain, standard_two, factor_two
    )
    grad_attended = grad_middle.astype(low)
    grad_out_weight = weight_grad(gated_rows, grad_attended)
    grad_gated = project_back(grad_attended, out_weight)
    grad_queries = (grad_gated * mixed_rows).astype(low)
    grad_mixed = grad_gated * queries
    grad_skip = jnp.sum(grad_mixed * product, axis=0)
    grad_sums, first = per_lanes(
        functools.partial(backward_states, width), [cells, states], [states], grad_mixed, ssm_rate
    )
    grad_entering = carried(first, ssm_rate, row_count, False)
    grad_product, grad_coef, grad_rate = per_lanes(
        functools.partial(backward_mix, width),
        [row_count, states, states],
        [states, states, row_count, cells, width],
        grad_mixed,
        product,
        grad_sums,
        held,
        grad_entering,
        ssm_rate,
        ssm_coef,
        skip_row,
        kernel,
    )
    grad_keys_mixed = grad_product * value_rows
    grad_values = (grad_product * keys_mixed).astype(low)
    grad_blocks = grad_keys_mixed.reshape(width, CHUNKS, channels)
    after = passed_along(grad_blocks[:halo, 0], "seq", -1)
    tail = jnp.concatenate([grad_blocks[:halo, 1:], after[:, None]], axis=1)
    grad_extended = jnp.concatenate([grad_keys_mixed, tail.reshape(halo * CHUNKS, channels)], 0)
    grad_keys = sum(
        shift_taps[offset] * grad_extended[offset * CHUNKS : offset * CHUNKS + row_count]
        for offset in range(tap_count)
    ).astype(low)
    grad_taps = jnp.stack(
        [jnp.sum(grad_keys_mixed * delayed(offset), axis=0) for offset in range(tap_count)]
    )
    grad_query_weight = weight_grad(normed_low, grad_queries)
    grad_key_weight = weight_grad(normed_low, grad_keys)
    grad_value_weight = weight_grad(normed_low, grad_values)
    grad_normed = (
        project_back(grad_queries, query_weight)
        + project_back(grad_keys, key_weight)
        + project_back(grad_values, value_weight)
    )
    grad_gain_one = jnp.sum(grad_normed * standard_one, axis=0)
    grad_bias_one = jnp.sum(grad_normed, axis=0)
    grad_inputs = grad_middle + norm_back(grad_normed, norm1_gain, standard_one, factor_one)
    summed = lax.psum(
        (
            grad_gain_one,
            grad_bias_one,
            grad_query_weight,
            grad_key_weight,
            grad_value_weight,
            grad_taps,
            grad_coef,
            grad_rate,
            grad_skip,
            grad_out_weight,
            grad_gain_two,
            grad_bias_two,
            grad_up,
            grad_down,
        ),
        ("seq", "batch"),
    )
    return (token_order(mixed_out), token_order(grad_inputs)) + tuple(summed)


def solution(mesh):
    placed = (P("batch", "seq", None),) + (P(),) * 14 + (P("batch", "seq", None),)
    return jax.shard_map(
        on_device,
        mesh=mesh,
        in_specs=placed,
        out_specs=(P("batch", "seq", None),) * 2 + (P(),) * 14,
        check_vma=False,
    )
```

time: 2130 us -> 676 us (0.32)
  blocking collectives: 538 us -> 44.3 us
  matrix products: 530 us -> 61.6 us
  other arithmetic: 192 us -> 9.36 us
  local copies, waits for them, and re-layouts: 233 us -> 50.4 us
  waiting for transfers between devices: 590 us -> 415 us
  Pallas kernels: 0 us -> 68.4 us
    all_to_all x4 -> x0, blocking collectives: 495 us -> none  [the longest x2 222 us: from_spectrum(): lax.all_to_all(jnp.stack([real_two, imag_two], 1), 'seq', split_axis=3, c...]
    dot_general x42 -> x18, matrix products: 530 us -> 61.6 us  [the longest x6 22.8 us: project(): return jnp.dot(rows_low, weight, preferred_element_type=jnp.float32)]
    all_to_all x4 -> x0, waiting for transfers between devices: 214 us -> none  [the longest x1 139 us: to_spectrum(): lax.all_to_all(jnp.stack([real_two, imag_two], 1), 'seq', split_axis=2, c...]
    reduce_sum x26 -> x6, other arithmetic: 108 us -> 7.23 us  [the longest x2 3.7 us: carried(): jnp.sum(jnp.where(hops[:, None, None] >= 0, every * decays, 0.0), axis=0)]
    all_to_all x10 -> x0, local copies, waits for them, and re-layouts: 94.3 us -> none  [the longest x6 73.8 us: from_spectrum(): lax.all_to_all(jnp.stack([real_two, imag_two], 1), 'seq', split_axis=3, c...]
    another operation x10 -> x4, local copies, waits for them, and re-layouts: 71.2 us -> 0.02 us  [on_device(): jnp.stack([jnp.sum(grad_keys_mixed * delayed(offset), axis=0) for offset...]
    pallas_call x0 -> x4, Pallas kernels: none -> 68.4 us  [per_lanes(): pl.pallas_call(body, grid=(channels // LANES,), in_specs=[pl.BlockSpec((a...]
    another operation x8 -> x1, other arithmetic: 37.8 us -> 0.02 us  [on_device(): jnp.stack([jnp.sum(grad_keys_mixed * delayed(offset), axis=0) for offset...]
  transfers between devices with their start and end apart: 7 -> 5, of which waited for: 5 -> 4; matrix products, arithmetic and copies ran while one was open for 9% -> 7% of each run, Pallas kernels for 0% -> 0%
where the time goes in v1:
time: 676 us; the launch traced here: 667 us
  waiting for transfers between devices  415 us (61%)
  Pallas kernels  68.4 us (10%)
  matrix products  61.6 us (9%)
  local copies, waits for them, and re-layouts  50.4 us (7%)
  blocking collectives  44.3 us (7%)
  between operations  14.9 us (2%)
  other arithmetic  9.36 us (1%)
    psum x1, waiting for transfers between devices, on_device(): lax.psum((grad_gain_one, grad_bias_one, grad_query_weight, grad_key_weigh...  387 us
    pallas_call x4, Pallas kernels, per_lanes(): pl.pallas_call(body, grid=(channels // LANES,), in_specs=[pl.BlockSpec((a...  68.4 us
    psum x1, blocking collectives, on_device(): lax.psum((grad_gain_one, grad_bias_one, grad_query_weight, grad_key_weigh...  44.3 us
    unnamed x148, local copies, waits for them, and re-layouts  42.7 us
    all_gather x2, waiting for transfers between devices, carried(): every = lax.all_gather(own, 'seq', axis=0)  27.2 us
    dot_general x6, matrix products, project(): return jnp.dot(rows_low, weight, preferred_element_type=jnp.float32)  22.8 us
    dot_general x6, matrix products, weight_grad(): lax.dot_general(rows_low, grads_low, (((0,), (0,)), ((), ())), preferred_...  21.8 us
    dot_general x6, matrix products, project_back(): lax.dot_general(grads_low, weight, (((1,), (1,)), ((), ())), preferred_el...  17 us
  transfers between devices with their start and end apart: 5, of which 4 were waited for; matrix products, arithmetic and copies ran while one was open for 7% of the time, Pallas kernels for 0%

profile of v1, /device:TPU:0, one launch (start us, length us, event | category | flops | bytes accessed | tf_op | source)
XLA Modules:
  0.0 667.2 jit_solution(7841828823321107681)
XLA Ops:
  7.2 1.7 copy.38
  10.1 0.9 fusion.20
  11.6 0.9 copy-done.56
  13.3 2.4 collective-permute-start
  16.6 2.6 fusion.30
  19.2 9.0 %shard_map.279 = (f32[1024,768]{1,0:T(8,128)S(1)}, f32[64,768]{1,0:T(8,128)}) custom-call(f32[512,768]{1,0:T(8,128)S(1)} %get-tuple-element.69.rows_ref, f32[64,768]{1,0:T(8,128)S(1)} %copy-done.3), custom_call_target="tpu_custom_call" | custom-call | tf_op jit(solution)/shard_map/pallas_call | solution.py:282
  28.1 1.7 copy-done.8
  29.9 2.5 copy.41
  32.4 7.9 %fusion.33 = f32[512,3072]{1,0:T(8,128)} fusion(bf16[512,768]{1,0:T(8,128)(2,1)} %bitcast.84, bf16[3072,768]{1,0:T(8,128)(2,1)} %param.30), kind=kOutput, calls=%fused_computation.96 | convolution fusion | flops 2415919104 | bytes 11796480 | tf_op jit(solution)/shard_map/dot_general | solution.py:44
  40.3 19.9 %all-gather.5.cloned.1.call-done = f32[512,768]{1,0:T(8,128)} async-done(((f32[64,768]{1,0:T(8,128)}), f32[512,768]{1,0:T(8,128)}) %all-gather.5.cloned.1.call-update) | async-done | bytes 1572880 | tf_op jit(solution)/shard_map/all_gather | solution.py:296
  60.2 1.8 select_reduce_fusion.1.entering_ref
  62.1 1.9 copy-done.9
  63.9 18.0 %shard_map.280 = (f32[512,768]{1,0:T(8,128)S(1)}, f32[1024,768]{1,0:T(8,128)S(1)}, f32[32,768]{1,0:T(8,128)S(1)}) custom-call(f32[512,768]{1,0:T(8,128)S(1)} %get-tuple-element.69.rows_ref, f32[1024,768]{1,0:T(8,128)S(1)} %copy-done.9, f32[64,768]{1,0:T(8,128)S(1)} %select_reduce_fusion.1.entering_ref, f32[64,768]{1,0:T(8,128)S(1)} %copy-done.3, ...), custom_call_target="tpu_custom_call" | custom-call | tf_op jit(solution)/shard_map/pallas_call | solution.py:282
  86.4 2.1 copy-done.61
  88.5 9.8 %fusion.6 = (bf16[512,3072]{1,0:T(8,128)(2,1)S(1)}, f32[512,3072]{1,0:T(8,128)}) fusion(f32[512,3072]{1,0:T(8,128)S(1)} %copy-done.61, bf16[768,3072]{1,0:T(8,128)(2,1)} %param.29, f32[512,768]{1,0:T(8,128)S(1)} %get-tuple-element.77, f32[768]{0:T(1024)S(1)} %copy-done.58, f32[768]{0:T(1024)S(1)} %copy-done.52, f32[512]{0:T(512)S(1)} %add_rsqrt_fusion.1, ...), kind=kOutput, calls=%fused_computation.8 | convolution fusion | flops 2449342464 | bytes 22030336 | tf_op jit(solution)/shard_map/dot_general | solution.py:40
  98.3 3.5 multiply_reduce_fusion
  102.5 2.5 multiply_reduce_fusion.1
  105.0 8.9 %shard_map.281 = (f32[1024,768]{1,0:T(8,128)S(1)}, f32[64,768]{1,0:T(8,128)}) custom-call(f32[512,768]{1,0:T(8,128)S(1)} %get-tuple-element.67.grads_ref, f32[64,768]{1,0:T(8,128)S(1)} %copy-done.3), custom_call_target="tpu_custom_call" | custom-call | tf_op jit(solution)/shard_map/pallas_call | solution.py:282
  113.9 1.2 copy-done.1
  115.1 1.7 copy-done.6
  116.8 3.7 fusion.36
  120.6 2.2 fusion.21
  122.8 1.0 copy-done.60
  123.8 5.8 fusion.27
  129.6 5.7 fusion.29
  135.3 7.3 %all-gather.7.cloned.1.call-done = f32[512,768]{1,0:T(8,128)} async-done(((f32[64,768]{1,0:T(8,128)}), f32[512,768]{1,0:T(8,128)}) %all-gather.7.cloned.1.call-update) | async-done | bytes 1572880 | tf_op jit(solution)/shard_map/all_gather | solution.py:296
  142.6 1.9 select_reduce_fusion.entering_ref
  144.5 1.9 copy-done.5
  146.4 1.9 copy-done.7
  148.3 32.5 %shard_map.282 = (f32[512,768]{1,0:T(8,128)S(1)}, f32[64,768]{1,0:T(8,128)}, f32[64,768]{1,0:T(8,128)}) custom-call(f32[512,768]{1,0:T(8,128)S(1)} %copy-done.2, f32[512,768]{1,0:T(8,128)S(1)} %get-tuple-element.69.rows_ref, f32[1024,768]{1,0:T(8,128)S(1)} %copy-done.7, f32[1024,768]{1,0:T(8,128)S(1)} %copy-done.5, ...), custom_call_target="tpu_custom_call" | custom-call | tf_op jit(solution)/shard_map/pallas_call | solution.py:282
  180.9 1.4 multiply_reduce_fusion.4
  182.3 1.3 collective-permute-start.1
  183.6 2.2 fusion.38
  186.4 2.2 fusion.37
  188.6 1.4 copy-done.22
  190.0 8.0 %add_convert_fusion = bf16[512,768]{1,0:T(8,128)(2,1)S(1)} fusion(f32[512,768]{1,0:T(8,128)S(1)} %copy-done.22, bf16[3072,768]{1,0:T(8,128)(2,1)} %param.30, f32[512,3072]{1,0:T(8,128)} %get-tuple-element.79), kind=kOutput, calls=%fused_computation.53 | convolution fusion | flops 2430861312 | bytes 13369344 | tf_op jit(solution)/shard_map/dot_general | solution.py:40
  198.0 1.1 copy.40
  202.2 1.4 multiply_reduce_fusion.6
  204.2 2.1 copy.43
  206.3 44.3 %all-reduce = (f32[768]{0:T(1024)}, f32[768]{0:T(1024)}, f32[4,768]{1,0:T(4,128)}, f32[768]{0:T(1024)}, f32[768]{0:T(1024)}, /*index=5*/f32[768]{0:T(1024)}) all-reduce(f32[768]{0:T(1024)S(1)} %get-tuple-element.41, f32[768]{0:T(1024)S(1)} %get-tuple-element.47, ...), channel_id=1, replica_groups=mesh['seq'=8,'batch'=4] {'seq','batch'}, use_global_device_ids=true, to_apply=%region_11.12 | all-reduce | flops 6912 | bytes 55296 | tf_op jit(solution)/shard_map/psum | solution.py:434
  250.6 386.5 %all-reduce.4.cloned.1.call-done = (f32[768,768]{1,0:T(8,128)}, f32[768,768]{1,0:T(8,128)}, f32[768,768]{1,0:T(8,128)}, f32[64,768]{1,0:T(8,128)}, f32[64,768]{1...) async-done(((f32[768,768]{1,0:T(8,128)}, f32[768,768]{1,0:T(8,128)}, f32[768,768]{1,0:T(8,128)}, f32[64,768]{1,0:T(8,128)}, ...) | async-done | bytes 28704784 | tf_op jit(solution)/shard_map/psum | solution.py:434
  637.1 3.4 copy.60
  640.4 1.4 copy.61
  641.9 1.1 copy-done.33
  643.0 1.4 copy.62
  645.8 1.4 copy.65
  647.2 9.3 %copy.66 = f32[768,3072]{1,0:T(8,128)} copy(f32[768,3072]{1,0:T(8,128)} %get-tuple-element.98) | data formatting | bytes 18874368
  656.5 3.7 copy.67
  (183 shorter events, 13.9 us)
Async XLA Ops:
  7.2 9.4 %copy-start = (bf16[768,768]{1,0:T(8,128)(2,1)S(1)}, bf16[768,768]{1,0:T(8,128)(2,1)}, u32[]{:S(2)}) copy-start(bf16[768,768]{1,0:T(8,128)(2,1)} %param.21) | copy-start | bytes 3538948
  7.2 53.0 %all-gather.5.cloned.1.call-start = ((), (), s32[]{:S(2)}) async-start(), calls=%async_computation | async-start | bytes 1769472 | tf_op jit(solution)/shard_map/all_gather | solution.py:296
  9.0 2.2 copy-start.11
  12.5 4.1 copy-start.14
  12.5 3.2 copy-start.50
  13.3 5.9 copy-start.35
  13.3 3.2 collective-permute-start
  16.6 2.6 copy-start.41
  16.6 2.6 copy-start.3
  19.2 10.7 %copy-start.53 = (f32[768]{0:T(1024)S(1)}, f32[768]{0:T(1024)}, u32[]{:S(2)}) copy-start(f32[768]{0:T(1024)} %param.25) | copy-start | bytes 9220
  29.8 112.8 %all-gather.7.cloned.1.call-start = ((), (), s32[]{:S(2)}) async-start(), calls=%async_computation.1 | async-start | bytes 1769472 | tf_op jit(solution)/shard_map/all_gather | solution.py:296
  40.3 21.7 %copy-start.10 = (f32[64,768]{1,0:T(8,128)S(1)}, f32[64,768]{1,0:T(8,128)}, u32[]{:S(2)}) copy-start(f32[64,768]{1,0:T(8,128)} %coef_ref.3) | copy-start | bytes 589828
  63.9 18.0 %copy-start.15 = (bf16[512,768]{1,0:T(8,128)(2,1)S(1)}, bf16[512,768]{1,0:T(8,128)(2,1)}, u32[]{:S(2)}) copy-start(bf16[512,768]{1,0:T(8,128)(2,1)} %copy-done.14) | copy-start | bytes 2359300
  63.9 18.0 %copy-start.39 = (bf16[768,768]{1,0:T(8,128)(2,1)S(1)}, bf16[768,768]{1,0:T(8,128)(2,1)}, u32[]{:S(2)}) copy-start(bf16[768,768]{1,0:T(8,128)(2,1)} %param.19) | copy-start | bytes 3538948
  82.0 2.5 copy-start.12
  82.0 3.1 copy-start.25
  83.6 2.4 copy-start.23
  85.1 3.4 copy-start.61
  86.0 15.9 %copy-start.20 = (f32[512,768]{1,0:T(8,128)}, f32[512,768]{1,0:T(8,128)S(1)}, u32[]{:S(2)}) copy-start(f32[512,768]{1,0:T(8,128)S(1)} %get-tuple-element.77) | copy-start | bytes 4718596
  86.0 2.5 copy-start.52
  86.0 2.5 copy-start.58
  86.0 12.3 %slice-start.3 = ((s8[4718592]{0:T(1024)(128)(4,1)}), s8[4194304]{0:T(1024)(128)(4,1)S(1)}, s32[]{:S(2)}) async-start(s8[4718592]{0:T(1024)(128)(4,1)} %bitcast.102), calls=%async_computation.6 | async-start | bytes 8388608
  88.5 9.8 %slice-start.4 = ((s8[4718592]{0:T(1024)(128)(4,1)}), s8[524288]{0:T(1024)(128)(4,1)S(1)}, s32[]{:S(2)}) async-start(s8[4718592]{0:T(1024)(128)(4,1)} %bitcast.102), calls=%async_computation.7 | async-start | bytes 1048576
  98.3 3.5 copy-start.59
  98.3 3.5 copy-start.26
  102.5 2.5 copy-start.17
  116.8 520.3 %all-reduce.4.cloned.1.call-start = ((), (), s32[]{:S(2)}) async-start(), calls=%async_computation.2 | async-start | bytes 57409536 | tf_op jit(solution)/shard_map/psum | solution.py:434
  116.8 3.8 copy-start.18
  116.8 3.8 copy-start.24
  120.6 2.2 copy-start.21
  120.6 3.2 copy-start.60
  120.6 9.0 %slice-start.5 = ((s8[6291456]{0:T(1024)(128)(4,1)}), s8[4194304]{0:T(1024)(128)(4,1)S(1)}, s32[]{:S(2)}) async-start(s8[6291456]{0:T(1024)(128)(4,1)} %bitcast.104), calls=%async_computation.8 | async-start | bytes 8388608
  123.8 5.8 copy-start.27
  123.8 5.8 slice-start.6
  148.3 32.6 %copy-start.36 = (f32[512,768]{1,0:T(8,128)S(1)}, f32[512,768]{1,0:T(8,128)}, u32[]{:S(2)}) copy-start(f32[512,768]{1,0:T(8,128)} %copy-done.35) | copy-start | bytes 4718596
  148.3 32.6 %copy-start.37 = (f32[512,768]{1,0:T(8,128)S(1)}, f32[512,768]{1,0:T(8,128)}, u32[]{:S(2)}) copy-start(f32[512,768]{1,0:T(8,128)} %get-tuple-element.70) | copy-start | bytes 4718596
  148.3 32.6 %copy-start.38 = (f32[512,768]{1,0:T(8,128)S(1)}, f32[512,768]{1,0:T(8,128)}, u32[]{:S(2)}) copy-start(f32[512,768]{1,0:T(8,128)} %get-tuple-element.73) | copy-start | bytes 4718596
  148.3 32.6 %copy-start.42 = (f32[3,16,768]{2,1,0:T(8,128)S(1)}, f32[3,16,768]{2,1,0:T(8,128)}, u32[]{:S(2)}) copy-start(f32[3,16,768]{2,1,0:T(8,128)} %copy-done.41) | copy-start | bytes 442372
  180.9 2.7 copy-start.16
  182.3 3.6 collective-permute-start.1
  186.3 2.2 copy-start.30
  190.0 9.1 %copy-start.40 = (bf16[768,768]{1,0:T(8,128)(2,1)S(1)}, bf16[768,768]{1,0:T(8,128)(2,1)}, u32[]{:S(2)}) copy-start(bf16[768,768]{1,0:T(8,128)(2,1)} %param.19) | copy-start | bytes 3538948
  637.1 3.4 copy-start.34
  640.4 2.5 copy-start.33
  643.0 2.8 copy-start.32
  645.8 10.7 %slice-start = ((s8[9437184]{0:T(1024)(128)(4,1)}), s8[4194304]{0:T(1024)(128)(4,1)S(1)}, s32[]{:S(2)}) async-start(s8[9437184]{0:T(1024)(128)(4,1)} %bitcast.79), calls=%async_computation.3 | async-start | bytes 8388608
  647.2 9.3 %slice-start.1 = ((s8[9437184]{0:T(1024)(128)(4,1)}), s8[4194304]{0:T(1024)(128)(4,1)S(1)}, s32[]{:S(2)}) async-start(s8[9437184]{0:T(1024)(128)(4,1)} %bitcast.79), calls=%async_computation.4 | async-start | bytes 8388608
  647.2 9.3 %slice-start.2 = ((s8[9437184]{0:T(1024)(128)(4,1)}), s8[1048576]{0:T(1024)(128)(4,1)S(1)}, s32[]{:S(2)}) async-start(s8[9437184]{0:T(1024)(128)(4,1)} %bitcast.79), calls=%async_computation.5 | async-start | bytes 2097152
  (26 other events, 41.5 us)
Sparse Core Ops, SparseCore 0:
  29.9 30.2 all-gather.4
  116.9 25.6 all-gather.6
  188.7 448.3 all-reduce.3

commit v2 on v1

--- a/solution.py
+++ b/solution.py
@@ -300,6 +300,429 @@
     return jnp.sum(jnp.where(hops[:, None, None] >= 0, every * decays, 0.0), axis=0)
 
 
+MESH = pl.DeviceIdType.MESH
+
+
+def add_rows(out_ref, out_start, a_ref, a_start, b_ref, b_start, rows):
+    columns = out_ref.shape[1]
+    size = 8
+    for option in (16, 24, 32, 48, 64):
+        if rows % option == 0 and option * columns <= 64 * 1024:
+            size = option
+
+    def body(i, unused):
+        at = i * size
+        out_ref[pl.ds(pl.multiple_of(out_start + at, 8), size), :] = (
+            a_ref[pl.ds(pl.multiple_of(a_start + at, 8), size), :]
+            + b_ref[pl.ds(pl.multiple_of(b_start + at, 8), size), :]
+        )
+        return unused
+
+    lax.fori_loop(0, rows // size, body, 0)
+
+
+class Lane:
+    def __init__(self, array, start, rows, columns, bits, line_first):
+        self.array, self.start, self.rows, self.columns = array, start, rows, columns
+        self.bits, self.line_first = bits, line_first
+
+    def buffers(self, line):
+        half = self.rows // 2
+        unit = half // line if self.line_first else half >> len(self.bits)
+        counts = [half, half]
+        size = half // line if self.line_first else half
+        for unused in self.bits:
+            size //= 2
+            counts.append(size)
+        counts.append(unit * (line + 1 if self.line_first else max(1, line // 2)))
+        return [pltpu.VMEM((count, self.columns), jnp.float32) for count in counts]
+
+    def copies(self, line):
+        chain = 4 * line + 1 if self.line_first else line
+        return 4 + 2 * len(self.bits) + chain
+
+
+def lane_steps(lane, line, source, target, buffers, send_sems, recv_sems, first_sem, pending):
+    acc, fin = buffers[:2]
+    landing = buffers[2 : 2 + len(lane.bits)]
+    chain = buffers[-1]
+    me = lax.axis_index("seq")
+    z = lax.axis_index("batch")
+    half = lane.rows // 2
+    core = me % 2
+    counter = [first_sem]
+
+    def fresh():
+        counter[0] += 1
+        return counter[0] - 1
+
+    def remote(src, dst, index, device):
+        return pltpu.make_async_remote_copy(
+            src_ref=src,
+            dst_ref=dst,
+            send_sem=send_sems.at[index],
+            recv_sem=recv_sems.at[index],
+            device_id=device,
+            device_id_type=MESH,
+        )
+
+    def rows_of(ref, start, count):
+        if not isinstance(start, int):
+            start = pl.multiple_of(start, 8)
+        return ref.at[pl.ds(start, count), :]
+
+    def side(bit):
+        return (me // bit) % 2
+
+    def partner(bit):
+        return (me + bit * (1 - 2 * side(bit)), z)
+
+    mine = lane.start + core * half
+    other = lane.start + (1 - core) * half
+    load_index, swap_index = fresh(), fresh()
+    load = pltpu.make_async_copy(rows_of(source, mine, half), acc, recv_sems.at[load_index])
+    swap = remote(rows_of(source, other, half), fin, swap_index, partner(1))
+
+    def begin():
+        load.start()
+        swap.start()
+
+    def add_swap():
+        load.wait()
+        swap.wait_recv()
+        add_rows(acc, 0, acc, 0, fin, 0, half)
+
+    pending.append(swap.wait_send)
+    steps = [[begin], [add_swap]]
+
+    def join(function):
+        steps[-1].append(function)
+
+    def step(function):
+        steps.append([function])
+
+    def neighbours_sum(base, size, final):
+        starts = [base]
+        for place, bit in enumerate(lane.bits):
+            size //= 2
+            start = starts[-1]
+            copy = remote(
+                rows_of(acc, start + (1 - side(bit)) * size, size),
+                landing[place],
+                fresh(),
+                partner(bit),
+            )
+            own = start + side(bit) * size
+            last = place == len(lane.bits) - 1
+            join(copy.start)
+            pending.append(copy.wait_send)
+
+            def receive(copy=copy, own=own, size=size, place=place, last=last):
+                copy.wait_recv()
+                add_rows(fin if final and last else acc, own, acc, own, landing[place], 0, size)
+
+            step(receive)
+            starts.append(own)
+        return starts, size
+
+    def neighbours_spread(starts, size):
+        for place in range(len(lane.bits) - 1, -1, -1):
+            bit = lane.bits[place]
+            start = starts[place + 1]
+            copy = remote(
+                rows_of(fin, start, size), rows_of(fin, start, size), fresh(), partner(bit)
+            )
+            join(copy.start)
+            pending.append(copy.wait_send)
+            step(copy.wait_recv)
+            size *= 2
+
+    if not lane.line_first:
+        starts, size = neighbours_sum(0, half, False)
+        at = starts[-1]
+        depth = jnp.minimum(z, line - 1 - z)
+        lower = z < line // 2
+        inward = (me, jnp.where(lower, z + 1, z - 1))
+        outward = (me, jnp.where(lower, z - 1, z + 1))
+        across = (me, line - 1 - z)
+        middle = line // 2 - 1
+
+        def on(level, function):
+            def guarded():
+                pl.when(depth == level)(function)
+
+            return guarded
+
+        for level in range(middle):
+            copy = remote(
+                rows_of(acc, at, size), rows_of(chain, level * size, size), fresh(), inward
+            )
+            join(on(level, copy.start))
+            pending.append(on(level, copy.wait_send))
+
+            def receive(copy=copy, level=level):
+                copy.wait_recv()
+                add_rows(acc, at, acc, at, chain, level * size, size)
+
+            step(on(level + 1, receive))
+        copy = remote(rows_of(acc, at, size), rows_of(chain, middle * size, size), fresh(), across)
+        join(on(middle, copy.start))
+        pending.append(on(middle, copy.wait_send))
+
+        def receive_across(copy=copy):
+            copy.wait_recv()
+            add_rows(fin, at, acc, at, chain, middle * size, size)
+
+        step(on(middle, receive_across))
+        for level in range(middle - 1, -1, -1):
+            copy = remote(rows_of(fin, at, size), rows_of(fin, at, size), fresh(), outward)
+            join(on(level + 1, copy.start))
+            pending.append(on(level + 1, copy.wait_send))
+            step(on(level, copy.wait_recv))
+        neighbours_spread(starts, size)
+    else:
+        unit = half // line
+        slots = [fresh() for unused in range(line + 1)]
+        outs = [[fresh() for unused in range(2)] for unused in range(line)]
+        spreads = [fresh() for unused in range(line)]
+
+        def on(place, function):
+            def guarded():
+                pl.when(z == place)(function)
+
+            return guarded
+
+        def beside(place):
+            return (me, place - 1 if place > 0 else place + 1)
+
+        def hop(place, member, step_to):
+            slot = line if step_to < 0 and member == place - 1 else member
+            return remote(
+                rows_of(acc, member * unit, unit),
+                rows_of(chain, slot * unit, unit),
+                slots[slot],
+                (me, place + step_to),
+            )
+
+        def arrived(place, slot, member):
+            remote(
+                rows_of(acc, member * unit, unit),
+                rows_of(chain, slot * unit, unit),
+                slots[slot],
+                beside(place),
+            ).wait_recv()
+            add_rows(acc, member * unit, acc, member * unit, chain, slot * unit, unit)
+
+        for turn in range(line - 1):
+
+            def rightward(place=turn):
+                for member in range(line - 1, place, -1):
+                    if place > 0:
+                        arrived(place, member, member)
+                    hop(place, member, 1).start()
+
+            def leftward(place=line - 1 - turn):
+                for member in range(place):
+                    if place < line - 1:
+                        arrived(place, member, member)
+                    hop(place, member, -1).start()
+
+            if turn > 0:
+                step(on(turn, rightward))
+            else:
+                join(on(turn, rightward))
+            join(on(line - 1 - turn, leftward))
+
+        def collect(place):
+            if place > 0:
+                arrived(place, place, place)
+            if place < line - 1:
+                arrived(place, line, place)
+
+        def collect_all():
+            for place in range(line):
+                on(place, functools.partial(collect, place))()
+
+        step(collect_all)
+
+        def sent(place):
+            for member in range(line - 1, place, -1):
+                hop(place, member, 1).wait_send()
+            for member in range(place):
+                hop(place, member, -1).wait_send()
+
+        for place in range(line):
+            pending.append(on(place, functools.partial(sent, place)))
+        base = z * unit
+        starts, size = neighbours_sum(base, unit, True)
+        neighbours_spread(starts, size)
+
+        def spread_at(place, distance, receive, send):
+            members = {place - distance, place + distance}
+            for member in sorted(members):
+                if not 0 <= member < line:
+                    continue
+                if receive and distance > 0:
+                    remote(
+                        rows_of(fin, member * unit, unit),
+                        rows_of(fin, member * unit, unit),
+                        spreads[member],
+                        beside(place),
+                    ).wait_recv()
+                if not send:
+                    continue
+                for step_to in (1, -1):
+                    going = member <= place if step_to > 0 else member >= place
+                    if going and 0 <= place + step_to < line:
+                        yield member, step_to
+
+        def pass_on(place, member, step_to):
+            return pltpu.make_async_remote_copy(
+                src_ref=rows_of(fin, member * unit, unit),
+                dst_ref=rows_of(fin, member * unit, unit),
+                send_sem=send_sems.at[outs[member][0 if step_to > 0 else 1]],
+                recv_sem=recv_sems.at[spreads[member]],
+                device_id=(me, place + step_to),
+                device_id_type=MESH,
+            )
+
+        for distance in range(line):
+
+            def forward(place, distance):
+                for member, step_to in spread_at(place, distance, True, True):
+                    pass_on(place, member, step_to).start()
+
+            def forward_all(distance=distance):
+                for place in range(line):
+                    on(place, functools.partial(forward, place, distance))()
+
+            if distance == 0:
+                join(forward_all)
+            else:
+                step(forward_all)
+
+        def passed(place):
+            for distance in range(line):
+                for member, step_to in spread_at(place, distance, False, True):
+                    pass_on(place, member, step_to).wait_send()
+
+        for place in range(line):
+            pending.append(on(place, functools.partial(passed, place)))
+
+    keep_index, give_index = fresh(), fresh()
+    keep = pltpu.make_async_copy(fin, rows_of(target, mine, half), recv_sems.at[keep_index])
+    give = remote(fin, rows_of(target, mine, half), give_index, partner(1))
+    join(keep.start)
+    join(give.start)
+    pending.append(keep.wait)
+    pending.append(give.wait)
+    assert counter[0] - first_sem <= lane.copies(line)
+    return steps
+
+
+def turn_order(lengths, order):
+    if [order.count(place) for place in range(len(lengths))] == lengths:
+        return order
+    turns = range(max(lengths))
+    return [place for turn in turns for place, length in enumerate(lengths) if turn < length]
+
+
+def all_sum_body(count, line, bits, lanes, order, *refs):
+    sources, targets = refs[:count], refs[count : 2 * count]
+    send_sems, recv_sems = refs[-2:]
+    buffers = list(refs[2 * count : -2])
+    me = lax.axis_index("seq")
+    z = lax.axis_index("batch")
+    barrier = pltpu.get_barrier_semaphore()
+    for bit in bits:
+        pl.semaphore_signal(
+            barrier,
+            inc=1,
+            device_id=(me + bit * (1 - 2 * ((me // bit) % 2)), z),
+            device_id_type=MESH,
+        )
+
+    @pl.when(z > 0)
+    def left():
+        pl.semaphore_signal(barrier, inc=1, device_id=(me, z - 1), device_id_type=MESH)
+
+    @pl.when(z < line - 1)
+    def right():
+        pl.semaphore_signal(barrier, inc=1, device_id=(me, z + 1), device_id_type=MESH)
+
+    pl.semaphore_wait(
+        barrier, len(bits) + jnp.where(z > 0, 1, 0) + jnp.where(z < line - 1, 1, 0)
+    )
+    pending = []
+    programs = []
+    first = 0
+    for lane in lanes:
+        own = [buffers.pop(0) for unused in lane.buffers(line)]
+        programs.append(
+            lane_steps(
+                lane,
+                line,
+                sources[lane.array],
+                targets[lane.array],
+                own,
+                send_sems,
+                recv_sems,
+                first,
+                pending,
+            )
+        )
+        first += lane.copies(line)
+    for place in turn_order([len(program) for program in programs], order):
+        for function in programs[place].pop(0):
+            function()
+    for wait in pending:
+        wait()
+
+
+def all_sum(arrays, plan, order):
+    size, line = lax.axis_size("seq"), lax.axis_size("batch")
+    bits = [1 << place for place in range(size.bit_length() - 1)]
+    lanes = []
+    for index, array in enumerate(arrays):
+        rows = array.shape[0] // len(plan[index])
+        for piece, (flipped, line_first) in enumerate(plan[index]):
+            if rows % (8 * size * line):
+                line_first = False
+            path = bits[:0:-1] if flipped else bits[1:]
+            lanes.append(Lane(index, piece * rows, rows, array.shape[1], path, line_first))
+    scratch = [buffer for lane in lanes for buffer in lane.buffers(line)]
+    copies = sum(lane.copies(line) for lane in lanes)
+    return pl.pallas_call(
+        functools.partial(all_sum_body, len(arrays), line, bits, lanes, order),
+        out_shape=[jax.ShapeDtypeStruct(array.shape, jnp.float32) for array in arrays],
+        in_specs=[pl.BlockSpec(memory_space=pltpu.HBM)] * len(arrays),
+        out_specs=[pl.BlockSpec(memory_space=pltpu.HBM)] * len(arrays),
+        scratch_shapes=scratch
+        + [pltpu.SemaphoreType.DMA((copies,)), pltpu.SemaphoreType.DMA((copies,))],
+        compiler_params=pltpu.CompilerParams(
+            collective_id=0, has_side_effects=True, vmem_limit_bytes=62 * 2**20
+        ),
+    )(*arrays)
+
+
+PLAN = [
+    [(False, True), (False, False), (False, True), (False, False)],
+    [(False, False), (True, False), (True, False)],
+    [(False, False)],
+    [(True, False)],
+    [(True, False)],
+    [(False, True)],
+    [(False, False)],
+]
+ORDER = [
+    11, 1, 0, 5, 7, 4, 2, 10, 9, 3, 6, 8, 11, 1, 0, 11, 5, 11, 7, 4, 2, 10, 1, 9, 0, 3, 6, 8, 5,
+    11, 0, 7, 1, 0, 11, 11, 2, 2, 9, 4, 2, 10, 3, 10, 6, 10, 5, 0, 1, 8, 9, 1, 5, 2, 7, 11, 9,
+    1, 6, 5, 4, 10, 7, 9, 3, 8, 0, 5, 2, 6, 11, 7, 9, 1, 10, 4, 5, 0, 6, 2, 7, 10, 3, 9, 4, 6,
+    8, 3, 4, 1, 5, 8, 0, 3, 2, 7, 10, 8, 6, 0, 9, 2, 4, 7, 10, 3, 8, 0, 2, 10, 6, 4, 0, 2, 8, 3,
+    10,
+]
+
+
 def on_device(
     tokens,
     norm1_gain,
@@ -431,26 +854,63 @@
     grad_gain_one = jnp.sum(grad_normed * standard_one, axis=0)
     grad_bias_one = jnp.sum(grad_normed, axis=0)
     grad_inputs = grad_middle + norm_back(grad_normed, norm1_gain, standard_one, factor_one)
-    summed = lax.psum(
-        (
-            grad_gain_one,
-            grad_bias_one,
+    small = jnp.concatenate(
+        [
+            grad_gain_one[None],
+            grad_bias_one[None],
+            grad_taps,
+            grad_coef,
+            grad_rate,
+            grad_skip[None],
+            grad_gain_two[None],
+            grad_bias_two[None],
+        ],
+        axis=0,
+    )
+    small_rows = small.shape[0]
+    unit = 8 * lax.axis_size("seq")
+    small = jnp.pad(small, ((0, -small_rows % unit), (0, 0)))
+    (
+        grad_down,
+        grad_up,
+        grad_query_weight,
+        grad_key_weight,
+        grad_value_weight,
+        grad_out_weight,
+        small,
+    ) = all_sum(
+        [
+            grad_down,
+            grad_up,
             grad_query_weight,
             grad_key_weight,
             grad_value_weight,
-            grad_taps,
-            grad_coef,
-            grad_rate,
-            grad_skip,
             grad_out_weight,
-            grad_gain_two,
-            grad_bias_two,
-            grad_up,
-            grad_down,
-        ),
-        ("seq", "batch"),
-    )
-    return (token_order(mixed_out), token_order(grad_inputs)) + tuple(summed)
+            small,
+        ],
+        PLAN,
+        ORDER,
+    )
+    first = 2 + tap_count
+    second = first + 2 * states
+    return (
+        token_order(mixed_out),
+        token_order(grad_inputs),
+        small[0],
+        small[1],
+        grad_query_weight,
+        grad_key_weight,
+        grad_value_weight,
+        small[2:first],
+        small[first : first + states],
+        small[first + states : second],
+        small[second],
+        grad_out_weight,
+        small[second + 1],
+        small[second + 2],
+        grad_up,
+        grad_down,
+    )
 
 
 def solution(mesh):

time: 676 us -> 449 us (0.66)
  waiting for transfers between devices: 415 us -> 20.4 us
  Pallas kernels: 68.4 us -> 279 us
  blocking collectives: 44.3 us -> 0 us
    psum x1 -> x0, waiting for transfers between devices: 387 us -> none  [on_device(): lax.psum((grad_gain_one, grad_bias_one, grad_query_weight, grad_key_weigh...]
    pallas_call x0 -> x1, Pallas kernels: none -> 211 us  [all_sum(): pl.pallas_call(functools.partial(all_sum_body, len(arrays), line, bits, l...]
    psum x1 -> x0, blocking collectives: 44.3 us -> none  [on_device(): lax.psum((grad_gain_one, grad_bias_one, grad_query_weight, grad_key_weigh...]
    all_gather x2, waiting for transfers between devices: 27.2 us -> 19.6 us  [carried(): every = lax.all_gather(own, 'seq', axis=0)]
    unnamed x148 -> x130, local copies, waits for them, and re-layouts: 42.7 us -> 41 us
  transfers between devices with their start and end apart: 5 -> 4, of which waited for: 4 -> 2; matrix products, arithmetic and copies ran while one was open for 7% -> 9% of each run, Pallas kernels for 0% -> 0%
where the time goes in v2:
time: 449 us; the launch traced here: 444 us
  Pallas kernels  279 us (62%)
  matrix products  60.1 us (13%)
  local copies, waits for them, and re-layouts  54.7 us (12%)
  waiting for transfers between devices  20.4 us (5%)
  between operations  15.3 us (3%)
  other arithmetic  11.2 us (2%)
    pallas_call x1, Pallas kernels, all_sum(): pl.pallas_call(functools.partial(all_sum_body, len(arrays), line, bits, l...  211 us
    pallas_call x4, Pallas kernels, per_lanes(): pl.pallas_call(body, grid=(channels // LANES,), in_specs=[pl.BlockSpec((a...  67.7 us
    unnamed x130, local copies, waits for them, and re-layouts  41 us
    dot_general x6, matrix products, project(): return jnp.dot(rows_low, weight, preferred_element_type=jnp.float32)  21.9 us
    dot_general x6, matrix products, weight_grad(): lax.dot_general(rows_low, grads_low, (((0,), (0,)), ((), ())), preferred_...  20.1 us
    all_gather x2, waiting for transfers between devices, carried(): every = lax.all_gather(own, 'seq', axis=0)  19.6 us
    dot_general x6, matrix products, project_back(): lax.dot_general(grads_low, weight, (((1,), (1,)), ((), ())), preferred_el...  18.1 us
  transfers between devices with their start and end apart: 4, of which 2 were waited for; matrix products, arithmetic and copies ran while one was open for 9% of the time, Pallas kernels for 0%

profile of v2, /device:TPU:0, one launch (start us, length us, event | category | flops | bytes accessed | tf_op | source)
XLA Modules:
  0.0 444.4 jit_solution(4681335153315702707)
XLA Ops:
  7.3 1.7 copy.38
  13.3 2.4 collective-permute-start
  16.6 2.6 fusion.30
  19.2 9.0 %shard_map.279 = (f32[1024,768]{1,0:T(8,128)S(1)}, f32[64,768]{1,0:T(8,128)}) custom-call(f32[512,768]{1,0:T(8,128)S(1)} %get-tuple-element.74.rows_ref, f32[64,768]{1,0:T(8,128)S(1)} %copy-done.6), custom_call_target="tpu_custom_call" | custom-call | tf_op jit(solution)/shard_map/pallas_call | solution.py:282
  28.1 1.1 copy-done.1
  29.3 1.7 copy-done.11
  31.3 2.5 copy.41
  33.8 7.9 %fusion.34 = f32[512,3072]{1,0:T(8,128)} fusion(bf16[512,768]{1,0:T(8,128)(2,1)} %bitcast.84, bf16[3072,768]{1,0:T(8,128)(2,1)} %param.30), kind=kOutput, calls=%fused_computation.101 | convolution fusion | flops 2415919104 | bytes 11796480 | tf_op jit(solution)/shard_map/dot_general | solution.py:44
  41.7 19.6 %all-gather.5.cloned.1.call-done = f32[512,768]{1,0:T(8,128)} async-done(((f32[64,768]{1,0:T(8,128)}), f32[512,768]{1,0:T(8,128)}) %all-gather.5.cloned.1.call-update) | async-done | bytes 1572880 | tf_op jit(solution)/shard_map/all_gather | solution.py:296
  61.3 1.9 select_reduce_fusion.1.entering_ref
  63.3 1.9 copy-done.12
  65.2 17.8 %shard_map.280 = (f32[512,768]{1,0:T(8,128)S(1)}, f32[1024,768]{1,0:T(8,128)S(1)}, f32[32,768]{1,0:T(8,128)S(1)}) custom-call(f32[512,768]{1,0:T(8,128)S(1)} %copy-done.2, f32[1024,768]{1,0:T(8,128)S(1)} %copy-done.12, f32[64,768]{1,0:T(8,128)S(1)} %select_reduce_fusion.1.entering_ref, f32[64,768]{1,0:T(8,128)S(1)} %copy-done.6, f32[64,768]{1,0:T(8,128)S(1)} %copy-done.13, ...), custom_call_target="tpu_custom_call" | custom-call | tf_op jit(solution)/shard_map/pallas_call | solution.py:282
  86.5 2.1 copy-done.53
  88.6 8.4 %fusion.6 = (bf16[512,3072]{1,0:T(8,128)(2,1)S(1)}, f32[512,3072]{1,0:T(8,128)}) fusion(f32[512,3072]{1,0:T(8,128)S(1)} %copy-done.53, bf16[768,3072]{1,0:T(8,128)(2,1)S(1)} %bitcast.103, f32[512,768]{1,0:T(8,128)S(1)} %get-tuple-element.84, f32[768]{0:T(1024)S(1)} %copy-done.50, f32[768]{0:T(1024)S(1)} %copy-done.46, f32[512]{0:T(512)S(1)} %add_rsqrt_fusion.1, ...), kind=kOutput, calls=%fused_computation.8 | convolution fusion | flops 2449342464 | bytes 22030336 | tf_op jit(solution)/shard_map/dot_general | solution.py:40
  97.0 3.0 multiply_reduce_fusion
  100.7 1.8 multiply_reduce_fusion.1
  102.6 9.1 %shard_map.281 = (f32[1024,768]{1,0:T(8,128)S(1)}, f32[64,768]{1,0:T(8,128)}) custom-call(f32[512,768]{1,0:T(8,128)S(1)} %get-tuple-element.72.grads_ref, f32[64,768]{1,0:T(8,128)S(1)} %copy-done.6), custom_call_target="tpu_custom_call" | custom-call | tf_op jit(solution)/shard_map/pallas_call | solution.py:282
  111.7 1.1 copy-done.4
  112.8 1.7 copy-done.9
  114.5 8.4 %add_convert_fusion = bf16[512,768]{1,0:T(8,128)(2,1)S(1)} fusion(f32[512,768]{1,0:T(8,128)} %copy-done.21, bf16[3072,768]{1,0:T(8,128)(2,1)} %param.30, f32[512,3072]{1,0:T(8,128)} %get-tuple-element.86), kind=kOutput, calls=%fused_computation.53 | convolution fusion | flops 2430861312 | bytes 13369344 | tf_op jit(solution)/shard_map/dot_general | solution.py:40
  123.0 1.1 copy.40
  124.2 2.0 fusion.35
  126.2 2.2 fusion.37.refs_2_
  128.5 2.2 fusion.21.refs_5_
  131.7 5.5 %fusion.27.refs_1_ = f32[768,3072]{1,0:T(8,128)} fusion(bf16[512,3072]{1,0:T(8,128)(2,1)S(1)} %copy-done.52, f32[512,768]{1,0:T(8,128)S(1)} %copy-done.22, f32[768]{0:T(1024)S(1)} %copy-done.50, f32[768]{0:T(1024)S(1)} %copy-done.46, f32[512]{0:T(512)S(1)} %add_rsqrt_fusion.1, f32[512]{0:T(512)S(1)} %broadcast_multiply_fusion.5), kind=kOutput, calls=%fused_computation.94 | convolution fusion | flops 2417885184 | bytes 14166016 | tf_op jit(solution)/shard_map/dot_general | solution.py:50
  137.2 5.6 %fusion.29.refs_0_ = f32[3072,768]{1,0:T(8,128)} fusion(bf16[512,768]{1,0:T(8,128)(2,1)S(1)} %bitcast.85, f32[512,3072]{1,0:T(8,128)S(1)} %bitcast.105), kind=kOutput, calls=%fused_computation.96 | convolution fusion | flops 2430074880 | bytes 16515072 | tf_op jit(solution)/shard_map/dot_general | solution.py:50
  142.8 1.9 select_reduce_fusion.entering_ref
  144.8 1.4 copy-done.5
  146.2 1.9 copy-done.8
  148.1 1.9 copy-done.10
  150.0 31.8 %shard_map.282 = (f32[512,768]{1,0:T(8,128)S(1)}, f32[64,768]{1,0:T(8,128)S(1)}, f32[64,768]{1,0:T(8,128)S(1)}) custom-call(f32[512,768]{1,0:T(8,128)S(1)} %copy-done.5, f32[512,768]{1,0:T(8,128)S(1)} %copy-done.3, f32[1024,768]{1,0:T(8,128)S(1)} %copy-done.10, f32[1024,768]{1,0:T(8,128)S(1)} %copy-done.8, f32[64,768]{1,0:T(8,128)S(1)} %select_reduce_fusion.entering_ref, ...), custom_call_target="tpu_custom_call" | custom-call | tf_op jit(solution)/shard_map/pallas_call | solution.py:282
  182.7 1.5 collective-permute-start.1
  184.2 2.2 fusion.39.refs_4_
  188.6 2.2 fusion.38.refs_3_
  190.8 2.5 multiply_reduce_fusion.6
  194.6 211.0 %shard_map.283 = (f32[3072,768]{1,0:T(8,128)}, f32[768,3072]{1,0:T(8,128)}, f32[768,768]{1,0:T(8,128)}, f32[768,768]{1,0:T(8,128)}, f32[768,768]{1,0:T(8,128)}, /*index=5*/f32[768,768]{1,0:T(8,128)}, f32[192,768]{1,0:T(8,128)}) custom-call(f32[3072,768]{1,0:T(8,128)} %fusion.29.refs_0_, f32[768,3072]{1,0:T(8,128)} %fusion.27.refs_1_, ...), custom_call_target="tpu_custom_call" | custom-call | tf_op jit(solution)/shard_map/pallas_call | solution.py:695
  405.6 1.3 slice.89
  406.9 1.5 slice_reduce_fusion
  408.4 1.8 fusion.31
  410.2 2.9 multiply_add_fusion
  413.0 2.1 copy.43
  415.1 1.4 copy.58
  416.5 1.1 copy-done.32
  417.6 1.4 copy.59
  420.1 1.4 copy.60
  422.7 1.4 copy.61
  424.1 9.3 %copy.62 = f32[768,3072]{1,0:T(8,128)} copy(f32[768,3072]{1,0:T(8,128)} %get-tuple-element.121) | data formatting | bytes 18874368
  433.4 3.7 copy.63
  (171 shorter events, 16.9 us)
Async XLA Ops:
  7.2 9.4 %copy-start = (bf16[768,768]{1,0:T(8,128)(2,1)S(1)}, bf16[768,768]{1,0:T(8,128)(2,1)}, u32[]{:S(2)}) copy-start(bf16[768,768]{1,0:T(8,128)(2,1)} %param.21) | copy-start | bytes 3538948
  7.2 54.2 %all-gather.5.cloned.1.call-start = ((), (), s32[]{:S(2)}) async-start(), calls=%async_computation | async-start | bytes 1769472 | tf_op jit(solution)/shard_map/all_gather | solution.py:296
  9.0 75.7 %copy-start.14 = (f32[16,32,768]{2,0,1:T(8,128)}, f32[16,32,768]{2,0,1:T(8,128)S(1)}, u32[]{:S(2)}) copy-start(f32[16,32,768]{2,0,1:T(8,128)S(1)} %copy.38) | copy-start | bytes 4718596
  9.2 2.0 copy-start.43
  9.2 2.0 copy-start.45
  12.5 4.1 copy-start.16
  12.5 3.2 copy-start.44
  13.3 5.9 %copy-start.34 = (f32[512,768]{1,0:T(8,128)}, f32[512,768]{1,0:T(8,128)S(1)}, u32[]{:S(2)}) copy-start(f32[512,768]{1,0:T(8,128)S(1)} %fusion.33) | copy-start | bytes 4718596
  13.3 3.2 collective-permute-start
  16.6 2.6 copy-start.41
  16.6 2.6 copy-start.6
  19.2 12.1 %copy-start.47 = (f32[768]{0:T(1024)S(1)}, f32[768]{0:T(1024)}, u32[]{:S(2)}) copy-start(f32[768]{0:T(1024)} %param.25) | copy-start | bytes 9220
  31.0 111.9 %all-gather.7.cloned.1.call-start = ((), (), s32[]{:S(2)}) async-start(), calls=%async_computation.1 | async-start | bytes 1769472 | tf_op jit(solution)/shard_map/all_gather | solution.py:296
  41.7 21.6 %copy-start.13 = (f32[64,768]{1,0:T(8,128)S(1)}, f32[64,768]{1,0:T(8,128)}, u32[]{:S(2)}) copy-start(f32[64,768]{1,0:T(8,128)} %coef_ref.3) | copy-start | bytes 589828
  65.2 17.9 %copy-start.17 = (bf16[512,768]{1,0:T(8,128)(2,1)S(1)}, bf16[512,768]{1,0:T(8,128)(2,1)}, u32[]{:S(2)}) copy-start(bf16[512,768]{1,0:T(8,128)(2,1)} %copy-done.16) | copy-start | bytes 2359300
  65.2 17.9 %copy-start.39 = (bf16[768,768]{1,0:T(8,128)(2,1)S(1)}, bf16[768,768]{1,0:T(8,128)(2,1)}, u32[]{:S(2)}) copy-start(bf16[768,768]{1,0:T(8,128)(2,1)} %param.19) | copy-start | bytes 3538948
  65.2 21.3 %slice-start.3 = ((s8[4718592]{0:T(1024)(128)(4,1)}), s8[4194304]{0:T(1024)(128)(4,1)S(1)}, s32[]{:S(2)}) async-start(s8[4718592]{0:T(1024)(128)(4,1)} %bitcast.102), calls=%async_computation.5 | async-start | bytes 8388608
  83.1 2.2 copy-start.25
  83.1 3.4 slice-start.4
  85.2 3.4 copy-start.53
  86.1 14.0 %copy-start.21 = (f32[512,768]{1,0:T(8,128)}, f32[512,768]{1,0:T(8,128)S(1)}, u32[]{:S(2)}) copy-start(f32[512,768]{1,0:T(8,128)S(1)} %get-tuple-element.84) | copy-start | bytes 4718596
  86.1 2.5 copy-start.46
  86.1 2.5 copy-start.50
  97.0 3.0 copy-start.51
  97.0 3.1 copy-start.26
  114.5 9.6 %copy-start.40 = (bf16[768,768]{1,0:T(8,128)(2,1)S(1)}, bf16[768,768]{1,0:T(8,128)(2,1)}, u32[]{:S(2)}) copy-start(bf16[768,768]{1,0:T(8,128)(2,1)} %param.19) | copy-start | bytes 3538948
  124.1 2.1 copy-start.18
  126.2 2.2 copy-start.20
  126.2 2.2 copy-start.24
  128.4 2.3 copy-start.22
  128.4 3.2 copy-start.52
  128.5 8.7 %slice-start.5 = ((s8[6291456]{0:T(1024)(128)(4,1)}), s8[4194304]{0:T(1024)(128)(4,1)S(1)}, s32[]{:S(2)}) async-start(s8[6291456]{0:T(1024)(128)(4,1)} %bitcast.104), calls=%async_computation.7 | async-start | bytes 8388608
  131.7 5.5 %copy-start.27 = (bf16[16,32,768]{2,0,1:T(8,128)(2,1)S(1)}, bf16[16,32,768]{2,0,1:T(8,128)(2,1)}, u32[]{:S(2)}) copy-start(bf16[16,32,768]{2,0,1:T(8,128)(2,1)} %copy.41) | copy-start | bytes 2359300
  131.7 5.5 %slice-start.6 = ((s8[6291456]{0:T(1024)(128)(4,1)}), s8[2097152]{0:T(1024)(128)(4,1)S(1)}, s32[]{:S(2)}) async-start(s8[6291456]{0:T(1024)(128)(4,1)} %bitcast.104), calls=%async_computation.8 | async-start | bytes 4194304
  150.0 31.8 %copy-start.35 = (f32[512,768]{1,0:T(8,128)S(1)}, f32[512,768]{1,0:T(8,128)}, u32[]{:S(2)}) copy-start(f32[512,768]{1,0:T(8,128)} %copy-done.34) | copy-start | bytes 4718596
  150.0 31.9 %copy-start.37 = (f32[512,768]{1,0:T(8,128)S(1)}, f32[512,768]{1,0:T(8,128)}, u32[]{:S(2)}) copy-start(f32[512,768]{1,0:T(8,128)} %get-tuple-element.75) | copy-start | bytes 4718596
  150.0 31.9 %copy-start.38 = (f32[512,768]{1,0:T(8,128)S(1)}, f32[512,768]{1,0:T(8,128)}, u32[]{:S(2)}) copy-start(f32[512,768]{1,0:T(8,128)} %get-tuple-element.80) | copy-start | bytes 4718596
  150.0 31.9 %copy-start.42 = (f32[3,16,768]{2,1,0:T(8,128)S(1)}, f32[3,16,768]{2,1,0:T(8,128)}, u32[]{:S(2)}) copy-start(f32[3,16,768]{2,1,0:T(8,128)} %copy-done.41) | copy-start | bytes 442372
  182.7 3.8 collective-permute-start.1
  188.5 2.2 copy-start.15
  188.6 2.2 copy-start.36
  413.0 2.1 copy-start.33
  415.1 2.5 copy-start.32
  417.6 2.5 copy-start.31
  420.1 2.5 copy-start.30
  422.7 10.7 %slice-start = ((s8[9437184]{0:T(1024)(128)(4,1)}), s8[4194304]{0:T(1024)(128)(4,1)S(1)}, s32[]{:S(2)}) async-start(s8[9437184]{0:T(1024)(128)(4,1)} %bitcast.79), calls=%async_computation.2 | async-start | bytes 8388608
  424.1 9.3 %slice-start.1 = ((s8[9437184]{0:T(1024)(128)(4,1)}), s8[4194304]{0:T(1024)(128)(4,1)S(1)}, s32[]{:S(2)}) async-start(s8[9437184]{0:T(1024)(128)(4,1)} %bitcast.79), calls=%async_computation.3 | async-start | bytes 8388608
  424.1 9.3 %slice-start.2 = ((s8[9437184]{0:T(1024)(128)(4,1)}), s8[1048576]{0:T(1024)(128)(4,1)S(1)}, s32[]{:S(2)}) async-start(s8[9437184]{0:T(1024)(128)(4,1)} %bitcast.79), calls=%async_computation.4 | async-start | bytes 2097152
  (17 other events, 26.9 us)
Sparse Core Ops, SparseCore 0:
  31.1 30.2 all-gather.4
  114.6 25.6 all-gather.6

commit v3 on v2

--- a/solution.py
+++ b/solution.py
@@ -88,42 +88,26 @@
     last_ref[...] = held
 
 
-def forward_mix(
-    width,
-    rows_ref,
-    sums_ref,
-    entering_ref,
-    rate_ref,
-    coef_ref,
-    skip_ref,
-    mixed_ref,
-    held_ref,
-    kernel_ref,
-    decay_ref,
-    taps_ref,
+def forward_near(
+    width, rows_ref, rate_ref, coef_ref, skip_ref, mixed_ref, kernel_ref, taps_ref
 ):
     states = rate_ref.shape[0]
-    decay_ref[...] = jnp.exp(-rate_ref[...])
-    hop = jnp.exp(-width * rate_ref[...])
-    held = entering_ref[...]
-    for chunk in range(CHUNKS):
-        held_ref[chunk_rows(chunk, states), :] = held
-        held = hop * held + sums_ref[chunk_rows(chunk, states), :]
     lags = lax.broadcasted_iota(jnp.int32, (8, LANES), 0).astype(jnp.float32)
 
-    def add_state(state, totals):
-        rate = rate_ref[pl.ds(state, 1), :]
-        term = coef_ref[pl.ds(state, 1), :] * jnp.exp(-rate * lags)
-        step = jnp.exp(-8.0 * rate)
-        out = []
-        for total in totals:
-            out.append(total + term)
-            term = term * step
-        return tuple(out)
-
-    totals = lax.fori_loop(
-        0, states, add_state, tuple(jnp.zeros((8, LANES), jnp.float32) for _ in range(width // 8))
-    )
+    def add_states(group, totals):
+        members = pl.ds(pl.multiple_of(group * GROUP, GROUP), GROUP)
+        rates, coefs = rate_ref[members, :], coef_ref[members, :]
+        steps = jnp.exp(-8.0 * rates)
+        totals = list(totals)
+        for i in range(GROUP):
+            term = coefs[i : i + 1] * jnp.exp(-rates[i : i + 1] * lags)
+            for place in range(width // 8):
+                totals[place] = totals[place] + term
+                term = term * steps[i : i + 1]
+        return tuple(totals)
+
+    zero = jnp.zeros((8, LANES), jnp.float32)
+    totals = lax.fori_loop(0, states // GROUP, add_states, (zero,) * (width // 8))
     kernel_ref[...] = jnp.concatenate(totals, axis=0)
     for lag in range(width):
         taps_ref[lag * CHUNKS : (lag + 1) * CHUNKS, :] = jnp.broadcast_to(
@@ -139,6 +123,18 @@
         for i in range(4):
             mixed_ref[(start + i) * CHUNKS : (start + i + 1) * CHUNKS, :] = sums[i]
 
+
+def forward_far(
+    width, sums_ref, entering_ref, rate_ref, coef_ref, mixed_ref, held_ref, decay_ref
+):
+    states = rate_ref.shape[0]
+    decay_ref[...] = jnp.exp(-rate_ref[...])
+    hop = jnp.exp(-width * rate_ref[...])
+    held = entering_ref[...]
+    for chunk in range(CHUNKS):
+        held_ref[chunk_rows(chunk, states), :] = held
+        held = hop * held + sums_ref[chunk_rows(chunk, states), :]
+
     def body(group, unused):
         decay = decay_ref[pl.ds(group * GROUP, GROUP), :][:, None, :]
         coef = coef_ref[pl.ds(group * GROUP, GROUP), :][:, None, :]
@@ -174,15 +170,13 @@
     first_ref[...] = held
 
 
-def backward_mix(
+def backward_near(
     width,
     grads_ref,
     rows_ref,
     sums_ref,
-    held_ref,
     entering_ref,
     rate_ref,
-    coef_ref,
     skip_ref,
     kernel_ref,
     back_ref,
@@ -195,7 +189,6 @@
     lag_ref,
 ):
     states = rate_ref.shape[0]
-    decay_ref[...] = jnp.exp(-rate_ref[...])
     hop = jnp.exp(-width * rate_ref[...])
     hop_ref[...] = hop
     held = entering_ref[...]
@@ -233,6 +226,22 @@
     coef_grad_ref[...] = near_coef
     rate_grad_ref[...] = near_rate
 
+
+def backward_far(
+    width,
+    grads_ref,
+    rows_ref,
+    sums_ref,
+    held_ref,
+    coef_ref,
+    back_ref,
+    coef_grad_ref,
+    rate_grad_ref,
+    decay_ref,
+    hop_ref,
+    after_ref,
+    groups,
+):
     def body(group, unused):
         members = pl.ds(group * GROUP, GROUP)
         cells = pl.ds(group * GROUP * CHUNKS, GROUP * CHUNKS)
@@ -272,32 +281,7 @@
         rate_grad_ref[members, :] += jnp.sum(total, axis=1)
         return unused
 
-    lax.fori_loop(0, states // GROUP, body, 0)
-    rate_grad_ref[...] = -coef_ref[...] * rate_grad_ref[...]
-
-
-def per_lanes(body, out_rows, scratch, *arrays):
-    channels = arrays[0].shape[1]
-    scratch = [pltpu.VMEM((rows, LANES), jnp.float32) for rows in scratch]
-    return pl.pallas_call(
-        body,
-        grid=(channels // LANES,),
-        in_specs=[pl.BlockSpec((array.shape[0], LANES), lambda i: (0, i)) for array in arrays],
-        out_specs=[pl.BlockSpec((rows, LANES), lambda i: (0, i)) for rows in out_rows],
-        out_shape=[jax.ShapeDtypeStruct((rows, channels), jnp.float32) for rows in out_rows],
-        scratch_shapes=scratch,
-        compiler_params=pltpu.CompilerParams(vmem_limit_bytes=40 * 2**20),
-    )(*arrays)
-
-
-def carried(own, rate, row_count, forward):
-    count = lax.axis_size("seq")
-    place = lax.axis_index("seq")
-    every = lax.all_gather(own, "seq", axis=0)
-    source = jnp.arange(count)
-    hops = place - 1 - source if forward else source - 1 - place
-    decays = jnp.exp(-rate[None] * (row_count * jnp.maximum(hops, 0)).astype(jnp.float32)[:, None, None])
-    return jnp.sum(jnp.where(hops[:, None, None] >= 0, every * decays, 0.0), axis=0)
+    lax.fori_loop(groups.start, groups.stop, body, 0)
 
 
 MESH = pl.DeviceIdType.MESH
@@ -322,14 +306,14 @@
 
 
 class Lane:
-    def __init__(self, array, start, rows, columns, bits, line_first):
+    def __init__(self, array, start, rows, columns, bits, line_first, in_place):
         self.array, self.start, self.rows, self.columns = array, start, rows, columns
-        self.bits, self.line_first = bits, line_first
+        self.bits, self.line_first, self.in_place = bits, line_first, in_place
 
     def buffers(self, line):
         half = self.rows // 2
         unit = half // line if self.line_first else half >> len(self.bits)
-        counts = [half, half]
+        counts = [half] if self.in_place else [half, half]
         size = half // line if self.line_first else half
         for unused in self.bits:
             size //= 2
@@ -343,6 +327,8 @@
 
 
 def lane_steps(lane, line, source, target, buffers, send_sems, recv_sems, first_sem, pending):
+    if lane.in_place:
+        buffers = [source] + buffers
     acc, fin = buffers[:2]
     landing = buffers[2 : 2 + len(lane.bits)]
     chain = buffers[-1]
@@ -379,18 +365,26 @@
 
     mine = lane.start + core * half
     other = lane.start + (1 - core) * half
-    load_index, swap_index = fresh(), fresh()
-    load = pltpu.make_async_copy(rows_of(source, mine, half), acc, recv_sems.at[load_index])
-    swap = remote(rows_of(source, other, half), fin, swap_index, partner(1))
-
-    def begin():
-        load.start()
-        swap.start()
-
-    def add_swap():
-        load.wait()
-        swap.wait_recv()
-        add_rows(acc, 0, acc, 0, fin, 0, half)
+    base_row = mine if lane.in_place else 0
+    swap = remote(rows_of(source, other, half), fin, fresh(), partner(1))
+    if lane.in_place:
+        begin = swap.start
+
+        def add_swap():
+            swap.wait_recv()
+            add_rows(acc, mine, acc, mine, fin, 0, half)
+
+    else:
+        load = pltpu.make_async_copy(rows_of(source, mine, half), acc, recv_sems.at[fresh()])
+
+        def begin():
+            load.start()
+            swap.start()
+
+        def add_swap():
+            load.wait()
+            swap.wait_recv()
+            add_rows(acc, 0, acc, 0, fin, 0, half)
 
     pending.append(swap.wait_send)
     steps = [[begin], [add_swap]]
@@ -407,7 +401,7 @@
             size //= 2
             start = starts[-1]
             copy = remote(
-                rows_of(acc, start + (1 - side(bit)) * size, size),
+                rows_of(acc, base_row + start + (1 - side(bit)) * size, size),
                 landing[place],
                 fresh(),
                 partner(bit),
@@ -419,7 +413,8 @@
 
             def receive(copy=copy, own=own, size=size, place=place, last=last):
                 copy.wait_recv()
-                add_rows(fin if final and last else acc, own, acc, own, landing[place], 0, size)
+                out, out_row = (fin, own) if final and last else (acc, base_row + own)
+                add_rows(out, out_row, acc, base_row + own, landing[place], 0, size)
 
             step(receive)
             starts.append(own)
@@ -455,23 +450,23 @@
 
         for level in range(middle):
             copy = remote(
-                rows_of(acc, at, size), rows_of(chain, level * size, size), fresh(), inward
+                rows_of(acc, base_row + at, size), rows_of(chain, level * size, size), fresh(), inward
             )
             join(on(level, copy.start))
             pending.append(on(level, copy.wait_send))
 
             def receive(copy=copy, level=level):
                 copy.wait_recv()
-                add_rows(acc, at, acc, at, chain, level * size, size)
+                add_rows(acc, base_row + at, acc, base_row + at, chain, level * size, size)
 
             step(on(level + 1, receive))
-        copy = remote(rows_of(acc, at, size), rows_of(chain, middle * size, size), fresh(), across)
+        copy = remote(rows_of(acc, base_row + at, size), rows_of(chain, middle * size, size), fresh(), across)
         join(on(middle, copy.start))
         pending.append(on(middle, copy.wait_send))
 
         def receive_across(copy=copy):
             copy.wait_recv()
-            add_rows(fin, at, acc, at, chain, middle * size, size)
+            add_rows(fin, at, acc, base_row + at, chain, middle * size, size)
 
         step(on(middle, receive_across))
         for level in range(middle - 1, -1, -1):
@@ -498,7 +493,7 @@
         def hop(place, member, step_to):
             slot = line if step_to < 0 and member == place - 1 else member
             return remote(
-                rows_of(acc, member * unit, unit),
+                rows_of(acc, base_row + member * unit, unit),
                 rows_of(chain, slot * unit, unit),
                 slots[slot],
                 (me, place + step_to),
@@ -506,12 +501,13 @@
 
         def arrived(place, slot, member):
             remote(
-                rows_of(acc, member * unit, unit),
+                rows_of(acc, base_row + member * unit, unit),
                 rows_of(chain, slot * unit, unit),
                 slots[slot],
                 beside(place),
             ).wait_recv()
-            add_rows(acc, member * unit, acc, member * unit, chain, slot * unit, unit)
+            row = base_row + member * unit
+            add_rows(acc, row, acc, row, chain, slot * unit, unit)
 
         for turn in range(line - 1):
 
@@ -623,16 +619,107 @@
 def turn_order(lengths, order):
     if [order.count(place) for place in range(len(lengths))] == lengths:
         return order
-    turns = range(max(lengths))
-    return [place for turn in turns for place, length in enumerate(lengths) if turn < length]
-
-
-def all_sum_body(count, line, bits, lanes, order, *refs):
-    sources, targets = refs[:count], refs[count : 2 * count]
-    send_sems, recv_sems = refs[-2:]
-    buffers = list(refs[2 * count : -2])
-    me = lax.axis_index("seq")
-    z = lax.axis_index("batch")
+    last = len(lengths) - 1
+    turns = range(max(lengths[:-1], default=0))
+    lanes = [place for turn in turns for place in range(last) if turn < lengths[place]]
+    return [last] * lengths[last] + lanes
+
+
+class Loop:
+    def __init__(self, count, *parts):
+        self.count, self.parts = count, parts
+
+    def steps(self):
+        return self.count * len(self.parts)
+
+
+def call_all(functions):
+    for function in functions:
+        function()
+
+
+def run_loop(loop, between):
+    parts = len(loop.parts)
+
+    def body(i, unused):
+        for place, part in enumerate(loop.parts):
+            part(i)
+            for turn in range(loop.count):
+                functions = between[turn * parts + place]
+                if functions:
+                    pl.when(i == turn)(functools.partial(call_all, functions))
+        return unused
+
+    lax.fori_loop(0, loop.count, body, 0)
+
+
+def run_programs(programs, work, order):
+    lengths = [len(program) for program in programs]
+    lengths.append(sum(item.steps() if isinstance(item, Loop) else 1 for item in work))
+    order = turn_order(lengths, order)
+    programs, work = [list(program) for program in programs], list(work)
+    last = len(programs)
+    at = 0
+    while at < len(order):
+        if order[at] != last:
+            call_all(programs[order[at]].pop(0))
+            at += 1
+            continue
+        item = work.pop(0)
+        at += 1
+        if not isinstance(item, Loop):
+            item()
+            continue
+        between = [[]]
+        while len(between) < item.steps():
+            if order[at] == last:
+                between.append([])
+            else:
+                between[-1] += programs[order[at]].pop(0)
+            at += 1
+        run_loop(item, between + [[]])
+
+
+def state_exchange(bits, row_count, rate, totals, arrivals, entering, sends, receives, forward):
+    me, z = lax.axis_index("seq"), lax.axis_index("batch")
+
+    def copy(level):
+        bit = bits[level]
+        return pltpu.make_async_remote_copy(
+            src_ref=totals[level],
+            dst_ref=arrivals[level],
+            send_sem=sends.at[level],
+            recv_sem=receives.at[level],
+            device_id=(me + bit * (1 - 2 * ((me // bit) % 2)), z),
+            device_id_type=MESH,
+        )
+
+    def arrive(level):
+        bit = bits[level]
+        copy(level).wait_recv()
+        place = me % bit
+        after = (me // bit) % 2 == (1 if forward else 0)
+        hops = (row_count * (place if forward else bit - 1 - place)).astype(jnp.float32)
+        term = jnp.exp(-rate[...] * hops) * arrivals[level][...]
+        term = jnp.where(after, term, 0.0)
+        entering[...] = term if level == 0 else entering[...] + term
+        if level + 1 < len(bits):
+            far = jnp.exp(-float(row_count * bit) * rate[...])
+            ours, theirs = totals[level][...], arrivals[level][...]
+            totals[level + 1][...] = jnp.where(after, ours + far * theirs, theirs + far * ours)
+            copy(level + 1).start()
+
+    return copy, arrive
+
+
+def forward_body(row_count, bits, *refs):
+    width = row_count // CHUNKS
+    product, rate, coef, skip, mixed, held, kernel, sums, taps, decay, entering = refs[:11]
+    levels = len(bits)
+    totals, arrivals = refs[11 : 11 + levels], refs[11 + levels : 11 + 2 * levels]
+    sends, receives = refs[-2:]
+    tiles = product.shape[1] // LANES
+    me, z = lax.axis_index("seq"), lax.axis_index("batch")
     barrier = pltpu.get_barrier_semaphore()
     for bit in bits:
         pl.semaphore_signal(
@@ -641,85 +728,425 @@
             device_id=(me + bit * (1 - 2 * ((me // bit) % 2)), z),
             device_id_type=MESH,
         )
-
-    @pl.when(z > 0)
-    def left():
-        pl.semaphore_signal(barrier, inc=1, device_id=(me, z - 1), device_id_type=MESH)
-
-    @pl.when(z < line - 1)
-    def right():
-        pl.semaphore_signal(barrier, inc=1, device_id=(me, z + 1), device_id_type=MESH)
-
+    pl.semaphore_wait(barrier, levels)
+    copy, arrive = state_exchange(
+        bits, row_count, rate, totals, arrivals, entering, sends, receives, True
+    )
+
+    def columns(tile):
+        return pl.ds(pl.multiple_of(tile * LANES, LANES), LANES)
+
+    def states_tile(tile):
+        here = columns(tile)
+        forward_states(
+            width, product.at[:, here], rate.at[:, here], sums.at[tile], totals[0].at[:, here], decay
+        )
+
+    def near_tile(tile):
+        here = columns(tile)
+        forward_near(
+            width,
+            product.at[:, here],
+            rate.at[:, here],
+            coef.at[:, here],
+            skip.at[:, here],
+            mixed.at[:, here],
+            kernel.at[:, here],
+            taps,
+        )
+
+    def far_tile(tile):
+        here = columns(tile)
+        forward_far(
+            width,
+            sums.at[tile],
+            entering.at[:, here],
+            rate.at[:, here],
+            coef.at[:, here],
+            mixed.at[:, here],
+            held.at[tile],
+            decay,
+        )
+
+    run_loop(Loop(tiles, states_tile), [[] for unused in range(tiles)])
+    copy(0).start()
+    between = [[] for unused in range(tiles)]
+    for level in range(levels):
+        between[(level + 1) * tiles // levels - 1].append(functools.partial(arrive, level))
+    run_loop(Loop(tiles, near_tile), between)
+    run_loop(Loop(tiles, far_tile), [[] for unused in range(tiles)])
+    for level in range(levels):
+        copy(level).wait_send()
+
+
+def forward_mixing(row_count, product, rate, coef, skip):
+    size = lax.axis_size("seq")
+    bits = [1 << place for place in range(size.bit_length() - 1)]
+    states, channels = rate.shape
+    tiles, width = channels // LANES, row_count // CHUNKS
+    whole = pl.BlockSpec(memory_space=pltpu.VMEM)
+    scratch = [(tiles, states * CHUNKS, LANES), (row_count, LANES), (states, LANES)]
+    scratch += [(states, channels)] * (1 + 2 * len(bits))
+    shapes = [(row_count, channels), (tiles, states * CHUNKS, LANES), (width, channels)]
+    return pl.pallas_call(
+        functools.partial(forward_body, row_count, bits),
+        out_shape=[jax.ShapeDtypeStruct(shape, jnp.float32) for shape in shapes],
+        in_specs=[whole] * 4,
+        out_specs=[whole] * 3,
+        scratch_shapes=[pltpu.VMEM(shape, jnp.float32) for shape in scratch]
+        + [pltpu.SemaphoreType.DMA((len(bits),))] * 2,
+        compiler_params=pltpu.CompilerParams(
+            collective_id=1, has_side_effects=True, vmem_limit_bytes=40 * 2**20
+        ),
+    )(product, rate, coef, skip)
+
+
+NAMES = ["down", "up", "out", "grad_mixed", "product", "held", "values", "keys_mixed", "key_rows"]
+NAMES += ["standard", "factor", "grad_middle", "query_weight", "key_weight", "value_weight"]
+RESIDENT = ["rate", "coef", "skip", "taps", "kernel", "gain", "normed_turned", "grad_queries"]
+RESIDENT += ["small"]
+ROWS_AT_ONCE = 64
+
+
+def backward_body(row_count, size, line, bits, lanes, order, *refs):
+    width = row_count // CHUNKS
+    counts = [len(NAMES) + len(RESIDENT), 8]
+    given = dict(zip(NAMES + RESIDENT, refs[: counts[0]]))
+    results = refs[counts[0] : sum(counts)]
+    rest = list(refs[sum(counts) :])
+    send_sems, recv_sems, load_sems, swap_send, swap_recv = rest[-5:]
+    rest = rest[:-5]
+
+    def take(count):
+        taken = rest[:count]
+        del rest[:count]
+        return taken
+
+    (grad_query, grad_value, grad_key, small) = take(4)
+    (lanes_g, lanes_x, lanes_back, lanes_taps, lanes_other) = take(5)
+    (lanes_held, lanes_sums, lanes_after) = take(3)
+    (decay, hop, lag, first) = take(4)
+    (grad_keys_mixed, values_low, keys_low, weight, entering) = take(5)
+    (block_a, block_b, block_c, block_f, edge_out, edge_in) = take(6)
+    levels = len(bits)
+    totals, arrivals = take(levels), take(levels)
+
+    me = lax.axis_index("seq")
+    z = lax.axis_index("batch")
+    channels = small.shape[1]
+    tiles = channels // LANES
+    rate, coef = given["rate"], given["coef"]
+    states = rate.shape[0]
+    tap_count = given["taps"].shape[0]
+    halo = tap_count - 1
+
+    barrier = pltpu.get_barrier_semaphore()
+
+    def greet(device):
+        pl.semaphore_signal(barrier, inc=1, device_id=device, device_id_type=MESH)
+
+    for bit in bits:
+        greet((me + bit * (1 - 2 * ((me // bit) % 2)), z))
+    pl.when(z > 0)(lambda: greet((me, z - 1)))
+    pl.when(z < line - 1)(lambda: greet((me, z + 1)))
+    pl.when(me > 0)(lambda: greet((me - 1, z)))
+    pl.when(me < size - 1)(lambda: greet((me + 1, z)))
     pl.semaphore_wait(
-        barrier, len(bits) + jnp.where(z > 0, 1, 0) + jnp.where(z < line - 1, 1, 0)
+        barrier,
+        len(bits)
+        + jnp.where(z > 0, 1, 0)
+        + jnp.where(z < line - 1, 1, 0)
+        + jnp.where(me > 0, 1, 0)
+        + jnp.where(me < size - 1, 1, 0),
     )
-    pending = []
+
+    def columns(tile):
+        return pl.ds(pl.multiple_of(tile * LANES, LANES), LANES)
+
+    def fetch(*pairs):
+        copies = [
+            pltpu.make_async_copy(source, target, load_sems.at[i])
+            for i, (source, target) in enumerate(pairs)
+        ]
+        for copy in copies:
+            copy.start()
+        for copy in copies:
+            copy.wait()
+
+    exchange, arrive = state_exchange(
+        bits, row_count, rate, totals, arrivals, entering, swap_send, swap_recv, False
+    )
+
+    def states_of(tile, target):
+        backward_states(width, lanes_g, rate.at[:, columns(tile)], lanes_sums, target, decay)
+
+    def first_tile(tile):
+        fetch((given["grad_mixed"].at[:, columns(tile)], lanes_g))
+        states_of(tile, totals[0].at[:, columns(tile)])
+
+    def weight_sum(target, grads):
+        def body(i):
+            rows = pl.ds(pl.multiple_of(i * 256, 256), 256)
+            target[rows, :] = jnp.dot(
+                given["normed_turned"][rows, :], grads[...], preferred_element_type=jnp.float32
+            )
+
+        return Loop(channels // 256, body)
+
+    def second_fetch(tile):
+        here = columns(tile)
+        fetch(
+            (given["grad_mixed"].at[:, here], lanes_g),
+            (given["product"].at[:, here], lanes_x),
+            (given["held"].at[tile], lanes_held),
+            (given["values"].at[:, here], lanes_other.at[:row_count]),
+        )
+        states_of(tile, first)
+
+    def second_near(tile):
+        here = columns(tile)
+        backward_near(
+            width,
+            lanes_g,
+            lanes_x,
+            lanes_sums,
+            entering.at[:, here],
+            rate.at[:, here],
+            given["skip"].at[:, here],
+            given["kernel"].at[:, here],
+            lanes_back,
+            small.at[0:states, here],
+            small.at[states : 2 * states, here],
+            decay,
+            hop,
+            lanes_taps,
+            lanes_after,
+            lag,
+        )
+
+    def second_far(half):
+        def part(tile):
+            here = columns(tile)
+            groups = states // GROUP // 2
+            backward_far(
+                width,
+                lanes_g,
+                lanes_x,
+                lanes_sums,
+                lanes_held,
+                coef.at[:, here],
+                lanes_back,
+                small.at[0:states, here],
+                small.at[states : 2 * states, here],
+                decay,
+                hop,
+                lanes_after,
+                range(half * groups, (half + 1) * groups),
+            )
+
+        return part
+
+    def second_end(tile):
+        here = columns(tile)
+        row = 2 * states + tap_count
+        small[row : row + 1, here] = jnp.sum(lanes_g[...] * lanes_x[...], axis=0, keepdims=True)
+        small[states : 2 * states, here] = -coef[:, here] * small[states : 2 * states, here]
+        grad_keys_mixed[0:row_count, here] = lanes_back[...] * lanes_other[0:row_count, :]
+        fetch((given["keys_mixed"].at[:, here], lanes_x))
+        values_low[:, here] = (lanes_back[...] * lanes_x[...]).astype(jnp.bfloat16)
+
+    def send_edge():
+        edge_out[...] = jnp.zeros(edge_out.shape, jnp.float32)
+        for place in range(halo):
+            edge_out[place : place + 1, :] = grad_keys_mixed[place * CHUNKS : place * CHUNKS + 1, :]
+        pl.when(me > 0)(edge(me - 1).start)
+
+        @pl.when(me == size - 1)
+        def at_end():
+            edge_in[...] = jnp.zeros(edge_in.shape, jnp.float32)
+
+    def edge(device):
+        return pltpu.make_async_remote_copy(
+            src_ref=edge_out,
+            dst_ref=edge_in,
+            send_sem=swap_send.at[levels],
+            recv_sem=swap_recv.at[levels],
+            device_id=(device, z),
+            device_id_type=MESH,
+        )
+
+    def keys_tile(tile):
+        here = columns(tile)
+        fetch((given["key_rows"].at[:, here], lanes_other))
+        for place in range(halo):
+            rows = grad_keys_mixed[place * CHUNKS : (place + 1) * CHUNKS, here]
+            start = row_count + place * CHUNKS
+            grad_keys_mixed[start : start + CHUNKS, here] = jnp.concatenate(
+                [rows[1:], edge_in[place : place + 1, here]], axis=0
+            )
+        tap = given["taps"]
+        total = tap[0:1, here] * grad_keys_mixed[0:row_count, here]
+        for offset in range(1, tap_count):
+            start = offset * CHUNKS
+            total = total + tap[offset : offset + 1, here] * (
+                grad_keys_mixed[start : start + row_count, here]
+            )
+        keys_low[:, here] = total.astype(jnp.bfloat16)
+        grads = grad_keys_mixed[0:row_count, here]
+        for offset in range(tap_count):
+            start = (halo - offset) * CHUNKS
+            row = 2 * states + offset
+            small[row : row + 1, here] = jnp.sum(
+                grads * lanes_other[start : start + row_count, :], axis=0, keepdims=True
+            )
+
+    back = grad_keys_mixed
+
+    def back_sum(index, grads):
+        def body(i):
+            rows = pl.ds(pl.multiple_of(i * 128, 128), 128)
+            term = lax.dot_general(
+                grads[rows, :],
+                weight[...],
+                (((1,), (1,)), ((), ())),
+                preferred_element_type=jnp.float32,
+            )
+            back[rows, :] = term if index == 0 else back[rows, :] + term
+
+        return Loop(row_count // 128, body)
+
+    def norm_rows(i):
+        rows = pl.ds(pl.multiple_of(i * ROWS_AT_ONCE, ROWS_AT_ONCE), ROWS_AT_ONCE)
+        fetch(
+            (given["standard"].at[rows, :], block_a),
+            (given["grad_middle"].at[rows, :], block_b),
+            (given["factor"].at[rows, :], block_f),
+        )
+        grads, standard = back[rows, :], block_a[...]
+        block_c[...] = block_b[...] + norm_back(grads, given["gain"][...], standard, block_f[:, 0:1])
+        fetch((block_c, results[7].at[rows, :]))
+        row = 2 * states + tap_count + 1
+        small[row : row + 1, :] += jnp.sum(grads * standard, axis=0, keepdims=True)
+        small[row + 1 : row + 2, :] += jnp.sum(grads, axis=0, keepdims=True)
+
+    def begin():
+        small[...] = given["small"][...]
+
+    work = [begin, Loop(tiles, first_tile), exchange(0).start]
+    work.append(weight_sum(grad_query, given["grad_queries"]))
+    for level in range(levels):
+        work.append(functools.partial(arrive, level))
+    parts = (second_fetch, second_near, second_far(0), second_far(1), second_end)
+    work.append(Loop(tiles, *parts))
+    work.append(send_edge)
+    work.append(weight_sum(grad_value, values_low))
+    work.append(lambda: pl.when(me < size - 1)(edge(me + 1).wait_recv))
+    work.append(Loop(tiles, keys_tile))
+    work.append(weight_sum(grad_key, keys_low))
+    chain = (
+        (given["query_weight"], given["grad_queries"]),
+        (given["key_weight"], keys_low),
+        (given["value_weight"], values_low),
+    )
+    for index, (source, grads) in enumerate(chain):
+        work.append(functools.partial(fetch, (source, weight)))
+        work.append(back_sum(index, grads))
+    work.append(Loop(row_count // ROWS_AT_ONCE, norm_rows))
+
+    sources = [given["down"], given["up"], given["out"], grad_query, grad_value, grad_key, small]
+    pending = [exchange(level).wait_send for level in range(levels)]
+    pending.append(lambda: pl.when(me > 0)(edge(me - 1).wait_send))
     programs = []
-    first = 0
+    start = 0
     for lane in lanes:
-        own = [buffers.pop(0) for unused in lane.buffers(line)]
         programs.append(
             lane_steps(
                 lane,
                 line,
                 sources[lane.array],
-                targets[lane.array],
-                own,
+                results[lane.array],
+                take(len(lane.buffers(line))),
                 send_sems,
                 recv_sems,
-                first,
+                start,
                 pending,
             )
         )
-        first += lane.copies(line)
-    for place in turn_order([len(program) for program in programs], order):
-        for function in programs[place].pop(0):
-            function()
+        start += lane.copies(line)
+    run_programs(programs, work, order)
     for wait in pending:
         wait()
 
 
-def all_sum(arrays, plan, order):
+def backward(row_count, arrays, resident, plan, order):
     size, line = lax.axis_size("seq"), lax.axis_size("batch")
     bits = [1 << place for place in range(size.bit_length() - 1)]
+    channels = arrays["down"].shape[1]
+    states = resident["rate"].shape[0]
+    cells = states * CHUNKS
+    small_rows = resident["small"].shape[0]
+    square = (channels, channels)
+    shapes = [arrays["down"].shape, arrays["up"].shape] + [square] * 4 + [(small_rows, channels)]
     lanes = []
-    for index, array in enumerate(arrays):
-        rows = array.shape[0] // len(plan[index])
+    for index, shape in enumerate(shapes):
+        rows = shape[0] // len(plan[index])
         for piece, (flipped, line_first) in enumerate(plan[index]):
             if rows % (8 * size * line):
                 line_first = False
             path = bits[:0:-1] if flipped else bits[1:]
-            lanes.append(Lane(index, piece * rows, rows, array.shape[1], path, line_first))
-    scratch = [buffer for lane in lanes for buffer in lane.buffers(line)]
+            lanes.append(Lane(index, piece * rows, rows, shape[1], path, line_first, index > 2))
+    key_rows = arrays["key_rows"].shape[0]
+    width = row_count // CHUNKS
+    full, low = jnp.float32, jnp.bfloat16
+    scratch = [(square, full)] * 3 + [((small_rows, channels), full)]
+    scratch += [((row_count, LANES), full)] * 4 + [((key_rows, LANES), full)]
+    scratch += [((cells, LANES), full)] * 3
+    scratch += [((states, LANES), full)] * 2 + [((width, LANES), full), ((states, LANES), full)]
+    scratch += [((key_rows, channels), full), ((row_count, channels), low)]
+    scratch += [((row_count, channels), low), (square, low), ((states, channels), full)]
+    scratch += [((ROWS_AT_ONCE, channels), full)] * 3 + [((ROWS_AT_ONCE, LANES), full)]
+    scratch += [((8, channels), full)] * 2
+    scratch += [((states, channels), full)] * (2 * len(bits))
+    scratch = [pltpu.VMEM(shape, kind) for shape, kind in scratch]
+    scratch += [buffer for lane in lanes for buffer in lane.buffers(line)]
     copies = sum(lane.copies(line) for lane in lanes)
+    scratch += [pltpu.SemaphoreType.DMA((count,)) for count in (copies, copies, 8)]
+    scratch += [pltpu.SemaphoreType.DMA((len(bits) + 1,))] * 2
+    shapes.append((row_count, channels))
     return pl.pallas_call(
-        functools.partial(all_sum_body, len(arrays), line, bits, lanes, order),
-        out_shape=[jax.ShapeDtypeStruct(array.shape, jnp.float32) for array in arrays],
-        in_specs=[pl.BlockSpec(memory_space=pltpu.HBM)] * len(arrays),
-        out_specs=[pl.BlockSpec(memory_space=pltpu.HBM)] * len(arrays),
-        scratch_shapes=scratch
-        + [pltpu.SemaphoreType.DMA((copies,)), pltpu.SemaphoreType.DMA((copies,))],
+        functools.partial(backward_body, row_count, size, line, bits, lanes, order),
+        out_shape=[jax.ShapeDtypeStruct(shape, full) for shape in shapes],
+        in_specs=[pl.BlockSpec(memory_space=pltpu.HBM)] * len(NAMES)
+        + [pl.BlockSpec(memory_space=pltpu.VMEM)] * len(RESIDENT),
+        out_specs=[pl.BlockSpec(memory_space=pltpu.HBM)] * len(shapes),
+        scratch_shapes=scratch,
         compiler_params=pltpu.CompilerParams(
-            collective_id=0, has_side_effects=True, vmem_limit_bytes=62 * 2**20
+            collective_id=0, has_side_effects=True, vmem_limit_bytes=VMEM_LIMIT
         ),
-    )(*arrays)
+    )(*[arrays[name] for name in NAMES], *[resident[name] for name in RESIDENT])
+
+
+VMEM_LIMIT = 64 * 2**20
 
 
 PLAN = [
-    [(False, True), (False, False), (False, True), (False, False)],
-    [(False, False), (True, False), (True, False)],
+    [(False, False), (True, False), (False, False), (False, False)],
+    [(True, False), (True, True), (False, True)],
     [(False, False)],
+    [(False, False)],
+    [(True, True)],
     [(True, False)],
     [(True, False)],
-    [(False, True)],
-    [(False, False)],
 ]
 ORDER = [
-    11, 1, 0, 5, 7, 4, 2, 10, 9, 3, 6, 8, 11, 1, 0, 11, 5, 11, 7, 4, 2, 10, 1, 9, 0, 3, 6, 8, 5,
-    11, 0, 7, 1, 0, 11, 11, 2, 2, 9, 4, 2, 10, 3, 10, 6, 10, 5, 0, 1, 8, 9, 1, 5, 2, 7, 11, 9,
-    1, 6, 5, 4, 10, 7, 9, 3, 8, 0, 5, 2, 6, 11, 7, 9, 1, 10, 4, 5, 0, 6, 2, 7, 10, 3, 9, 4, 6,
-    8, 3, 4, 1, 5, 8, 0, 3, 2, 7, 10, 8, 6, 0, 9, 2, 4, 7, 10, 3, 8, 0, 2, 10, 6, 4, 0, 2, 8, 3,
-    10,
+    0, 4, 5, 1, 3, 7, 6, 2, 12, 0, 12, 4, 12, 5, 1, 12, 3, 7, 12, 0, 6, 2, 12, 12, 12, 12, 4,
+    12, 12, 8, 12, 5, 3, 8, 1, 5, 7, 0, 5, 3, 6, 2, 7, 6, 5, 4, 2, 12, 0, 6, 12, 12, 0, 3, 12,
+    12, 8, 7, 12, 12, 12, 0, 3, 1, 12, 5, 8, 4, 12, 12, 7, 12, 6, 12, 0, 5, 3, 2, 12, 6, 12, 4,
+    12, 5, 7, 12, 1, 12, 12, 2, 12, 8, 3, 12, 0, 4, 6, 12, 12, 12, 12, 7, 12, 5, 12, 12, 1, 3,
+    12, 2, 12, 12, 8, 12, 12, 12, 12, 12, 4, 9, 2, 12, 12, 12, 12, 9, 5, 6, 12, 12, 12, 12, 1,
+    12, 12, 10, 12, 12, 12, 12, 10, 12, 8, 12, 12, 12, 7, 12, 12, 4, 9, 12, 12, 12, 12, 12, 5,
+    12, 12, 9, 12, 12, 2, 12, 10, 12, 6, 12, 12, 11, 8, 1, 9, 11, 10, 6, 10, 1, 6, 9, 8, 10, 9,
+    11, 9, 11, 11, 9, 10, 11, 10, 9, 11, 11, 9, 10, 9, 11,
 ]
 
 
@@ -773,22 +1200,7 @@
     keys_mixed = sum(shift_taps[offset] * delayed(offset) for offset in range(tap_count))
     product = keys_mixed * value_rows
     skip_row = ssm_skip[None]
-    cells = states * CHUNKS
-    sums, last = per_lanes(
-        functools.partial(forward_states, width), [cells, states], [states], product, ssm_rate
-    )
-    entering = carried(last, ssm_rate, row_count, True)
-    mixed_rows, held, kernel = per_lanes(
-        functools.partial(forward_mix, width),
-        [row_count, cells, width],
-        [states, row_count],
-        product,
-        sums,
-        entering,
-        ssm_rate,
-        ssm_coef,
-        skip_row,
-    )
+    mixed_rows, held, kernel = forward_mixing(row_count, product, ssm_rate, ssm_coef, skip_row)
     gated_rows = (queries * mixed_rows).astype(low)
     middle = inputs + project(gated_rows, out_weight)
     standard_two, factor_two = standardize(middle)
@@ -811,103 +1223,73 @@
     grad_gated = project_back(grad_attended, out_weight)
     grad_queries = (grad_gated * mixed_rows).astype(low)
     grad_mixed = grad_gated * queries
-    grad_skip = jnp.sum(grad_mixed * product, axis=0)
-    grad_sums, first = per_lanes(
-        functools.partial(backward_states, width), [cells, states], [states], grad_mixed, ssm_rate
+    misc = 2 * states
+    last_rows = jnp.stack(
+        [
+            jnp.sum(grad_normed_two * standard_two, axis=0),
+            jnp.sum(grad_normed_two, axis=0),
+        ]
     )
-    grad_entering = carried(first, ssm_rate, row_count, False)
-    grad_product, grad_coef, grad_rate = per_lanes(
-        functools.partial(backward_mix, width),
-        [row_count, states, states],
-        [states, states, row_count, cells, width],
-        grad_mixed,
-        product,
-        grad_sums,
-        held,
-        grad_entering,
-        ssm_rate,
-        ssm_coef,
-        skip_row,
-        kernel,
-    )
-    grad_keys_mixed = grad_product * value_rows
-    grad_values = (grad_product * keys_mixed).astype(low)
-    grad_blocks = grad_keys_mixed.reshape(width, CHUNKS, channels)
-    after = passed_along(grad_blocks[:halo, 0], "seq", -1)
-    tail = jnp.concatenate([grad_blocks[:halo, 1:], after[:, None]], axis=1)
-    grad_extended = jnp.concatenate([grad_keys_mixed, tail.reshape(halo * CHUNKS, channels)], 0)
-    grad_keys = sum(
-        shift_taps[offset] * grad_extended[offset * CHUNKS : offset * CHUNKS + row_count]
-        for offset in range(tap_count)
-    ).astype(low)
-    grad_taps = jnp.stack(
-        [jnp.sum(grad_keys_mixed * delayed(offset), axis=0) for offset in range(tap_count)]
-    )
-    grad_query_weight = weight_grad(normed_low, grad_queries)
-    grad_key_weight = weight_grad(normed_low, grad_keys)
-    grad_value_weight = weight_grad(normed_low, grad_values)
-    grad_normed = (
-        project_back(grad_queries, query_weight)
-        + project_back(grad_keys, key_weight)
-        + project_back(grad_values, value_weight)
-    )
-    grad_gain_one = jnp.sum(grad_normed * standard_one, axis=0)
-    grad_bias_one = jnp.sum(grad_normed, axis=0)
-    grad_inputs = grad_middle + norm_back(grad_normed, norm1_gain, standard_one, factor_one)
-    small = jnp.concatenate(
-        [
-            grad_gain_one[None],
-            grad_bias_one[None],
-            grad_taps,
-            grad_coef,
-            grad_rate,
-            grad_skip[None],
-            grad_gain_two[None],
-            grad_bias_two[None],
-        ],
-        axis=0,
-    )
-    small_rows = small.shape[0]
+    lead = misc + tap_count + 3
     unit = 8 * lax.axis_size("seq")
-    small = jnp.pad(small, ((0, -small_rows % unit), (0, 0)))
+    small = jnp.pad(last_rows, ((lead, -(lead + 2) % unit), (0, 0)))
     (
         grad_down,
         grad_up,
+        grad_out_weight,
+        grad_query_weight,
+        grad_value_weight,
+        grad_key_weight,
+        small,
+        grad_inputs,
+    ) = backward(
+        row_count,
+        dict(
+            down=grad_down,
+            up=grad_up,
+            out=grad_out_weight,
+            grad_mixed=grad_mixed,
+            product=product,
+            held=held,
+            values=value_rows,
+            keys_mixed=keys_mixed,
+            key_rows=extended,
+            standard=standard_one,
+            factor=jnp.broadcast_to(factor_one, (row_count, LANES)),
+            grad_middle=grad_middle,
+            query_weight=query_weight,
+            key_weight=key_weight,
+            value_weight=value_weight,
+        ),
+        dict(
+            rate=ssm_rate,
+            coef=ssm_coef,
+            skip=skip_row,
+            taps=shift_taps,
+            kernel=kernel,
+            gain=norm1_gain[None],
+            normed_turned=normed_low.T,
+            grad_queries=grad_queries,
+            small=small,
+        ),
+        PLAN,
+        ORDER,
+    )
+    return (
+        token_order(mixed_out),
+        token_order(grad_inputs),
+        small[lead - 2],
+        small[lead - 1],
         grad_query_weight,
         grad_key_weight,
         grad_value_weight,
+        small[misc : misc + tap_count],
+        small[:states],
+        small[states:misc],
+        small[misc + tap_count],
         grad_out_weight,
-        small,
-    ) = all_sum(
-        [
-            grad_down,
-            grad_up,
-            grad_query_weight,
-            grad_key_weight,
-            grad_value_weight,
-            grad_out_weight,
-            small,
-        ],
-        PLAN,
-        ORDER,
-    )
-    first = 2 + tap_count
-    second = first + 2 * states
-    return (
-        token_order(mixed_out),
-        token_order(grad_inputs),
-        small[0],
-        small[1],
-        grad_query_weight,
-        grad_key_weight,
-        grad_value_weight,
-        small[2:first],
-        small[first : first + states],
-        small[first + states : second],
-        small[second],
-        grad_out_weight,
-        small[second + 1],
-        small[second + 2],
+        small[lead],
+        small[lead + 1],
         grad_up,
         grad_down,
     )

time: 449 us -> 382 us (0.85)
  waiting for transfers between devices: 20.4 us -> 0.01 us
  local copies, waits for them, and re-layouts: 54.7 us -> 39 us
  matrix products: 60.1 us -> 44.6 us
  between operations: 15.3 us -> 1.11 us
    all_gather x2 -> x0, waiting for transfers between devices: 19.6 us -> none  [carried(): every = lax.all_gather(own, 'seq', axis=0)]
    unnamed x130 -> x79, local copies, waits for them, and re-layouts: 41 us -> 21.9 us
    dot_general x6 -> x3, matrix products: 20.1 us -> 13.4 us  [weight_grad(): lax.dot_general(rows_low, grads_low, (((0,), (0,)), ((), ())), preferred_...]
    dot_general x6 -> x3, matrix products: 18.1 us -> 12.2 us  [project_back(): lax.dot_general(grads_low, weight, (((1,), (1,)), ((), ())), preferred_el...]
    reduce_sum x3 -> x0, other arithmetic: 4.62 us -> none  [the longest x2 3.83 us: carried(): jnp.sum(jnp.where(hops[:, None, None] >= 0, every * decays, 0.0), axis=0)]
    pallas_call x5 -> x2, Pallas kernels: 279 us -> 283 us  [the longest x1 249 us: backward(): pl.pallas_call(functools.partial(backward_body, row_count, size, line, bi...]
  transfers between devices with their start and end apart: 4 -> 1, of which waited for: 2 -> 0; matrix products, arithmetic and copies ran while one was open for 9% -> 3% of each run, Pallas kernels for 0% -> 0%
where the time goes in v3:
time: 382 us; the launch traced here: 381 us
  Pallas kernels  283 us (74%)
  matrix products  44.6 us (12%)
  local copies, waits for them, and re-layouts  39 us (10%)
  other arithmetic  10.6 us (3%)
    pallas_call x1, Pallas kernels, backward(): pl.pallas_call(functools.partial(backward_body, row_count, size, line, bi...  249 us
    pallas_call x1, Pallas kernels, forward_mixing(): pl.pallas_call(functools.partial(forward_body, row_count, bits), out_shap...  33.8 us
    unnamed x79, local copies, waits for them, and re-layouts  21.9 us
    dot_general x6, matrix products, project(): return jnp.dot(rows_low, weight, preferred_element_type=jnp.float32)  19 us
    dot_general x3, matrix products, weight_grad(): lax.dot_general(rows_low, grads_low, (((0,), (0,)), ((), ())), preferred_...  13.4 us
    dot_general x3, matrix products, project_back(): lax.dot_general(grads_low, weight, (((1,), (1,)), ((), ())), preferred_el...  12.2 us
  transfers between devices with their start and end apart: 1, of which 0 were waited for; matrix products, arithmetic and copies ran while one was open for 3% of the time, Pallas kernels for 0%

profile of v3, /device:TPU:0, one launch (start us, length us, event | category | flops | bytes accessed | tf_op | source)
XLA Modules:
  0.0 380.6 jit_solution(11982488976451299557)
XLA Ops:
  0.7 1.4 fusion.16
  2.1 1.5 multiply_reduce_fusion.3
  3.6 0.2 convert_bitcast_fusion
  3.9 0.1 rsqrt.20
  4.0 0.9 copy.55
  5.0 1.6 copy.57
  6.6 2.9 add_convert_fusion.2
  9.5 0.8 fusion.29
  10.4 2.5 collective-permute-start
  12.9 0.4 copy.61
  13.4 6.9 %fusion.30 = f32[512,3072]{1,0:T(8,128)} fusion(bf16[512,768]{1,0:T(8,128)(2,1)S(1)} %bitcast.57, bf16[3072,768]{1,0:T(8,128)(2,1)} %param.30), kind=kOutput, calls=%fused_computation.74 | convolution fusion | flops 2415919104 | bytes 11796480 | tf_op jit(solution)/shard_map/dot_general | solution.py:44
  20.3 0.6 broadcast_in_dim.11.refs_20_
  21.0 3.0 copy.62.refs_9_
  24.1 2.9 pad_maximum_fusion.refs_8_
  27.0 2.7 fusion.25
  29.7 33.8 %shard_map.279 = (f32[512,768]{1,0:T(8,128)S(1)}, f32[6,1024,128]{2,1,0:T(8,128)S(1)}, f32[32,768]{1,0:T(8,128)S(1)}) custom-call(f32[512,768]{1,0:T(8,128)S(1)} %get-tuple-element.51.refs_0_.refs_4_, f32[64,768]{1,0:T(8,128)S(1)} %copy-done.2, f32[64,768]{1,0:T(8,128)S(1)} %copy-done.3, f32[1,768]{1,0:T(1,128)S(1)} %broadcast_in_dim.9.refs_3_.refs_17_), custom_call_target="tpu_custom_call" | custom-call | tf_op jit(solution)/shard_map/pallas_call | solution.py:791
  63.5 0.8 multiply_convert_fusion.2
  64.4 0.7 copy-done.1
  65.1 0.5 copy-done.9
  65.7 0.9 fusion.28
  66.6 0.3 multiply_reduce_fusion.2
  66.9 0.3 copy-done.23
  67.3 9.2 %fusion.6 = (bf16[512,3072]{1,0:T(8,128)(2,1)S(1)}, f32[512,3072]{1,0:T(8,128)S(1)}) fusion(f32[512,3072]{1,0:T(8,128)} %fusion.30, bf16[768,3072]{1,0:T(8,128)(2,1)S(1)} %bitcast.73, f32[512,768]{1,0:T(8,128)S(1)} %get-tuple-element.63, f32[768]{0:T(1024)S(1)} %copy-done.25, f32[768]{0:T(1024)S(1)} %copy-done.23, f32[512]{0:T(512)S(1)} %add_rsqrt_fusion.1, ...), kind=kOutput, calls=%fused_computation.8 | convolution fusion | flops 2449342464 | bytes 22030336 | tf_op jit(solution)/shard_map/dot_general | solution.py:40
  76.5 4.7 %add_convert_fusion = bf16[512,768]{1,0:T(8,128)(2,1)} fusion(f32[512,768]{1,0:T(8,128)S(1)} %get-tuple-element.63, bf16[3072,768]{1,0:T(8,128)(2,1)S(1)} %bitcast.71, f32[512,3072]{1,0:T(8,128)S(1)} %get-tuple-element.65), kind=kOutput, calls=%fused_computation.31 | convolution fusion | flops 2430861312 | bytes 13369344 | tf_op jit(solution)/shard_map/dot_general | solution.py:40
  81.2 5.6 %fusion.24.refs_0_ = f32[3072,768]{1,0:T(8,128)} fusion(bf16[512,768]{1,0:T(8,128)(2,1)S(1)} %bitcast.58, f32[512,3072]{1,0:T(8,128)S(1)} %get-tuple-element.65), kind=kOutput, calls=%fused_computation.69 | convolution fusion | flops 2430074880 | bytes 16515072 | tf_op jit(solution)/shard_map/dot_general | solution.py:50
  86.8 3.0 multiply_reduce_fusion
  89.8 5.5 %fusion.22.refs_1_ = f32[768,3072]{1,0:T(8,128)} fusion(bf16[512,3072]{1,0:T(8,128)(2,1)S(1)} %get-tuple-element.64, f32[512,768]{1,0:T(8,128)S(1)} %get-tuple-element.63, f32[768]{0:T(1024)S(1)} %copy-done.25, f32[768]{0:T(1024)S(1)} %copy-done.23, f32[512]{0:T(512)S(1)} %add_rsqrt_fusion.1, f32[512]{0:T(512)S(1)} %broadcast_multiply_fusion.3), kind=kOutput, calls=%fused_computation.67 | convolution fusion | flops 2417885184 | bytes 14166016 | tf_op jit(solution)/shard_map/dot_general | solution.py:50
  95.4 0.6 multiply_add_fusion.refs_11_
  96.0 2.2 fusion.20.refs_2_
  98.2 2.3 multiply_convert_fusion.1
  100.5 0.8 select_maximum_fusion.refs_23_
  101.3 0.8 broadcast_in_dim.10.refs_10_
  102.2 249.0 %shard_map.280 = (f32[3072,768]{1,0:T(8,128)}, f32[768,3072]{1,0:T(8,128)}, f32[768,768]{1,0:T(8,128)}, f32[768,768]{1,0:T(8,128)}, f32[768,768]{1,0:T(8,128)}, ...) custom-call(f32[3072,768]{1,0:T(8,128)} %fusion.24.refs_0_, f32[768,3072]{1,0:T(8,128)} %fusion.22.refs_1_, ...), custom_call_target="tpu_custom_call" | custom-call | tf_op jit(solution)/shard_map/pallas_call | solution.py:1116
  351.2 1.5 slice.62
  352.6 1.5 slice_reduce_fusion
  354.2 1.8 fusion.27
  356.0 2.4 copy.60
  358.4 2.1 copy.63
  360.4 3.4 copy.73
  363.8 1.4 copy.74
  365.2 1.1 copy-done.12
  366.3 1.4 copy.75
  367.7 1.1 copy-done.11
  368.8 1.4 copy.76
  370.3 4.8 %copy.77 = f32[768,3072]{1,0:T(8,128)} copy(f32[768,3072]{1,0:T(8,128)S(1)} %bitcast.52) | data formatting | bytes 18874368
  375.1 1.6 slice-done.1
  376.7 0.2 slice-done.2
  376.9 3.7 copy.78
  (87 shorter events, 0.6 us)
Async XLA Ops:
  0.6 3.0 copy-start.7
  5.0 1.6 copy-start.21
  5.0 1.6 copy-start.22
  6.6 2.9 copy-start.17
  9.5 54.0 %copy-start.8 = (bf16[512,768]{0,1:T(8,128)(2,1)}, bf16[512,768]{0,1:T(8,128)(2,1)S(1)}, u32[]{:S(2)}) copy-start(bf16[512,768]{0,1:T(8,128)(2,1)S(1)} %get-tuple-element.53) | copy-start | bytes 2359300
  9.5 3.4 copy-start.19
  10.3 10.6 %copy-start.14 = (f32[512,768]{1,0:T(8,128)}, f32[512,768]{1,0:T(8,128)S(1)}, u32[]{:S(2)}) copy-start(f32[512,768]{1,0:T(8,128)S(1)} %fusion.29) | copy-start | bytes 4718596
  10.4 13.6 %collective-permute-start = (f32[3,768]{1,0:T(4,128)S(1)}, f32[3,768]{1,0:T(4,128)S(1)}, u32[]{:S(2)}, u32[]{:S(2)}) collective-permute-start(f32[3,768]{1,0:T(4,128)S(1)} %bitcast.68), channel_id=1, source_target_pairs={{0,4},{4,8},{8,12},{12,16},{16,20},{20,24},{24,28},{1,5},{5,9},{9,... | collective-permute-start | bytes 27656 | tf_op jit(solution)/shard_map/ppermute | solution.py:19
  13.4 6.9 %copy-start.20 = (f32[4,768]{1,0:T(4,128)S(1)}, f32[4,768]{1,0:T(4,128)}, u32[]{:S(2)}) copy-start(f32[4,768]{1,0:T(4,128)} %refs_18_.1) | copy-start | bytes 36868
  13.4 7.5 %copy-start.24 = (f32[768]{0:T(1024)S(1)}, f32[768]{0:T(1024)}, u32[]{:S(2)}) copy-start(f32[768]{0:T(1024)} %param.25) | copy-start | bytes 9220
  21.0 8.7 %copy-start.5 = (f32[1,768]{1,0:T(1,128)}, f32[1,768]{1,0:T(1,128)S(1)}, u32[]{:S(2)}) copy-start(f32[1,768]{1,0:T(1,128)S(1)} %broadcast_in_dim.9.refs_3_.refs_17_) | copy-start | bytes 9220
  24.0 2.9 copy-start.15
  24.1 2.9 copy-start.18
  26.9 2.7 copy-start.2
  26.9 2.7 copy-start.3
  26.9 40.0 %slice-start.8 = ((s8[4718592]{0:T(1024)(128)(4,1)}), s8[4194304]{0:T(1024)(128)(4,1)S(1)}, s32[]{:S(2)}) async-start(s8[4718592]{0:T(1024)(128)(4,1)} %bitcast.72), calls=%async_computation.8 | async-start | bytes 8388608
  29.6 34.7 %copy-start = (f32[512,768]{1,0:T(8,128)}, f32[512,768]{1,0:T(8,128)S(1)}, u32[]{:S(2)}) copy-start(f32[512,768]{1,0:T(8,128)S(1)} %get-tuple-element.51.refs_0_.refs_4_) | copy-start | bytes 4718596
  29.6 33.8 %copy-start.10 = (bf16[768,768]{1,0:T(8,128)(2,1)S(1)}, bf16[768,768]{1,0:T(8,128)(2,1)}, u32[]{:S(2)}) copy-start(bf16[768,768]{1,0:T(8,128)(2,1)} %refs_12_.1) | copy-start | bytes 3538948
  63.4 1.7 copy-start.1
  63.5 1.7 copy-start.4
  63.5 2.2 copy-start.9
  63.5 3.4 slice-start.9
  66.5 0.7 copy-start.23
  66.5 0.7 copy-start.25
  66.6 9.9 %slice-start.6 = ((s8[4718592]{0:T(1024)(128)(4,1)}), s8[4194304]{0:T(1024)(128)(4,1)S(1)}, s32[]{:S(2)}) async-start(s8[4718592]{0:T(1024)(128)(4,1)} %bitcast.70), calls=%async_computation.6 | async-start | bytes 8388608
  67.2 9.2 %slice-start.7 = ((s8[4718592]{0:T(1024)(128)(4,1)}), s8[524288]{0:T(1024)(128)(4,1)S(1)}, s32[]{:S(2)}) async-start(s8[4718592]{0:T(1024)(128)(4,1)} %bitcast.70), calls=%async_computation.7 | async-start | bytes 1048576
  96.0 2.2 copy-start.6
  351.2 7.2 %copy-start.16 = (f32[512,768]{1,0:T(8,128)S(1)}, f32[512,768]{1,0:T(8,128)}, u32[]{:S(2)}) copy-start(f32[512,768]{1,0:T(8,128)} %get-tuple-element.30) | copy-start | bytes 4718596
  356.0 7.8 %copy-start.13 = (f32[768,768]{1,0:T(8,128)S(1)}, f32[768,768]{1,0:T(8,128)}, u32[]{:S(2)}) copy-start(f32[768,768]{1,0:T(8,128)} %get-tuple-element.91) | copy-start | bytes 7077892
  358.4 11.9 %slice-start.3 = ((s8[9437184]{0:T(1024)(128)(4,1)}), s8[4194304]{0:T(1024)(128)(4,1)S(1)}, s32[]{:S(2)}) async-start(s8[9437184]{0:T(1024)(128)(4,1)} %bitcast.51), calls=%async_computation.3 | async-start | bytes 8388608
  360.4 9.8 %slice-start.4 = ((s8[9437184]{0:T(1024)(128)(4,1)}), s8[4194304]{0:T(1024)(128)(4,1)S(1)}, s32[]{:S(2)}) async-start(s8[9437184]{0:T(1024)(128)(4,1)} %bitcast.51), calls=%async_computation.4 | async-start | bytes 8388608
  363.8 2.5 copy-start.12
  366.3 2.5 copy-start.11
  366.3 3.9 %slice-start.5 = ((s8[9437184]{0:T(1024)(128)(4,1)}), s8[1048576]{0:T(1024)(128)(4,1)S(1)}, s32[]{:S(2)}) async-start(s8[9437184]{0:T(1024)(128)(4,1)} %bitcast.51), calls=%async_computation.5 | async-start | bytes 2097152
  368.8 6.2 %slice-start = ((s8[9437184]{0:T(1024)(128)(4,1)}), s8[4194304]{0:T(1024)(128)(4,1)S(1)}, s32[]{:S(2)}) async-start(s8[9437184]{0:T(1024)(128)(4,1)} %bitcast.49), calls=%async_computation | async-start | bytes 8388608
  370.2 6.4 %slice-start.1 = ((s8[9437184]{0:T(1024)(128)(4,1)}), s8[4194304]{0:T(1024)(128)(4,1)S(1)}, s32[]{:S(2)}) async-start(s8[9437184]{0:T(1024)(128)(4,1)} %bitcast.49), calls=%async_computation.1 | async-start | bytes 8388608
  370.3 6.6 %slice-start.2 = ((s8[9437184]{0:T(1024)(128)(4,1)}), s8[1048576]{0:T(1024)(128)(4,1)S(1)}, s32[]{:S(2)}) async-start(s8[9437184]{0:T(1024)(128)(4,1)} %bitcast.49), calls=%async_computation.2 | async-start | bytes 2097152

commit v4 on v3

v4 whole, which is shorter than its diff:
```python
import functools
import math
from types import SimpleNamespace
from typing import Any, NamedTuple

import jax
import jax.numpy as jnp
from jax import lax
from jax.experimental import pallas as pl
from jax.experimental.pallas import tpu as pltpu
from jax.sharding import PartitionSpec as P

epsilon = 1e-05
CHUNKS = 16
GROUP = 8
LANES = 128

VMEM_LIMIT = 64 * 2**20
ROWS_AT_ONCE = 64


def standardize(values):
    row_mean = jnp.mean(values, axis=-1, keepdims=True)
    centered = values - row_mean
    spread = jnp.mean(centered * centered, axis=-1, keepdims=True)
    factor = lax.rsqrt(spread + epsilon)
    return centered * factor, factor


def norm_back(grads, gain, standard, factor):
    scaled = grads * gain
    return factor * (
        scaled
        - jnp.mean(scaled, axis=-1, keepdims=True)
        - standard * jnp.mean(scaled * standard, axis=-1, keepdims=True)
    )


def project_back(grads_low, weight):
    return lax.dot_general(
        grads_low, weight, (((1,), (1,)), ((), ())), preferred_element_type=jnp.float32
    )


def weight_grad(rows_low, grads_low):
    return lax.dot_general(
        rows_low, grads_low, (((0,), (0,)), ((), ())), preferred_element_type=jnp.float32
    )


def block(ref, place):
    return ref[place * CHUNKS : (place + 1) * CHUNKS, :]


def chunk_rows(chunk, states):
    return pl.ds(chunk, states, stride=CHUNKS)


def state_sums(width, rows_ref, decay_ref, out_ref, group, places, weight, lead):
    decay = decay_ref[pl.ds(group * GROUP, GROUP), :][:, None, :]
    running = jnp.zeros((GROUP, CHUNKS, LANES), jnp.float32)
    for place in places:
        rows = block(rows_ref, place)
        if weight is not None:
            rows = rows * weight(place)
        running = decay * (running + rows[None]) if lead else decay * running + rows[None]
    return running


def forward_states(width, rows_ref, rate_ref, sums_ref, last_ref, decay_ref):
    states = rate_ref.shape[0]
    decay_ref[...] = jnp.exp(-rate_ref[...])

    def body(group, unused):
        running = state_sums(width, rows_ref, decay_ref, None, group, range(width), None, False)
        sums_ref[pl.ds(group * GROUP * CHUNKS, GROUP * CHUNKS), :] = running.reshape(-1, LANES)
        return unused

    lax.fori_loop(0, states // GROUP, body, 0)
    hop = jnp.exp(-width * rate_ref[...])
    held = jnp.zeros((states, LANES), jnp.float32)
    for chunk in range(CHUNKS):
        held = hop * held + sums_ref[chunk_rows(chunk, states), :]
    last_ref[...] = held


def forward_near(
    width, rows_ref, rate_ref, coef_ref, skip_ref, mixed_ref, kernel_ref, taps_ref
):
    states = rate_ref.shape[0]
    lags = lax.broadcasted_iota(jnp.int32, (8, LANES), 0).astype(jnp.float32)

    def add_states(group, totals):
        members = pl.ds(pl.multiple_of(group * GROUP, GROUP), GROUP)
        rates, coefs = rate_ref[members, :], coef_ref[members, :]
        steps = jnp.exp(-8.0 * rates)
        totals = list(totals)
        for i in range(GROUP):
            term = coefs[i : i + 1] * jnp.exp(-rates[i : i + 1] * lags)
            for place in range(width // 8):
                totals[place] = totals[place] + term
                term = term * steps[i : i + 1]
        return tuple(totals)

    zero = jnp.zeros((8, LANES), jnp.float32)
    totals = lax.fori_loop(0, states // GROUP, add_states, (zero,) * (width // 8))
    kernel_ref[...] = jnp.concatenate(totals, axis=0)
    for lag in range(width):
        taps_ref[lag * CHUNKS : (lag + 1) * CHUNKS, :] = jnp.broadcast_to(
            kernel_ref[lag : lag + 1, :], (CHUNKS, LANES)
        )
    for start in range(0, width, 4):
        sums = [skip_ref[...] * block(rows_ref, start + i) for i in range(4)]
        for place in range(start + 4):
            rows = block(rows_ref, place)
            for i in range(4):
                if start + i >= place:
                    sums[i] = sums[i] + block(taps_ref, start + i - place) * rows
        for i in range(4):
            mixed_ref[(start + i) * CHUNKS : (start + i + 1) * CHUNKS, :] = sums[i]


def forward_far(
    width, sums_ref, entering_ref, rate_ref, coef_ref, mixed_ref, held_ref, decay_ref
):
    states = rate_ref.shape[0]
    decay_ref[...] = jnp.exp(-rate_ref[...])
    hop = jnp.exp(-width * rate_ref[...])
    held = entering_ref[...]
    for chunk in range(CHUNKS):
        held_ref[chunk_rows(chunk, states), :] = held
        held = hop * held + sums_ref[chunk_rows(chunk, states), :]

    def body(group, unused):
        decay = decay_ref[pl.ds(group * GROUP, GROUP), :][:, None, :]
        coef = coef_ref[pl.ds(group * GROUP, GROUP), :][:, None, :]
        term = held_ref[pl.ds(group * GROUP * CHUNKS, GROUP * CHUNKS), :].reshape(
            GROUP, CHUNKS, LANES
        )
        term = term * (coef * decay)
        for place in range(width):
            mixed_ref[place * CHUNKS : (place + 1) * CHUNKS, :] += jnp.sum(term, axis=0)
            if place < width - 1:
                term = term * decay
        return unused

    lax.fori_loop(0, states // GROUP, body, 0)


def backward_states(width, grads_ref, rate_ref, sums_ref, first_ref, decay_ref):
    states = rate_ref.shape[0]
    decay_ref[...] = jnp.exp(-rate_ref[...])

    def body(group, unused):
        running = state_sums(
            width, grads_ref, decay_ref, None, group, range(width - 1, -1, -1), None, True
        )
        sums_ref[pl.ds(group * GROUP * CHUNKS, GROUP * CHUNKS), :] = running.reshape(-1, LANES)
        return unused

    lax.fori_loop(0, states // GROUP, body, 0)
    hop = jnp.exp(-width * rate_ref[...])
    held = jnp.zeros((states, LANES), jnp.float32)
    for chunk in range(CHUNKS - 1, -1, -1):
        held = hop * held + sums_ref[chunk_rows(chunk, states), :]
    first_ref[...] = held


def backward_near(
    width,
    grads_ref,
    rows_ref,
    sums_ref,
    entering_ref,
    rate_ref,
    skip_ref,
    kernel_ref,
    back_ref,
    coef_grad_ref,
    rate_grad_ref,
    decay_ref,
    hop_ref,
    taps_ref,
    after_ref,
    lag_ref,
):
    states = rate_ref.shape[0]
    hop = jnp.exp(-width * rate_ref[...])
    hop_ref[...] = hop
    held = entering_ref[...]
    for chunk in range(CHUNKS - 1, -1, -1):
        after_ref[chunk_rows(chunk, states), :] = held
        held = hop * held + sums_ref[chunk_rows(chunk, states), :]
    for lag in range(width):
        taps_ref[lag * CHUNKS : (lag + 1) * CHUNKS, :] = jnp.broadcast_to(
            kernel_ref[lag : lag + 1, :], (CHUNKS, LANES)
        )
    for start in range(0, width, 4):
        sums = [skip_ref[...] * block(grads_ref, start + i) for i in range(4)]
        for place in range(start, width):
            grads = block(grads_ref, place)
            for i in range(4):
                if place >= start + i:
                    sums[i] = sums[i] + block(taps_ref, place - start - i) * grads
        for i in range(4):
            back_ref[(start + i) * CHUNKS : (start + i + 1) * CHUNKS, :] = sums[i]
    for start in range(0, width, 4):
        sums = [jnp.zeros((CHUNKS, LANES), jnp.float32) for i in range(4)]
        for place in range(start, width):
            grads = block(grads_ref, place)
            for i in range(4):
                if place >= start + i:
                    sums[i] = sums[i] + block(rows_ref, place - start - i) * grads
        for i in range(4):
            lag_ref[start + i : start + i + 1, :] = jnp.sum(sums[i], axis=0, keepdims=True)
    decay_all = decay_ref[...]
    near_coef = jnp.zeros((states, LANES), jnp.float32)
    near_rate = jnp.zeros((states, LANES), jnp.float32)
    for lag in range(width - 1, -1, -1):
        near_coef = near_coef * decay_all + lag_ref[lag : lag + 1, :]
        near_rate = near_rate * decay_all + float(lag) * lag_ref[lag : lag + 1, :]
    coef_grad_ref[...] = near_coef
    rate_grad_ref[...] = near_rate


def backward_far(
    width,
    grads_ref,
    rows_ref,
    sums_ref,
    held_ref,
    coef_ref,
    back_ref,
    coef_grad_ref,
    rate_grad_ref,
    decay_ref,
    hop_ref,
    after_ref,
    groups,
):
    def body(group, unused):
        members = pl.ds(group * GROUP, GROUP)
        cells = pl.ds(group * GROUP * CHUNKS, GROUP * CHUNKS)
        cube = (GROUP, CHUNKS, LANES)
        decay = decay_ref[members, :][:, None, :]
        coef = coef_ref[members, :][:, None, :]
        after = after_ref[cells, :].reshape(cube)
        term = after * coef
        for place in range(width - 1, -1, -1):
            back_ref[place * CHUNKS : (place + 1) * CHUNKS, :] += jnp.sum(term, axis=0)
            if place > 0:
                term = term * decay
        held = held_ref[cells, :].reshape(cube)
        coef_grad_ref[members, :] += jnp.sum(held * sums_ref[cells, :].reshape(cube), axis=1)
        slope = state_sums(
            width,
            rows_ref,
            decay_ref,
            None,
            group,
            range(width),
            lambda place: float(width - 1 - place),
            False,
        )
        total = after * (float(width) * hop_ref[members, :][:, None, :] * held + slope)
        slope = state_sums(
            width,
            grads_ref,
            decay_ref,
            None,
            group,
            range(width - 1, -1, -1),
            lambda place: float(place + 1),
            True,
        )
        total = total + held * slope
        rate_grad_ref[members, :] += jnp.sum(total, axis=1)
        return unused

    lax.fori_loop(groups.start, groups.stop, body, 0)


MESH = pl.DeviceIdType.MESH


def add_rows(out_ref, out_start, a_ref, a_start, b_ref, b_start, rows):
    columns = out_ref.shape[1]
    size = 8
    for option in (16, 24, 32, 48, 64):
        if rows % option == 0 and option * columns <= 64 * 1024:
            size = option

    def body(i, unused):
        at = i * size
        out_ref[pl.ds(pl.multiple_of(out_start + at, 8), size), :] = (
            a_ref[pl.ds(pl.multiple_of(a_start + at, 8), size), :]
            + b_ref[pl.ds(pl.multiple_of(b_start + at, 8), size), :]
        )
        return unused

    lax.fori_loop(0, rows // size, body, 0)


class Lane:
    def __init__(self, rows, columns, bits, line_first, in_place):
        self.rows, self.columns = rows, columns
        self.bits, self.line_first, self.in_place = bits, line_first, in_place

    def buffers(self, line):
        half = self.rows // 2
        unit = half // line if self.line_first else half >> len(self.bits)
        counts = [half]
        size = half // line if self.line_first else half
        for unused in self.bits:
            size //= 2
            counts.append(size)
        counts.append(unit * (line + 1 if self.line_first else max(1, line // 2)))
        return [pltpu.VMEM((count, self.columns), jnp.float32) for count in counts]

    def copies(self, line):
        chain = 4 * line + 3 if self.line_first else line
        return 4 + 2 * len(self.bits) + chain


def lane_steps(
    lane, line, source, target, buffers, stage, load_sem, semaphores, first_sem, pending
):
    send_sems, recv_sems, free_sems = semaphores
    first, chain = buffers[0], buffers[-1]
    landing = buffers[1:-1]
    acc = source if lane.in_place else first
    me = lax.axis_index("seq")
    z = lax.axis_index("batch")
    half = lane.rows // 2
    core = me % 2
    counter = [first_sem]

    def fresh():
        counter[0] += 1
        return counter[0] - 1

    def remote(src, dst, index, device):
        return pltpu.make_async_remote_copy(
            src_ref=src,
            dst_ref=dst,
            send_sem=send_sems.at[index],
            recv_sem=recv_sems.at[index],
            device_id=device,
            device_id_type=MESH,
        )

    def rows_of(ref, start, count):
        if not isinstance(start, int):
            start = pl.multiple_of(start, 8)
        return ref.at[pl.ds(start, count), :]

    def side(bit):
        return (me // bit) % 2

    def partner(bit):
        return (me + bit * (1 - 2 * side(bit)), z)

    def free(index, device):
        pl.semaphore_signal(
            free_sems.at[index], inc=1, device_id=device, device_id_type=MESH
        )

    def wait_free(index):
        pl.semaphore_wait(free_sems.at[index], 1)

    mine, other = core * half, (1 - core) * half
    base_row = mine if lane.in_place else 0
    swap = remote(rows_of(source, other, half), first, fresh(), partner(1))

    def add_swap():
        if lane.in_place:
            swap.wait_recv()
            add_rows(acc, mine, acc, mine, first, 0, half)
        else:
            load = pltpu.make_async_copy(rows_of(source, mine, half), stage, load_sem)
            load.start()
            swap.wait_recv()
            load.wait()
            add_rows(acc, 0, acc, 0, stage, 0, half)

    pending.append(swap.wait_send)
    steps = [[swap.start], [add_swap]]

    def join(function):
        steps[-1].append(function)

    def step(function):
        steps.append([function])

    def neighbours_sum(base, size):
        starts, indices = [base], []
        for place, bit in enumerate(lane.bits):
            size //= 2
            start, index = starts[-1], fresh()
            copy = remote(
                rows_of(acc, base_row + start + (1 - side(bit)) * size, size),
                landing[place],
                index,
                partner(bit),
            )
            own = start + side(bit) * size
            join(copy.start)

            def receive(copy=copy, own=own, size=size, place=place, bit=bit, index=index):
                copy.wait()
                free(index, partner(bit))
                add_rows(acc, base_row + own, acc, base_row + own, landing[place], 0, size)

            step(receive)
            starts.append(own)
            indices.append(index)
        return starts, size, indices

    def neighbours_spread(starts, size, indices):
        for place in range(len(lane.bits) - 1, -1, -1):
            rows = rows_of(acc, base_row + starts[place + 1], size)
            copy = remote(rows, rows, fresh(), partner(lane.bits[place]))
            join(functools.partial(wait_free, indices[place]))
            join(copy.start)
            pending.append(copy.wait_send)
            step(copy.wait_recv)
            size *= 2

    if not lane.line_first:
        starts, size, indices = neighbours_sum(0, half)
        at = starts[-1]
        depth = jnp.minimum(z, line - 1 - z)
        lower = z < line // 2
        inward = (me, jnp.where(lower, z + 1, z - 1))
        outward = (me, jnp.where(lower, z - 1, z + 1))
        across = (me, line - 1 - z)
        middle = line // 2 - 1

        def on(level, function):
            def guarded():
                pl.when(depth == level)(function)

            return guarded

        passed = []
        for level in range(middle):
            rows = rows_of(acc, base_row + at, size)
            passed.append(fresh())
            copy = remote(rows, rows_of(chain, level * size, size), passed[-1], inward)
            join(on(level, copy.start))

            def receive(copy=copy, level=level):
                copy.wait_recv()
                add_rows(acc, base_row + at, acc, base_row + at, chain, level * size, size)

            def release(copy=copy, index=passed[-1]):
                copy.wait_send()
                free(index, inward)

            step(on(level + 1, receive))
            join(on(level, release))
        rows = rows_of(acc, base_row + at, size)
        copy = remote(rows, rows_of(chain, middle * size, size), fresh(), across)
        join(on(middle, copy.start))

        def receive_across(copy=copy):
            copy.wait()
            add_rows(acc, base_row + at, acc, base_row + at, chain, middle * size, size)

        step(on(middle, receive_across))
        for level in range(middle - 1, -1, -1):
            rows = rows_of(acc, base_row + at, size)
            copy = remote(rows, rows, fresh(), outward)
            join(on(level + 1, functools.partial(wait_free, passed[level])))
            join(on(level + 1, copy.start))
            pending.append(on(level + 1, copy.wait_send))
            step(on(level, copy.wait_recv))
        neighbours_spread(starts, size, indices)
    else:
        unit = half // line
        slots = [fresh() for unused in range(line + 1)]
        outs = [[fresh() for unused in range(2)] for unused in range(line)]
        spreads = [fresh() for unused in range(line)]

        def on(place, function):
            def guarded():
                pl.when(z == place)(function)

            return guarded

        def beside(place):
            return (me, place - 1 if place > 0 else place + 1)

        def hop(place, member, step_to):
            slot = line if step_to < 0 and member == place - 1 else member
            return remote(
                rows_of(acc, base_row + member * unit, unit),
                rows_of(chain, slot * unit, unit),
                slots[slot],
                (me, place + step_to),
            )

        def arrived(place, slot, member):
            remote(
                rows_of(acc, base_row + member * unit, unit),
                rows_of(chain, slot * unit, unit),
                slots[slot],
                beside(place),
            ).wait_recv()
            row = base_row + member * unit
            add_rows(acc, row, acc, row, chain, slot * unit, unit)

        for turn in range(line - 1):

            def rightward(place=turn):
                for member in range(line - 1, place, -1):
                    if place > 0:
                        arrived(place, member, member)
                    hop(place, member, 1).start()

            def leftward(place=line - 1 - turn):
                for member in range(place):
                    if place < line - 1:
                        arrived(place, member, member)
                    hop(place, member, -1).start()

            if turn > 0:
                step(on(turn, rightward))
            else:
                join(on(turn, rightward))
            join(on(line - 1 - turn, leftward))

        to_right, to_left = fresh(), fresh()

        def collect(place):
            if place > 0:
                arrived(place, place, place)
            if place < line - 1:
                arrived(place, line, place)
            for member in range(line - 1, place, -1):
                hop(place, member, 1).wait_send()
            if place < line - 1:
                free(to_right, (me, place + 1))
            for member in range(place):
                hop(place, member, -1).wait_send()
            if place > 0:
                free(to_left, (me, place - 1))

        def collect_all():
            for place in range(line):
                on(place, functools.partial(collect, place))()

        step(collect_all)

        base = z * unit
        starts, size, indices = neighbours_sum(base, unit)
        neighbours_spread(starts, size, indices)

        def spread_at(place, distance, receive, send):
            members = {place - distance, place + distance}
            for member in sorted(members):
                if not 0 <= member < line:
                    continue
                if receive and distance > 0:
                    remote(
                        rows_of(acc, base_row + member * unit, unit),
                        rows_of(acc, base_row + member * unit, unit),
                        spreads[member],
                        beside(place),
                    ).wait_recv()
                if not send:
                    continue
                for step_to in (1, -1):
                    going = member <= place if step_to > 0 else member >= place
                    if going and 0 <= place + step_to < line:
                        yield member, step_to

        def pass_on(place, member, step_to):
            return pltpu.make_async_remote_copy(
                src_ref=rows_of(acc, base_row + member * unit, unit),
                dst_ref=rows_of(acc, base_row + member * unit, unit),
                send_sem=send_sems.at[outs[member][0 if step_to > 0 else 1]],
                recv_sem=recv_sems.at[spreads[member]],
                device_id=(me, place + step_to),
                device_id_type=MESH,
            )

        for distance in range(line):

            def forward(place, distance):
                if distance == 0 and place > 0:
                    wait_free(to_right)
                if distance == 0 and place < line - 1:
                    wait_free(to_left)
                for member, step_to in spread_at(place, distance, True, True):
                    pass_on(place, member, step_to).start()

            def forward_all(distance=distance):
                for place in range(line):
                    on(place, functools.partial(forward, place, distance))()

            if distance == 0:
                join(forward_all)
            else:
                step(forward_all)

        def gone(place):
            for distance in range(line):
                for member, step_to in spread_at(place, distance, False, True):
                    pass_on(place, member, step_to).wait_send()

        for place in range(line):
            pending.append(on(place, functools.partial(gone, place)))

    keep_index, give_index = fresh(), fresh()
    done = rows_of(acc, base_row, half)
    keep = pltpu.make_async_copy(done, rows_of(target, mine, half), recv_sems.at[keep_index])
    give = remote(done, rows_of(target, mine, half), give_index, partner(1))
    join(keep.start)
    join(give.start)
    pending.append(keep.wait)
    pending.append(give.wait)
    assert counter[0] - first_sem <= lane.copies(line)
    return steps


def turn_order(lengths, order):
    if [order.count(place) for place in range(len(lengths))] == lengths:
        return order
    last = len(lengths) - 1
    turns = range(max(lengths[:-1], default=0))
    lanes = [place for turn in turns for place in range(last) if turn < lengths[place]]
    return [last] * lengths[last] + lanes


class Loop:
    def __init__(self, count, *parts):
        self.count, self.parts = count, parts

    def steps(self):
        return self.count * len(self.parts)


def call_all(functions):
    for function in functions:
        function()


def run_loop(loop, between):
    parts = len(loop.parts)

    def body(i, unused):
        for place, part in enumerate(loop.parts):
            part(i)
            for turn in range(loop.count):
                functions = between[turn * parts + place]
                if functions:
                    pl.when(i == turn)(functools.partial(call_all, functions))
        return unused

    lax.fori_loop(0, loop.count, body, 0)


class Runner:
    def __init__(self, programs, count, order):
        lengths = [len(program) for program in programs] + [count]
        self.programs = [list(program) for program in programs]
        self.order = turn_order(lengths, order)
        self.work_place = len(programs)
        self.at = 0

    def lanes(self):
        functions = []
        while self.at < len(self.order) and self.order[self.at] != self.work_place:
            functions += self.programs[self.order[self.at]].pop(0)
            self.at += 1
        return functions

    def run(self, work):
        for item in work:
            call_all(self.lanes())
            self.at += 1
            if not isinstance(item, Loop):
                item()
                continue
            between = []
            for unused in range(item.steps() - 1):
                between.append(self.lanes())
                self.at += 1
            run_loop(item, between + [[]])


def steps_in(work):
    return sum(item.steps() if isinstance(item, Loop) else 1 for item in work)


def state_exchange(bits, row_count, rate, totals, arrivals, entering, sends, receives, forward):
    me, z = lax.axis_index("seq"), lax.axis_index("batch")

    def copy(level):
        bit = bits[level]
        return pltpu.make_async_remote_copy(
            src_ref=totals[level],
            dst_ref=arrivals[level],
            send_sem=sends.at[level],
            recv_sem=receives.at[level],
            device_id=(me + bit * (1 - 2 * ((me // bit) % 2)), z),
            device_id_type=MESH,
        )

    def arrive(level):
        bit = bits[level]
        copy(level).wait_recv()
        place = me % bit
        after = (me // bit) % 2 == (1 if forward else 0)
        hops = (row_count * (place if forward else bit - 1 - place)).astype(jnp.float32)
        term = jnp.exp(-rate[...] * hops) * arrivals[level][...]
        term = jnp.where(after, term, 0.0)
        entering[...] = term if level == 0 else entering[...] + term
        if level + 1 < len(bits):
            far = jnp.exp(-float(row_count * bit) * rate[...])
            ours, theirs = totals[level][...], arrivals[level][...]
            totals[level + 1][...] = jnp.where(after, ours + far * theirs, theirs + far * ours)
            copy(level + 1).start()

    return copy, arrive


def lane_columns(tile):
    return pl.ds(pl.multiple_of(tile * LANES, LANES), LANES)


def row_block(i, count):
    return pl.ds(pl.multiple_of(i * count, count), count)


SKIP, GAIN_ONE, BIAS_ONE, GAIN_TWO, BIAS_TWO = range(5)


def vector(ref, place):
    return ref[place : place + 1, :]


class ForwardIn(NamedTuple):
    tokens: Any
    token_grads: Any
    vectors: Any
    query_weight: Any
    key_weight: Any
    value_weight: Any
    out_weight: Any
    taps: Any
    rate: Any
    coef: Any


class ForwardOut(NamedTuple):
    product: Any
    held: Any
    kernel: Any
    values: Any
    keys_mixed: Any
    key_rows: Any
    queries: Any
    mixed: Any
    gated: Any
    middle: Any
    normed_two: Any
    standard_two: Any
    factor_two: Any
    normed_one: Any
    standard_one: Any
    factor_one: Any
    out_grad: Any


def forward_body(row_count, size, bits, *refs):
    width = row_count // CHUNKS
    levels = len(bits)
    taken, outs = len(ForwardIn._fields), len(ForwardOut._fields)
    given = ForwardIn(*refs[:taken])
    results = ForwardOut(*refs[taken : taken + outs])
    own = ForwardOut(*refs[taken + outs : taken + 2 * outs])
    refs = refs[taken + 2 * outs :]
    sums, taps, decay, entering, edge_out, edge_in = refs[:6]
    totals, arrivals = refs[6 : 6 + levels], refs[6 + levels : 6 + 2 * levels]
    sends, receives, keeps = refs[-3:]
    rate, coef, skip = given.rate, given.coef, given.vectors.at[0:1]
    vectors = given.vectors
    channels = rate.shape[1]
    tiles = channels // LANES
    tap_count = given.taps.shape[0]
    halo = tap_count - 1
    low = jnp.bfloat16
    me, z = lax.axis_index("seq"), lax.axis_index("batch")
    barrier = pltpu.get_barrier_semaphore()

    def greet(device):
        pl.semaphore_signal(barrier, inc=1, device_id=device, device_id_type=MESH)

    for bit in bits:
        greet((me + bit * (1 - 2 * ((me // bit) % 2)), z))
    pl.when(me > 0)(lambda: greet((me - 1, z)))
    pl.when(me < size - 1)(lambda: greet((me + 1, z)))

    kept = ForwardOut(
        *[
            pltpu.make_async_copy(own[i], results[i], keeps.at[i])
            for i in range(len(ForwardOut._fields))
        ]
    )

    copy, arrive = state_exchange(
        bits, row_count, rate, totals, arrivals, entering, sends, receives, True
    )

    def edge(device):
        return pltpu.make_async_remote_copy(
            src_ref=edge_out,
            dst_ref=edge_in,
            send_sem=sends.at[levels],
            recv_sem=receives.at[levels],
            device_id=(device, z),
            device_id_type=MESH,
        )

    def reordered(rows, i):
        shape = (128, row_count)
        row = i * 128 + lax.broadcasted_iota(jnp.int32, shape, 0)
        token = lax.rem(row, CHUNKS) * width + lax.div(row, CHUNKS)
        chosen = lax.broadcasted_iota(jnp.int32, shape, 1) == token
        picks = jnp.where(chosen, 1.0, 0.0).astype(low)
        return jnp.dot(picks, rows[...], preferred_element_type=jnp.float32)

    def norm_rows(i):
        rows = row_block(i, 128)
        inputs = reordered(given.tokens, i)
        own.middle[rows, :] = inputs
        standard, factor = standardize(inputs)
        own.standard_one[rows, :] = standard
        own.factor_one[rows, :] = jnp.broadcast_to(factor, (128, LANES))
        own.normed_one[rows, :] = (
            standard * vector(vectors, GAIN_ONE) + vector(vectors, BIAS_ONE)
        ).astype(low)

    def grad_rows(i):
        own.out_grad[row_block(i, 128), :] = reordered(given.token_grads, i).astype(low)

    def project_to(target, weight, lead):
        def body(i):
            cols = row_block(i, 256)
            target[lead : lead + row_count, cols] = jnp.dot(
                own.normed_one[...], weight[:, cols], preferred_element_type=jnp.float32
            )

        return Loop(channels // 256, body)

    lead = halo * CHUNKS

    def send_edge():
        edge_out[...] = jnp.zeros(edge_out.shape, jnp.float32)
        for i in range(halo):
            row = lead + (width - halo + i) * CHUNKS + CHUNKS - 1
            edge_out[i : i + 1, :] = own.key_rows[row : row + 1, :]
        pl.semaphore_wait(
            barrier, levels + jnp.where(me > 0, 1, 0) + jnp.where(me < size - 1, 1, 0)
        )
        pl.when(me < size - 1)(edge(me + 1).start)

        @pl.when(me == 0)
        def at_start():
            edge_in[...] = jnp.zeros(edge_in.shape, jnp.float32)

    def take_edge():
        pl.when(me > 0)(edge(me - 1).wait_recv)

    def states_tile(tile):
        here = lane_columns(tile)
        keys, tap = own.key_rows, given.taps
        for i in range(halo):
            row = lead + (width - halo + i) * CHUNKS
            rows = keys[row : row + CHUNKS, here]
            keys[i * CHUNKS : (i + 1) * CHUNKS, here] = jnp.concatenate(
                [edge_in[i : i + 1, here], rows[: CHUNKS - 1]], axis=0
            )
        total = tap[0:1, here] * keys[lead : lead + row_count, here]
        for offset in range(1, tap_count):
            start = lead - offset * CHUNKS
            total = total + tap[offset : offset + 1, here] * keys[start : start + row_count, here]
        own.keys_mixed[:, here] = total
        own.product[:, here] = total * own.values[:, here]
        forward_states(
            width,
            own.product.at[:, here],
            rate.at[:, here],
            sums.at[tile],
            totals[0].at[:, here],
            decay,
        )

    def near_tile(tile):
        here = lane_columns(tile)
        forward_near(
            width,
            own.product.at[:, here],
            rate.at[:, here],
            coef.at[:, here],
            skip.at[:, here],
            own.mixed.at[:, here],
            own.kernel.at[:, here],
            taps,
        )

    def far_tile(tile):
        here = lane_columns(tile)
        forward_far(
            width,
            sums.at[tile],
            entering.at[:, here],
            rate.at[:, here],
            coef.at[:, here],
            own.mixed.at[:, here],
            own.held.at[tile],
            decay,
        )

    def out_rows(i):
        rows = row_block(i, 128)
        gated = (own.queries[rows, :] * own.mixed[rows, :]).astype(low)
        own.gated[rows, :] = gated
        middle = own.middle[rows, :] + jnp.dot(
            gated, given.out_weight[...], preferred_element_type=jnp.float32
        )
        own.middle[rows, :] = middle
        standard, factor = standardize(middle)
        own.standard_two[rows, :] = standard
        own.factor_two[rows, :] = jnp.broadcast_to(factor, (128, LANES))
        own.normed_two[rows, :] = (
            standard * vector(vectors, GAIN_TWO) + vector(vectors, BIAS_TWO)
        ).astype(low)

    def loop(item, between=()):
        between = list(between)
        run_loop(item, between + [[]] * (item.steps() - len(between)))

    def keep_all(*copies):
        for one in copies:
            one.start()

    loop(Loop(row_count // 128, norm_rows))
    keep_all(kept.standard_one, kept.factor_one, kept.normed_one)
    loop(project_to(own.key_rows, given.key_weight, lead))
    send_edge()
    loop(project_to(own.values, given.value_weight, 0))
    keep_all(kept.values)
    take_edge()
    loop(Loop(tiles, states_tile))
    copy(0).start()
    keep_all(kept.key_rows, kept.keys_mixed, kept.product)
    loop(project_to(own.queries, given.query_weight, 0))
    keep_all(kept.queries)
    loop(Loop(row_count // 128, grad_rows))
    keep_all(kept.out_grad)
    between = [[] for unused in range(tiles)]
    for level in range(levels):
        between[level * tiles // levels].append(functools.partial(arrive, level))
    loop(Loop(tiles, near_tile), between)
    keep_all(kept.kernel)
    loop(Loop(tiles, far_tile))
    keep_all(kept.mixed, kept.held)
    loop(Loop(row_count // 128, out_rows))
    keep_all(kept.gated, kept.middle, kept.normed_two, kept.standard_two, kept.factor_two)
    for level in range(levels):
        copy(level).wait_send()
    pl.when(me < size - 1)(edge(me + 1).wait_send)
    for one in kept:
        one.wait()


def forward(row_count, arrays):
    size = lax.axis_size("seq")
    bits = [1 << place for place in range(size.bit_length() - 1)]
    states, channels = arrays.rate.shape
    tiles, width = channels // LANES, row_count // CHUNKS
    halo = arrays.taps.shape[0] - 1
    full, low = jnp.float32, jnp.bfloat16
    square = ((row_count, channels), full)
    low_square = ((row_count, channels), low)
    thin = ((row_count, LANES), full)
    held = ((tiles, states * CHUNKS, LANES), full)
    outs = ForwardOut(
        product=square,
        held=held,
        kernel=((width, channels), full),
        values=square,
        keys_mixed=square,
        key_rows=((row_count + halo * CHUNKS, channels), full),
        queries=square,
        mixed=square,
        gated=low_square,
        middle=square,
        normed_two=low_square,
        standard_two=square,
        factor_two=thin,
        normed_one=low_square,
        standard_one=square,
        factor_one=thin,
        out_grad=low_square,
    )
    scratch = list(outs) + [held, thin, ((states, LANES), full), ((states, channels), full)]
    scratch += [((8, channels), full)] * 2 + [((states, channels), full)] * (2 * len(bits))
    counts = [len(bits) + 1, len(bits) + 1, len(outs)]
    found = pl.pallas_call(
        functools.partial(forward_body, row_count, size, bits),
        out_shape=[jax.ShapeDtypeStruct(*out) for out in outs],
        in_specs=[pl.BlockSpec(memory_space=pltpu.VMEM)] * len(ForwardIn._fields),
        out_specs=[pl.BlockSpec(memory_space=pltpu.HBM)] * len(outs),
        scratch_shapes=[pltpu.VMEM(*shape) for shape in scratch]
        + [pltpu.SemaphoreType.DMA((count,)) for count in counts],
        compiler_params=pltpu.CompilerParams(
            collective_id=1, has_side_effects=True, vmem_limit_bytes=VMEM_LIMIT
        ),
    )(*[getattr(arrays, name) for name in ForwardIn._fields])
    return ForwardOut(*found)


class BackwardIn(NamedTuple):
    up_weight: Any
    down_weight: Any
    out_weight: Any
    query_weight: Any
    key_weight: Any
    value_weight: Any
    product: Any
    held: Any
    values: Any
    keys_mixed: Any
    key_rows: Any
    queries: Any
    mixed: Any
    gated: Any
    middle: Any
    standard_two: Any
    factor_two: Any
    standard_one: Any
    factor_one: Any
    rate: Any
    coef: Any
    vectors: Any
    taps: Any
    kernel: Any
    out_grad: Any
    normed_one: Any
    normed_two: Any


FAR = 19


class Results(NamedTuple):
    down: Any
    up: Any
    out: Any
    query: Any
    value: Any
    key: Any
    small: Any
    tokens: Any
    mixed_out: Any
    own_down: Any
    own_up: Any
    own_out: Any


HIDDEN_AT_ONCE = 256


def gelu_pair(values):
    slope = math.sqrt(2.0 / math.pi)
    squared = values * values
    bent = jnp.tanh(slope * (values + 0.044715 * (values * squared)))
    half = 0.5 * (1.0 + bent)
    steep = 0.5 * values * (1.0 - bent * bent) * (slope * (1.0 + 3.0 * 0.044715 * squared))
    return values * half, half + steep


def backward_body(row_count, size, line, bits, lanes, order, *refs):
    width = row_count // CHUNKS
    given = BackwardIn(*refs[: len(BackwardIn._fields)])
    rest = list(refs[len(given) :])

    def take(count):
        taken = rest[:count]
        del rest[:count]
        return taken

    results = Results(*take(len(Results._fields)))
    semaphores = rest[-6:-3]
    load_sems, swap_send, swap_recv = rest[-3:]
    del rest[-6:]
    (grad_query, grad_value, grad_key, small) = take(4)
    (shifted, total, grad_middle) = take(3)
    (grad_queries, values_low, keys_low, weight) = take(4)
    (entering, edge_out, edge_in, stage) = take(4)
    levels = len(bits)
    totals, arrivals = take(levels), take(levels)

    me = lax.axis_index("seq")
    z = lax.axis_index("batch")
    channels = small.shape[1]
    tiles = channels // LANES
    rate, coef = given.rate, given.coef
    states = rate.shape[0]
    tap_count = given.taps.shape[0]
    halo = tap_count - 1
    hidden = given.up_weight.shape[1]
    low, full = jnp.bfloat16, jnp.float32
    misc = 2 * states

    barrier = pltpu.get_barrier_semaphore()

    def greet(device):
        pl.semaphore_signal(barrier, inc=1, device_id=device, device_id_type=MESH)

    for bit in bits:
        greet((me + bit * (1 - 2 * ((me // bit) % 2)), z))
    pl.when(z > 0)(lambda: greet((me, z - 1)))
    pl.when(z < line - 1)(lambda: greet((me, z + 1)))
    pl.when(me > 0)(lambda: greet((me - 1, z)))
    pl.when(me < size - 1)(lambda: greet((me + 1, z)))
    pl.semaphore_wait(
        barrier,
        len(bits)
        + jnp.where(z > 0, 1, 0)
        + jnp.where(z < line - 1, 1, 0)
        + jnp.where(me > 0, 1, 0)
        + jnp.where(me < size - 1, 1, 0),
    )

    def local(source, target, place):
        return pltpu.make_async_copy(source, target, load_sems.at[place])

    def fetch(*triples):
        copies = [local(*triple) for triple in triples]
        for copy in copies:
            copy.start()
        for copy in copies:
            copy.wait()

    def add_small(row, value):
        small[row : row + 1, :] += jnp.sum(value, axis=0, keepdims=True)

    exchange, arrive = state_exchange(
        bits, row_count, rate, totals, arrivals, entering, swap_send, swap_recv, False
    )

    def edge(device):
        return pltpu.make_async_remote_copy(
            src_ref=edge_out,
            dst_ref=edge_in,
            send_sem=swap_send.at[levels],
            recv_sem=swap_recv.at[levels],
            device_id=(device, z),
            device_id_type=MESH,
        )

    steps = hidden // HIDDEN_AT_ONCE
    per_block = channels // HIDDEN_AT_ONCE
    held_weight = local(given.out_weight, weight, 7)
    held_standard = local(given.standard_two, shifted.at[:row_count], 8)
    held_gated = local(given.gated, values_low, 9)
    held_middle = local(given.middle, total, 10)
    out_rows = local(keys_low, results.mixed_out, 10)

    def feed_forward(
        up_tile, down_tile, active, grad_low, slope, down_sum, up_sum, block_a, block_b, thin
    ):
        def weights(step):
            here = row_block(step, HIDDEN_AT_ONCE)
            slot = step % 2
            return (
                local(given.up_weight.at[:, here], up_tile.at[slot], slot),
                local(given.down_weight.at[here, :], down_tile.at[slot], 2 + slot),
            )

        def sums(step):
            part = step // per_block
            here = row_block(step % per_block, HIDDEN_AT_ONCE)
            return (
                local(down_sum, results.own_down.at[part, here, :], 4),
                local(up_sum, results.own_up.at[part, :, here], 5),
            )

        def start():
            for copy in weights(0):
                copy.start()
            for copy in (held_middle, held_weight, held_standard, held_gated):
                copy.start()
            small[...] = jnp.zeros(small.shape, full)
            grad_middle[...] = jnp.zeros(grad_middle.shape, full)
            held_middle.wait()

        def part_one(step):
            slot = step % 2
            for copy in weights(step):
                copy.wait()

            @pl.when(step + 1 < steps)
            def following():
                for copy in weights(step + 1):
                    copy.start()

            before = jnp.dot(
                given.normed_two[...], up_tile[slot], preferred_element_type=full
            )
            after, steep = gelu_pair(before)
            active[...] = after.astype(low)
            slope[...] = steep

        def part_two(step):
            slot = step % 2
            total[...] += jnp.dot(active[...], down_tile[slot], preferred_element_type=full)
            grads = project_back(given.out_grad[...], down_tile[slot])
            grad_low[...] = (grads * slope[...]).astype(low)

        def part_three(step):
            @pl.when(step > 0)
            def previous():
                for copy in sums(step - 1):
                    copy.wait()

            down_sum[...] = weight_grad(active[...], given.out_grad[...])
            up_sum[...] = weight_grad(given.normed_two[...], grad_low[...])
            for copy in sums(step):
                copy.start()

        def part_four(step):
            grad_middle[...] += project_back(grad_low[...], up_tile[step % 2])

        def finish():
            for copy in sums(steps - 1):
                copy.wait()
            keys_low[...] = total[...].astype(low)
            out_rows.start()
            held_standard.wait()
            held_weight.wait()
            held_gated.wait()
            out_rows.wait()

        def norm_two(i):
            rows = row_block(i, 128)
            fetch((given.factor_two.at[rows, :], thin, 11))
            grads, standard = grad_middle[rows, :], shifted[rows, :]
            add_small(misc + tap_count + 3, grads * standard)
            add_small(misc + tap_count + 4, grads)
            back = given.out_grad[rows, :].astype(full) + norm_back(
                grads, vector(given.vectors, GAIN_TWO), standard, thin[:, 0:1]
            )
            grad_middle[rows, :] = back
            keys_low[rows, :] = back.astype(low)

        def out_sum(i):
            here = row_block(i, 256)
            down_sum[...] = weight_grad(values_low[:, here], keys_low[...])
            fetch((down_sum, results.own_out.at[0, here, :], 4))

        def gate(i):
            rows = row_block(i, 128)
            fetch(
                (given.mixed.at[rows, :], block_a, 11),
                (given.queries.at[rows, :], block_b, 12),
            )
            grads = project_back(keys_low[rows, :], weight[...])
            grad_queries[rows, :] = (grads * block_a[...]).astype(low)
            total[rows, :] = grads * block_b[...]

        return [
            start,
            Loop(steps, part_one, part_two, part_three, part_four),
            finish,
            Loop(row_count // 128, norm_two),
            Loop(channels // 256, out_sum),
            Loop(row_count // 128, gate),
        ]

    def weight_sum(target, grads):
        def body(i):
            rows = row_block(i, 256)
            target[rows, :] = weight_grad(given.normed_one[:, rows], grads[...])

        return Loop(channels // 256, body)

    back = shifted

    def mixer(
        rows_tile, keys_tile, other, held_tile, back_tile, taps, sums, after, decay, hop, lag
    ):
        def tile_loads(tile):
            here, slot = lane_columns(tile), tile % 2
            return (
                local(given.product.at[:, here], rows_tile.at[slot], 10 + slot),
                local(given.held.at[tile], held_tile.at[slot], 12 + slot),
                local(given.values.at[:, here], other.at[slot, pl.ds(0, row_count)], 14 + slot),
                local(given.keys_mixed.at[:, here], keys_tile.at[slot], 16 + slot),
            )

        def key_loads(tile):
            slot = tile % 2
            return local(given.key_rows.at[:, lane_columns(tile)], other.at[slot], 14 + slot)

        def first_tile(tile):
            here = lane_columns(tile)
            backward_states(
                width,
                total.at[:, here],
                rate.at[:, here],
                sums.at[tile],
                totals[0].at[:, here],
                decay,
            )

        def start_tiles():
            for copy in tile_loads(0):
                copy.start()
            exchange(0).start()

        def near(tile):
            here, slot = lane_columns(tile), tile % 2
            for copy in tile_loads(tile):
                copy.wait()

            @pl.when(tile + 1 < tiles)
            def following():
                for copy in tile_loads(tile + 1):
                    copy.start()

            decay[...] = jnp.exp(-rate[:, here])
            backward_near(
                width,
                total.at[:, here],
                rows_tile.at[slot],
                sums.at[tile],
                entering.at[:, here],
                rate.at[:, here],
                given.vectors.at[0:1, here],
                given.kernel.at[:, here],
                back_tile,
                small.at[0:states, here],
                small.at[states:misc, here],
                decay,
                hop,
                taps,
                after,
                lag,
            )

        def far(half):
            def part(tile):
                here, slot = lane_columns(tile), tile % 2
                groups = states // GROUP // 2
                backward_far(
                    width,
                    total.at[:, here],
                    rows_tile.at[slot],
                    sums.at[tile],
                    held_tile.at[slot],
                    coef.at[:, here],
                    back_tile,
                    small.at[0:states, here],
                    small.at[states:misc, here],
                    decay,
                    hop,
                    after,
                    range(half * groups, (half + 1) * groups),
                )

            return part

        def end(tile):
            here, slot = lane_columns(tile), tile % 2
            row = misc + tap_count
            small[row : row + 1, here] = jnp.sum(
                total[:, here] * rows_tile[slot], axis=0, keepdims=True
            )
            small[states:misc, here] = -coef[:, here] * small[states:misc, here]
            shifted[0:row_count, here] = back_tile[...] * other[slot, 0:row_count, :]
            values_low[:, here] = (back_tile[...] * keys_tile[slot]).astype(low)

        held_ones = local(given.standard_one, total, 7)
        held_factor = local(given.factor_one, back_tile, 8)

        def send_edge():
            key_loads(0).start()
            held_ones.start()
            held_factor.start()
            edge_out[...] = jnp.zeros(edge_out.shape, full)
            for place in range(halo):
                row = place * CHUNKS
                edge_out[place : place + 1, :] = shifted[row : row + 1, :]
            pl.when(me > 0)(edge(me - 1).start)

            @pl.when(me == size - 1)
            def at_end():
                edge_in[...] = jnp.zeros(edge_in.shape, full)

        def take_edge():
            pl.when(me < size - 1)(edge(me + 1).wait_recv)

        def keys_part(tile):
            here, slot = lane_columns(tile), tile % 2
            key_loads(tile).wait()

            @pl.when(tile + 1 < tiles)
            def following():
                key_loads(tile + 1).start()

            for place in range(halo):
                rows = shifted[place * CHUNKS : (place + 1) * CHUNKS, here]
                start = row_count + place * CHUNKS
                shifted[start : start + CHUNKS, here] = jnp.concatenate(
                    [rows[1:], edge_in[place : place + 1, here]], axis=0
                )
            tap = given.taps
            sum_rows = tap[0:1, here] * shifted[0:row_count, here]
            for offset in range(1, tap_count):
                start = offset * CHUNKS
                sum_rows = sum_rows + tap[offset : offset + 1, here] * (
                    shifted[start : start + row_count, here]
                )
            keys_low[:, here] = sum_rows.astype(low)
            grads = shifted[0:row_count, here]
            for offset in range(tap_count):
                start = (halo - offset) * CHUNKS
                small[misc + offset : misc + offset + 1, here] = jnp.sum(
                    grads * other[slot, start : start + row_count, :], axis=0, keepdims=True
                )

        def back_sum(index, grads):
            def body(i):
                rows = row_block(i, 128)
                term = project_back(grads[rows, :], weight[...])
                back[rows, :] = term if index == 0 else back[rows, :] + term

            return Loop(row_count // 128, body)

        def before_norm():
            held_ones.wait()
            held_factor.wait()

        def norm_one(i):
            rows = row_block(i, ROWS_AT_ONCE)
            grads, standard = back[rows, :], total[rows, :]
            add_small(misc + tap_count + 1, grads * standard)
            add_small(misc + tap_count + 2, grads)
            grad_middle[rows, :] += norm_back(
                grads, vector(given.vectors, GAIN_ONE), standard, back_tile[rows, 0:1]
            )

        tokens_out = local(grad_middle, results.tokens, 9)
        work = [Loop(tiles, first_tile), start_tiles]
        work.append(weight_sum(grad_query, grad_queries))
        for level in range(levels):
            work.append(functools.partial(arrive, level))
        work.append(Loop(tiles, near, far(0), far(1), end))
        work.append(send_edge)
        work.append(weight_sum(grad_value, values_low))
        work.append(take_edge)
        work.append(Loop(tiles, keys_part))
        work.append(weight_sum(grad_key, keys_low))
        chain = (
            (given.query_weight, grad_queries),
            (given.key_weight, keys_low),
            (given.value_weight, values_low),
        )
        for index, (source, grads) in enumerate(chain):
            work.append(functools.partial(fetch, (source, weight, 0)))
            work.append(back_sum(index, grads))
        work.append(before_norm)
        work.append(Loop(row_count // ROWS_AT_ONCE, norm_one))
        work.append(tokens_out.start)
        work.append(tokens_out.wait)
        return work

    def block_of(lane):
        cols = pl.ds(lane.column, lane.columns)
        if lane.array == 0:
            target = results.down.at[pl.ds(lane.part * channels, channels), cols]
            return results.own_down.at[lane.part, :, cols], target
        if lane.array == 1:
            target = results.up.at[:, pl.ds(lane.part * channels + lane.column, lane.columns)]
            return results.own_up.at[lane.part, :, cols], target
        if lane.array == 2:
            return results.own_out.at[0, :, cols], results.out.at[:, cols]
        source = (grad_query, grad_value, grad_key, small)[lane.array - 3]
        return source.at[:, cols], results[lane.array].at[:, cols]

    pending = [exchange(level).wait_send for level in range(levels)]
    pending.append(lambda: pl.when(me > 0)(edge(me - 1).wait_send))
    programs = []
    start = 0
    for lane in lanes:
        source, target = block_of(lane)
        programs.append(
            lane_steps(
                lane,
                line,
                source,
                target,
                take(len(lane.buffers(line))),
                stage,
                load_sems.at[6],
                semaphores,
                start,
                pending,
            )
        )
        start += lane.copies(line)

    def vmem(*shape, kind=full):
        return pltpu.VMEM(shape, kind)

    count = work_steps(row_count, channels, hidden, levels)
    runner = Runner(programs, count, order)
    done = [0]

    def run(make):
        def scoped(*refs):
            work = make(*refs)
            done[0] += steps_in(work)
            runner.run(work)

        return scoped

    pl.run_scoped(
        run(feed_forward),
        vmem(2, channels, HIDDEN_AT_ONCE, kind=low),
        vmem(2, HIDDEN_AT_ONCE, channels, kind=low),
        vmem(row_count, HIDDEN_AT_ONCE, kind=low),
        vmem(row_count, HIDDEN_AT_ONCE, kind=low),
        vmem(row_count, HIDDEN_AT_ONCE),
        vmem(HIDDEN_AT_ONCE, channels),
        vmem(channels, HIDDEN_AT_ONCE),
        vmem(128, channels),
        vmem(128, channels),
        vmem(128, LANES),
    )
    cells = states * CHUNKS
    pl.run_scoped(
        run(mixer),
        vmem(2, row_count, LANES),
        vmem(2, row_count, LANES),
        vmem(2, row_count + halo * CHUNKS, LANES),
        vmem(2, cells, LANES),
        vmem(row_count, LANES),
        vmem(row_count, LANES),
        vmem(tiles, cells, LANES),
        vmem(cells, LANES),
        vmem(states, LANES),
        vmem(states, LANES),
        vmem(width, LANES),
    )
    assert done[0] == count
    call_all(runner.lanes())
    call_all(pending)


def work_steps(row_count, channels, hidden, levels):
    tiles, weights = channels // LANES, channels // 256
    first = 2 + 4 * (hidden // HIDDEN_AT_ONCE) + 2 * (row_count // 128) + weights
    second = 6 * tiles + 3 * weights + levels + 6 + 3 * (row_count // 128)
    return first + second + row_count // ROWS_AT_ONCE + 3


def backward(row_count, arrays, plan, order):
    size, line = lax.axis_size("seq"), lax.axis_size("batch")
    bits = [1 << place for place in range(size.bit_length() - 1)]
    channels, hidden = arrays.up_weight.shape
    states = arrays.rate.shape[0]
    tap_count = arrays.taps.shape[0]
    misc_rows = 2 * states + tap_count + 5
    small_rows = misc_rows + -misc_rows % (8 * size)
    full, low = jnp.float32, jnp.bfloat16
    parts = hidden // channels
    lanes = []
    for index, pieces in enumerate(plan):
        columns = channels if index == 6 else channels // 2
        for piece, (flipped, line_first) in enumerate(pieces):
            rows = small_rows if index == 6 else channels
            if rows % (8 * size * line):
                line_first = False
            path = bits[:0:-1] if flipped else bits[1:]
            lane = Lane(rows, columns, path, line_first, index > 2)
            lane.array, lane.part, lane.column = index, piece // 2, piece % 2 * columns
            lanes.append(lane)
    square = ((channels, channels), full)
    wide = ((row_count, channels), full)
    low_wide = ((row_count, channels), low)
    small = ((small_rows, channels), full)
    key_rows = arrays.key_rows.shape[0]
    one = ((states, channels), full)
    scratch = [square] * 3 + [small, ((key_rows, channels), full), wide, wide]
    scratch += [low_wide] * 3 + [((channels, channels), low)]
    scratch += [one] + [((8, channels), full)] * 2 + [((channels // 2, channels // 2), full)]
    scratch += [one] * (2 * len(bits))
    scratch = [pltpu.VMEM(*shape) for shape in scratch]
    scratch += [buffer for lane in lanes for buffer in lane.buffers(line)]
    copies = sum(lane.copies(line) for lane in lanes)
    counts = [20, len(bits) + 1, len(bits) + 1]
    outs = [((hidden, channels), full), ((channels, hidden), full)] + [square] * 4
    outs += [small, wide, low_wide]
    outs += [((parts, channels, channels), full)] * 2 + [((1, channels, channels), full)]
    found = pl.pallas_call(
        functools.partial(backward_body, row_count, size, line, bits, lanes, order),
        out_shape=[jax.ShapeDtypeStruct(*out) for out in outs],
        in_specs=[pl.BlockSpec(memory_space=pltpu.HBM)] * FAR
        + [pl.BlockSpec(memory_space=pltpu.VMEM)] * (len(BackwardIn._fields) - FAR),
        out_specs=[pl.BlockSpec(memory_space=pltpu.HBM)] * len(outs),
        scratch_shapes=scratch
        + [pltpu.SemaphoreType.DMA((copies,)), pltpu.SemaphoreType.DMA((copies,))]
        + [pltpu.SemaphoreType.REGULAR((copies,))]
        + [pltpu.SemaphoreType.DMA((count,)) for count in counts],
        compiler_params=pltpu.CompilerParams(
            collective_id=0, has_side_effects=True, vmem_limit_bytes=VMEM_LIMIT
        ),
    )(*[getattr(arrays, name) for name in BackwardIn._fields])
    return Results(*found)


PLAN = [
    [(True, False), (False, False), (False, True), (True, True), (True, False), (True, False), (False, True), (False, False)],
    [(False, False), (True, True), (False, False), (True, False), (False, False), (False, True), (False, False), (True, True)],
    [(True, False), (True, False)],
    [(True, False), (False, False)],
    [(True, False), (True, False)],
    [(False, True), (False, False)],
    [(False, False)],
]
ORDER = [
    25, 25, 25, 25, 25, 25, 25, 25, 25, 25, 25, 25, 8, 25, 25, 25, 25, 0, 9, 1, 8, 25, 25, 25,
    0, 25, 9, 25, 1, 25, 25, 25, 10, 25, 25, 8, 25, 10, 25, 11, 3, 2, 25, 0, 25, 9, 25, 11, 25,
    3, 8, 25, 1, 2, 25, 9, 25, 25, 12, 25, 25, 25, 25, 12, 4, 5, 13, 25, 11, 9, 3, 10, 25, 4,
    25, 1, 5, 0, 25, 13, 9, 25, 3, 25, 25, 25, 8, 14, 25, 10, 25, 6, 12, 3, 15, 7, 14, 25, 6,
    11, 15, 9, 2, 4, 7, 8, 25, 25, 2, 25, 1, 5, 8, 14, 9, 25, 25, 0, 12, 2, 4, 25, 3, 16, 1, 17,
    25, 25, 0, 16, 13, 1, 17, 7, 8, 25, 14, 25, 0, 9, 5, 13, 25, 3, 2, 10, 25, 25, 16, 13, 6,
    25, 1, 8, 10, 25, 0, 3, 25, 6, 11, 17, 10, 25, 25, 16, 25, 25, 18, 13, 19, 25, 7, 2, 6, 18,
    11, 19, 15, 1, 11, 15, 0, 17, 3, 12, 15, 10, 4, 25, 13, 2, 6, 14, 12, 9, 4, 18, 19, 12, 15,
    5, 14, 11, 16, 25, 9, 25, 6, 4, 13, 7, 25, 5, 10, 14, 25, 17, 19, 2, 25, 16, 25, 12, 9, 3,
    25, 18, 15, 7, 25, 5, 19, 25, 25, 6, 4, 11, 13, 17, 25, 2, 25, 18, 16, 25, 14, 25, 3, 25,
    12, 15, 25, 7, 19, 25, 25, 4, 15, 5, 25, 6, 13, 25, 7, 25, 16, 17, 25, 18, 25, 2, 25, 25, 5,
    25, 25, 14, 25, 3, 25, 21, 20, 19, 21, 20, 16, 7, 25, 25, 15, 25, 25, 25, 25, 6, 17, 19, 25,
    25, 25, 25, 23, 22, 25, 13, 25, 25, 23, 25, 22, 21, 18, 25, 25, 19, 25, 25, 25, 2, 25, 25,
    25, 25, 25, 20, 15, 25, 25, 25, 22, 25, 23, 25, 25, 6, 25, 25, 25, 21, 25, 22, 24, 25, 25,
    13, 17, 24, 18, 21, 23, 15, 20, 6, 21, 23, 24, 18, 22, 20, 24, 23, 22, 21, 24, 22, 20, 23,
    22, 24, 21, 22, 20, 23, 24, 20, 22, 21, 22, 24, 23, 22, 24, 20,
]


def on_device(
    tokens,
    norm1_gain,
    norm1_bias,
    query_weight,
    key_weight,
    value_weight,
    shift_taps,
    ssm_coef,
    ssm_rate,
    ssm_skip,
    out_weight,
    norm2_gain,
    norm2_bias,
    up_weight,
    down_weight,
    out_grad,
):
    unused, row_count, channels = tokens.shape
    width = row_count // CHUNKS
    states = ssm_rate.shape[0]
    tap_count = shift_taps.shape[0]

    def token_order(values):
        return values.reshape(width, CHUNKS, channels).swapaxes(0, 1).reshape(1, row_count, channels)

    vectors = jnp.stack([ssm_skip, norm1_gain, norm1_bias, norm2_gain, norm2_bias])
    arrays = SimpleNamespace(
        tokens=tokens[0],
        token_grads=out_grad[0],
        vectors=jnp.concatenate([vectors, jnp.zeros_like(vectors[:3])], axis=0),
        query_weight=query_weight,
        key_weight=key_weight,
        value_weight=value_weight,
        out_weight=out_weight,
        up_weight=up_weight,
        down_weight=down_weight,
        taps=shift_taps,
        rate=ssm_rate,
        coef=ssm_coef,
    )
    vars(arrays).update(forward(row_count, arrays)._asdict())
    found = backward(row_count, arrays, PLAN, ORDER)
    small = found.small
    misc = 2 * states
    first = misc + tap_count
    return (
        token_order(found.mixed_out),
        token_order(found.tokens),
        small[first + 1],
        small[first + 2],
        found.query,
        found.key,
        found.value,
        small[misc:first],
        small[:states],
        small[states:misc],
        small[first],
        found.out,
        small[first + 3],
        small[first + 4],
        found.up,
        found.down,
    )


def solution(mesh):
    placed = (P("batch", "seq", None),) + (P(),) * 14 + (P("batch", "seq", None),)
    return jax.shard_map(
        on_device,
        mesh=mesh,
        in_specs=placed,
        out_specs=(P("batch", "seq", None),) * 2 + (P(),) * 14,
        check_vma=False,
    )
```

time: 382 us -> 326 us (0.85)
  matrix products: 44.6 us -> 0 us
  other arithmetic: 10.6 us -> 0.01 us
  Pallas kernels: 283 us -> 290 us
  local copies, waits for them, and re-layouts: 39 us -> 33.5 us
    dot_general x12 -> x0, matrix products: 44.6 us -> none  [the longest x6 19 us: project(): return jnp.dot(rows_low, weight, preferred_element_type=jnp.float32)]
    pallas_call x1, Pallas kernels: 33.8 us -> 46.4 us  [forward(): pl.pallas_call(functools.partial(forward_body, row_count, size, bits), ou...]
    pallas_call x1, Pallas kernels: 249 us -> 244 us  [backward(): pl.pallas_call(functools.partial(backward_body, row_count, size, line, bi...]
    unnamed x79 -> x26, local copies, waits for them, and re-layouts: 21.9 us -> 20.2 us
  transfers between devices with their start and end apart: 1 -> 0, of which waited for: 0 -> 0; matrix products, arithmetic and copies ran while one was open for 3% -> 0% of each run, Pallas kernels for 0% -> 0%
where the time goes in v4:
time: 326 us; the launch traced here: 325 us
  Pallas kernels  290 us (89%)
  local copies, waits for them, and re-layouts  33.5 us (10%)
    pallas_call x1, Pallas kernels, backward(): pl.pallas_call(functools.partial(backward_body, row_count, size, line, bi...  244 us
    pallas_call x1, Pallas kernels, forward(): pl.pallas_call(functools.partial(forward_body, row_count, size, bits), ou...  46.4 us
    unnamed x26, local copies, waits for them, and re-layouts  20.2 us

profile of v4, /device:TPU:0, one launch (start us, length us, event | category | flops | bytes accessed | tf_op | source)
XLA Modules:
  0.0 324.6 jit_solution(10719773018156428971)
XLA Ops:
  0.6 0.7 stack.16
  1.3 0.7 stack.17
  2.0 0.7 stack.15
  2.7 0.7 stack.18
  3.4 0.7 stack.19
  4.1 0.6 concatenate.3.refs_2_.refs_21_
  4.7 46.4 %shard_map.279 = (f32[512,768]{1,0:T(8,128)}, f32[6,1024,128]{2,1,0:T(8,128)}, f32[32,768]{1,0:T(8,128)}, f32[512,768]{1,0:T(8,128)}, f32[512,768]{1,0:T(8,128)}...) custom-call(bf16[512,768]{1,0:T(8,128)(2,1)} %bitcast.18, ...), custom_call_target="tpu_custom_call" | custom-call | tf_op jit(solution)/shard_map/pallas_call | solution.py:1013
  51.1 244.0 %shard_map.280 = (f32[3072,768]{1,0:T(8,128)}, f32[768,3072]{1,0:T(8,128)}, f32[768,768]{1,0:T(8,128)}, f32[768,768]{1,0:T(8,128)}, f32[768,768]{1,0:T(8,128)}, ...) custom-call(bf16[768,3072]{1,0:T(8,128)(2,1)} %refs_0_.1, ...), custom_call_target="tpu_custom_call" | custom-call | tf_op jit(solution)/shard_map/pallas_call | solution.py:1612
  295.1 0.0 copy-start.3
  295.1 2.4 copy.32
  297.5 0.0 copy-done.3
  297.5 0.0 slice-start.3
  297.5 2.1 copy.33
  299.6 1.3 slice.26
  300.9 1.6 slice_reduce_fusion
  302.5 0.0 copy-start.2
  302.5 1.9 fusion
  304.4 0.0 slice-start.4
  304.4 3.4 %copy.40 = f32[768,768]{1,0:T(8,128)} copy(f32[768,768]{1,0:T(8,128)} %get-tuple-element.95) | data formatting | bytes 4718592
  307.8 0.0 copy-done.2
  307.8 0.0 copy-start.1
  307.8 1.4 copy.41
  309.2 1.1 copy-done.1
  310.3 0.0 copy-start
  310.3 0.0 slice-start.5
  310.3 1.4 copy.42
  311.7 1.1 copy-done
  312.8 0.0 slice-start
  312.8 1.4 copy.43
  314.3 0.0 slice-done.3
  314.3 0.0 slice-done.4
  314.3 0.0 slice-done.5
  314.3 0.0 slice-start.1
  314.3 0.0 slice-start.2
  314.3 4.8 %copy.44 = f32[768,3072]{1,0:T(8,128)} copy(f32[768,3072]{1,0:T(8,128)S(1)} %bitcast.13) | data formatting | bytes 18874368
  319.1 0.0 slice-done
  319.1 1.6 slice-done.1
  320.7 0.2 slice-done.2
  320.9 3.7 %copy.45 = f32[3072,768]{1,0:T(8,128)} copy(f32[3072,768]{1,0:T(8,128)S(1)} %bitcast.11) | data formatting | bytes 18874368
  (3 shorter events, 0.0 us)
Async XLA Ops:
  295.1 2.4 copy-start.3
  297.5 16.7 %slice-start.3 = ((s8[9437184]{0:T(1024)(128)(4,1)}), s8[4194304]{0:T(1024)(128)(4,1)S(1)}, s32[]{:S(2)}) async-start(s8[9437184]{0:T(1024)(128)(4,1)} %bitcast.12), calls=%async_computation.3 | async-start | bytes 8388608
  302.5 5.3 %copy-start.2 = (f32[768,768]{1,0:T(8,128)S(1)}, f32[768,768]{1,0:T(8,128)}, u32[]{:S(2)}) copy-start(f32[768,768]{1,0:T(8,128)} %get-tuple-element.96) | copy-start | bytes 7077892
  304.4 9.8 %slice-start.4 = ((s8[9437184]{0:T(1024)(128)(4,1)}), s8[4194304]{0:T(1024)(128)(4,1)S(1)}, s32[]{:S(2)}) async-start(s8[9437184]{0:T(1024)(128)(4,1)} %bitcast.12), calls=%async_computation.4 | async-start | bytes 8388608
  307.8 2.5 copy-start.1
  310.3 2.5 copy-start
  310.3 3.9 %slice-start.5 = ((s8[9437184]{0:T(1024)(128)(4,1)}), s8[1048576]{0:T(1024)(128)(4,1)S(1)}, s32[]{:S(2)}) async-start(s8[9437184]{0:T(1024)(128)(4,1)} %bitcast.12), calls=%async_computation.5 | async-start | bytes 2097152
  312.8 6.2 %slice-start = ((s8[9437184]{0:T(1024)(128)(4,1)}), s8[4194304]{0:T(1024)(128)(4,1)S(1)}, s32[]{:S(2)}) async-start(s8[9437184]{0:T(1024)(128)(4,1)} %bitcast.10), calls=%async_computation | async-start | bytes 8388608
  314.3 6.4 %slice-start.1 = ((s8[9437184]{0:T(1024)(128)(4,1)}), s8[4194304]{0:T(1024)(128)(4,1)S(1)}, s32[]{:S(2)}) async-start(s8[9437184]{0:T(1024)(128)(4,1)} %bitcast.10), calls=%async_computation.1 | async-start | bytes 8388608
  314.3 6.6 %slice-start.2 = ((s8[9437184]{0:T(1024)(128)(4,1)}), s8[1048576]{0:T(1024)(128)(4,1)S(1)}, s32[]{:S(2)}) async-start(s8[9437184]{0:T(1024)(128)(4,1)} %bitcast.10), calls=%async_computation.2 | async-start | bytes 2097152

commit v5 on v4

--- a/solution.py
+++ b/solution.py
@@ -323,7 +323,7 @@
 
 
 def lane_steps(
-    lane, line, source, target, buffers, stage, load_sem, semaphores, first_sem, pending
+    lane, line, source, target, buffers, stages, semaphores, first_sem, pending
 ):
     send_sems, recv_sems, free_sems = semaphores
     first, chain = buffers[0], buffers[-1]
@@ -372,19 +372,28 @@
     base_row = mine if lane.in_place else 0
     swap = remote(rows_of(source, other, half), first, fresh(), partner(1))
 
+    def load():
+        place = len(stages) - 1 if lane.stage is None else lane.stage
+        return pltpu.make_async_copy(rows_of(source, mine, half), *stages[place])
+
+    def begin():
+        swap.start()
+        if not lane.in_place and lane.stage is not None:
+            load().start()
+
     def add_swap():
         if lane.in_place:
             swap.wait_recv()
             add_rows(acc, mine, acc, mine, first, 0, half)
         else:
-            load = pltpu.make_async_copy(rows_of(source, mine, half), stage, load_sem)
-            load.start()
+            if lane.stage is None:
+                load().start()
             swap.wait_recv()
-            load.wait()
-            add_rows(acc, 0, acc, 0, stage, 0, half)
+            load().wait()
+            add_rows(acc, 0, acc, 0, stages[-1 if lane.stage is None else lane.stage][0], 0, half)
 
     pending.append(swap.wait_send)
-    steps = [[swap.start], [add_swap]]
+    steps = [[begin], [add_swap]]
 
     def join(function):
         steps[-1].append(function)
@@ -661,11 +670,25 @@
     lax.fori_loop(0, loop.count, body, 0)
 
 
+def give_stages(lanes, order, count):
+    free, seen = list(range(count)), [0] * len(lanes)
+    for place in order:
+        if place == len(lanes) or lanes[place].in_place:
+            continue
+        seen[place] += 1
+        lane = lanes[place]
+        if seen[place] == 1:
+            lane.stage = free.pop() if free else None
+        elif seen[place] == 2 and lane.stage is not None:
+            free.append(lane.stage)
+
+
 class Runner:
-    def __init__(self, programs, count, order):
+    def __init__(self, lanes, programs, count, order):
         lengths = [len(program) for program in programs] + [count]
         self.programs = [list(program) for program in programs]
         self.order = turn_order(lengths, order)
+        give_stages(lanes, self.order, STAGES)
         self.work_place = len(programs)
         self.at = 0
 
@@ -744,7 +767,11 @@
 class ForwardIn(NamedTuple):
     tokens: Any
     token_grads: Any
-    vectors: Any
+    skip: Any
+    gain_one: Any
+    bias_one: Any
+    gain_two: Any
+    bias_two: Any
     query_weight: Any
     key_weight: Any
     value_weight: Any
@@ -772,6 +799,7 @@
     standard_one: Any
     factor_one: Any
     out_grad: Any
+    vectors: Any
 
 
 def forward_body(row_count, size, bits, *refs):
@@ -785,8 +813,8 @@
     sums, taps, decay, entering, edge_out, edge_in = refs[:6]
     totals, arrivals = refs[6 : 6 + levels], refs[6 + levels : 6 + 2 * levels]
     sends, receives, keeps = refs[-3:]
-    rate, coef, skip = given.rate, given.coef, given.vectors.at[0:1]
-    vectors = given.vectors
+    vectors = own.vectors
+    rate, coef, skip = given.rate, given.coef, vectors.at[0:1]
     channels = rate.shape[1]
     tiles = channels // LANES
     tap_count = given.taps.shape[0]
@@ -947,6 +975,11 @@
         for one in copies:
             one.start()
 
+    vectors[...] = jnp.zeros(vectors.shape, jnp.float32)
+    singles = (given.skip, given.gain_one, given.bias_one, given.gain_two, given.bias_two)
+    for place, single in enumerate(singles):
+        vectors[place : place + 1, :] = single[...][None]
+    keep_all(kept.vectors)
     loop(Loop(row_count // 128, norm_rows))
     keep_all(kept.standard_one, kept.factor_one, kept.normed_one)
     loop(project_to(own.key_rows, given.key_weight, lead))
@@ -1006,6 +1039,7 @@
         standard_one=square,
         factor_one=thin,
         out_grad=low_square,
+        vectors=((8, channels), full),
     )
     scratch = list(outs) + [held, thin, ((states, LANES), full), ((states, channels), full)]
     scratch += [((8, channels), full)] * 2 + [((states, channels), full)] * (2 * len(bits))
@@ -1073,6 +1107,7 @@
 
 
 HIDDEN_AT_ONCE = 256
+STAGES = 3
 
 
 def gelu_pair(values):
@@ -1101,7 +1136,8 @@
     (grad_query, grad_value, grad_key, small) = take(4)
     (shifted, total, grad_middle) = take(3)
     (grad_queries, values_low, keys_low, weight) = take(4)
-    (entering, edge_out, edge_in, stage) = take(4)
+    (entering, edge_out, edge_in) = take(3)
+    stages = [(ref, load_sems.at[20 + i]) for i, ref in enumerate(take(STAGES + 1))]
     levels = len(bits)
     totals, arrivals = take(levels), take(levels)
 
@@ -1507,8 +1543,7 @@
                 source,
                 target,
                 take(len(lane.buffers(line))),
-                stage,
-                load_sems.at[6],
+                stages,
                 semaphores,
                 start,
                 pending,
@@ -1520,7 +1555,7 @@
         return pltpu.VMEM(shape, kind)
 
     count = work_steps(row_count, channels, hidden, levels)
-    runner = Runner(programs, count, order)
+    runner = Runner(lanes, programs, count, order)
     done = [0]
 
     def run(make):
@@ -1600,12 +1635,12 @@
     one = ((states, channels), full)
     scratch = [square] * 3 + [small, ((key_rows, channels), full), wide, wide]
     scratch += [low_wide] * 3 + [((channels, channels), low)]
-    scratch += [one] + [((8, channels), full)] * 2 + [((channels // 2, channels // 2), full)]
+    scratch += [one] + [((8, channels), full)] * 2 + [((channels // 2, channels // 2), full)] * (STAGES + 1)
     scratch += [one] * (2 * len(bits))
     scratch = [pltpu.VMEM(*shape) for shape in scratch]
     scratch += [buffer for lane in lanes for buffer in lane.buffers(line)]
     copies = sum(lane.copies(line) for lane in lanes)
-    counts = [20, len(bits) + 1, len(bits) + 1]
+    counts = [21 + STAGES, len(bits) + 1, len(bits) + 1]
     outs = [((hidden, channels), full), ((channels, hidden), full)] + [square] * 4
     outs += [small, wide, low_wide]
     outs += [((parts, channels, channels), full)] * 2 + [((1, channels, channels), full)]
@@ -1626,32 +1661,125 @@
     return Results(*found)
 
 
+def finish_body(row_count, states, tap_count, *refs):
+    width = row_count // CHUNKS
+    count = 9
+    sources, targets = Results(*refs[:count], None, None, None), refs[count:]
+    large, (mixed_out, tokens) = targets[:6], targets[6:8]
+    (taps, coef, rate, skip, gain_one, bias_one, gain_two, bias_two) = targets[8:16]
+    held_small, held_mixed, held_tokens, load_sems, store_sems = targets[16:21]
+    passing = targets[21:]
+    tiles = held_tokens.shape[0]
+    pairs = [(sources.small, held_small), (sources.mixed_out, held_mixed)]
+    for tile in range(tiles):
+        pairs.append((sources.tokens.at[:, pl.ds(tile * LANES, LANES)], held_tokens.at[tile]))
+    loads, stores = [], []
+    for source, held, target in zip(sources[:6], passing, large):
+        size = PASSING_SIZE // target.shape[1]
+        for start in range(0, target.shape[0], size):
+            rows = pl.ds(start, size)
+            stores.append((held.at[rows, :], target.at[rows, :]))
+            loads.append((source.at[rows, :], held.at[rows, :]))
+    stores = [pltpu.make_async_copy(*pair, store_sems.at[i]) for i, pair in enumerate(stores)]
+    copies = [pltpu.make_async_copy(*pair, load_sems.at[i]) for i, pair in enumerate(pairs + loads)]
+    first_large = len(pairs)
+    for copy in copies[first_large:] + copies[:first_large]:
+        copy.start()
+    moves = list(zip(copies[first_large:], stores))
+
+    def move(some):
+        for load, store in some:
+            load.wait()
+            store.start()
+
+    move(moves[: len(moves) // 2])
+    copies[0].wait()
+    misc = 2 * states
+    first = misc + tap_count
+    coef[...] = held_small[0:states, :]
+    rate[...] = held_small[states:misc, :]
+    taps[...] = held_small[misc:first, :]
+    for row, target in enumerate((skip, gain_one, bias_one, gain_two, bias_two)):
+        target[...] = held_small[first + row, :]
+    for copy in copies[1:first_large]:
+        copy.wait()
+
+    def body(chunk, unused):
+        rows = row_block(chunk, width)
+        for tile in range(tiles):
+            tokens[rows, tile * LANES : (tile + 1) * LANES] = held_tokens.at[tile][
+                pl.ds(chunk, width, stride=CHUNKS), :
+            ]
+        return unused
+
+    lax.fori_loop(0, CHUNKS, body, 0)
+    token = lax.broadcasted_iota(jnp.int32, (128, row_count), 0)
+    row = lax.broadcasted_iota(jnp.int32, (128, row_count), 1)
+    for i in range(row_count // 128):
+        at = token + i * 128
+        chosen = row == lax.rem(at, width) * CHUNKS + lax.div(at, width)
+        picks = jnp.where(chosen, 1.0, 0.0).astype(jnp.bfloat16)
+        mixed_out[i * 128 : (i + 1) * 128, :] = jnp.dot(
+            picks, held_mixed[...], preferred_element_type=jnp.float32
+        ).astype(jnp.bfloat16)
+    move(moves[len(moves) // 2 :])
+    for store in stores:
+        store.wait()
+
+
+PASSING_SIZE = 384 * 768
+
+
+def finish(row_count, states, tap_count, found):
+    channels = found.small.shape[1]
+    full = jnp.float32
+    wide = (row_count, channels)
+    shapes = [(array.shape, full) for array in found[:6]]
+    shapes += [(wide, jnp.bfloat16), (wide, full), ((tap_count, channels), full)]
+    shapes += [((states, channels), full)] * 2 + [((channels,), full)] * 5
+    tiles = channels // LANES
+    scratch = [(found.small.shape, full), (wide, jnp.bfloat16), ((tiles, row_count, LANES), full)]
+    pieces = sum(array.size // PASSING_SIZE for array in found[:6])
+    counts = [2 + tiles + pieces, pieces]
+    memory = [pltpu.HBM] * 6 + [pltpu.VMEM] * 10
+    return pl.pallas_call(
+        functools.partial(finish_body, row_count, states, tap_count),
+        out_shape=[jax.ShapeDtypeStruct(*shape) for shape in shapes],
+        in_specs=[pl.BlockSpec(memory_space=pltpu.HBM)] * 9,
+        out_specs=[pl.BlockSpec(memory_space=space) for space in memory],
+        scratch_shapes=[pltpu.VMEM(*shape) for shape in scratch]
+        + [pltpu.SemaphoreType.DMA((count,)) for count in counts]
+        + [pltpu.VMEM(array.shape, full) for array in found[:6]],
+        compiler_params=pltpu.CompilerParams(vmem_limit_bytes=VMEM_LIMIT),
+    )(*found[:9])
+
+
 PLAN = [
-    [(True, False), (False, False), (False, True), (True, True), (True, False), (True, False), (False, True), (False, False)],
-    [(False, False), (True, True), (False, False), (True, False), (False, False), (False, True), (False, False), (True, True)],
-    [(True, False), (True, False)],
+    [(True, False), (True, True), (True, True), (True, False), (True, False), (False, True), (True, False), (False, False)],
+    [(True, False), (True, True), (False, False), (False, False), (False, True), (True, True), (True, False), (False, False)],
+    [(False, True), (False, False)],
     [(True, False), (False, False)],
     [(True, False), (True, False)],
     [(False, True), (False, False)],
     [(False, False)],
 ]
 ORDER = [
-    25, 25, 25, 25, 25, 25, 25, 25, 25, 25, 25, 25, 8, 25, 25, 25, 25, 0, 9, 1, 8, 25, 25, 25,
-    0, 25, 9, 25, 1, 25, 25, 25, 10, 25, 25, 8, 25, 10, 25, 11, 3, 2, 25, 0, 25, 9, 25, 11, 25,
-    3, 8, 25, 1, 2, 25, 9, 25, 25, 12, 25, 25, 25, 25, 12, 4, 5, 13, 25, 11, 9, 3, 10, 25, 4,
-    25, 1, 5, 0, 25, 13, 9, 25, 3, 25, 25, 25, 8, 14, 25, 10, 25, 6, 12, 3, 15, 7, 14, 25, 6,
-    11, 15, 9, 2, 4, 7, 8, 25, 25, 2, 25, 1, 5, 8, 14, 9, 25, 25, 0, 12, 2, 4, 25, 3, 16, 1, 17,
-    25, 25, 0, 16, 13, 1, 17, 7, 8, 25, 14, 25, 0, 9, 5, 13, 25, 3, 2, 10, 25, 25, 16, 13, 6,
-    25, 1, 8, 10, 25, 0, 3, 25, 6, 11, 17, 10, 25, 25, 16, 25, 25, 18, 13, 19, 25, 7, 2, 6, 18,
-    11, 19, 15, 1, 11, 15, 0, 17, 3, 12, 15, 10, 4, 25, 13, 2, 6, 14, 12, 9, 4, 18, 19, 12, 15,
-    5, 14, 11, 16, 25, 9, 25, 6, 4, 13, 7, 25, 5, 10, 14, 25, 17, 19, 2, 25, 16, 25, 12, 9, 3,
-    25, 18, 15, 7, 25, 5, 19, 25, 25, 6, 4, 11, 13, 17, 25, 2, 25, 18, 16, 25, 14, 25, 3, 25,
-    12, 15, 25, 7, 19, 25, 25, 4, 15, 5, 25, 6, 13, 25, 7, 25, 16, 17, 25, 18, 25, 2, 25, 25, 5,
-    25, 25, 14, 25, 3, 25, 21, 20, 19, 21, 20, 16, 7, 25, 25, 15, 25, 25, 25, 25, 6, 17, 19, 25,
-    25, 25, 25, 23, 22, 25, 13, 25, 25, 23, 25, 22, 21, 18, 25, 25, 19, 25, 25, 25, 2, 25, 25,
-    25, 25, 25, 20, 15, 25, 25, 25, 22, 25, 23, 25, 25, 6, 25, 25, 25, 21, 25, 22, 24, 25, 25,
-    13, 17, 24, 18, 21, 23, 15, 20, 6, 21, 23, 24, 18, 22, 20, 24, 23, 22, 21, 24, 22, 20, 23,
-    22, 24, 21, 22, 20, 23, 24, 20, 22, 21, 22, 24, 23, 22, 24, 20,
+    25, 25, 25, 25, 25, 25, 25, 25, 25, 25, 25, 25, 8, 25, 25, 25, 25, 0, 9, 1, 25, 25, 8, 25,
+    25, 25, 0, 25, 9, 1, 25, 25, 10, 25, 25, 25, 25, 3, 11, 25, 25, 8, 10, 25, 25, 3, 25, 25, 9,
+    11, 25, 25, 8, 12, 25, 0, 25, 25, 25, 4, 13, 5, 25, 12, 9, 25, 25, 25, 4, 10, 25, 1, 13, 3,
+    5, 25, 9, 25, 25, 14, 25, 25, 7, 1, 15, 11, 8, 6, 25, 4, 14, 0, 7, 25, 1, 8, 10, 3, 15, 9,
+    12, 6, 25, 4, 25, 8, 11, 25, 12, 25, 25, 16, 7, 25, 13, 1, 14, 12, 25, 16, 25, 15, 25, 9,
+    13, 6, 25, 8, 1, 5, 7, 25, 13, 25, 12, 15, 0, 9, 14, 5, 25, 25, 8, 1, 10, 6, 25, 0, 12, 13,
+    3, 5, 25, 25, 9, 25, 25, 18, 4, 19, 2, 17, 1, 10, 25, 12, 13, 5, 11, 0, 18, 3, 19, 2, 5, 17,
+    25, 12, 16, 13, 4, 18, 10, 5, 0, 7, 3, 11, 25, 25, 13, 15, 19, 25, 10, 25, 16, 4, 14, 25,
+    25, 11, 6, 25, 25, 0, 9, 7, 18, 25, 25, 16, 1, 19, 5, 25, 3, 25, 15, 11, 25, 25, 7, 25, 14,
+    25, 10, 25, 6, 25, 12, 4, 3, 25, 9, 16, 7, 25, 25, 13, 15, 25, 1, 25, 18, 14, 11, 25, 4, 25,
+    16, 25, 19, 6, 25, 25, 25, 21, 20, 2, 17, 15, 5, 12, 16, 7, 25, 25, 21, 25, 20, 9, 25, 18,
+    14, 25, 25, 25, 13, 25, 19, 6, 25, 25, 22, 23, 25, 1, 25, 25, 21, 25, 25, 22, 25, 23, 15,
+    25, 25, 25, 16, 25, 25, 12, 5, 20, 25, 25, 25, 21, 25, 25, 18, 25, 25, 22, 25, 25, 25, 25,
+    13, 25, 14, 25, 25, 25, 23, 22, 19, 24, 2, 17, 20, 24, 16, 6, 21, 18, 5, 23, 17, 24, 22, 19,
+    20, 21, 2, 22, 23, 17, 16, 18, 20, 24, 21, 19, 2, 22, 23, 24, 17, 22, 21, 2, 24, 16, 22, 17,
+    2, 20, 23, 24, 21, 2, 17, 22, 23, 20, 24, 2, 22, 2, 23, 20, 22, 24, 2,
 ]
 
 
@@ -1674,18 +1802,17 @@
     out_grad,
 ):
     unused, row_count, channels = tokens.shape
-    width = row_count // CHUNKS
     states = ssm_rate.shape[0]
     tap_count = shift_taps.shape[0]
 
-    def token_order(values):
-        return values.reshape(width, CHUNKS, channels).swapaxes(0, 1).reshape(1, row_count, channels)
-
-    vectors = jnp.stack([ssm_skip, norm1_gain, norm1_bias, norm2_gain, norm2_bias])
     arrays = SimpleNamespace(
         tokens=tokens[0],
         token_grads=out_grad[0],
-        vectors=jnp.concatenate([vectors, jnp.zeros_like(vectors[:3])], axis=0),
+        skip=ssm_skip,
+        gain_one=norm1_gain,
+        bias_one=norm1_bias,
+        gain_two=norm2_gain,
+        bias_two=norm2_bias,
         query_weight=query_weight,
         key_weight=key_weight,
         value_weight=value_weight,
@@ -1698,26 +1825,27 @@
     )
     vars(arrays).update(forward(row_count, arrays)._asdict())
     found = backward(row_count, arrays, PLAN, ORDER)
-    small = found.small
-    misc = 2 * states
-    first = misc + tap_count
+    (down, up, out, query, value, key, mixed_out, grad_tokens, *rest) = finish(
+        row_count, states, tap_count, found
+    )
+    (taps, coef, rate, skip, gain_one, bias_one, gain_two, bias_two) = rest
     return (
-        token_order(found.mixed_out),
-        token_order(found.tokens),
-        small[first + 1],
-        small[first + 2],
-        found.query,
-        found.key,
-        found.value,
-        small[misc:first],
-        small[:states],
-        small[states:misc],
-        small[first],
-        found.out,
-        small[first + 3],
-        small[first + 4],
-        found.up,
-        found.down,
+        mixed_out[None],
+        grad_tokens[None],
+        gain_one,
+        bias_one,
+        query,
+        key,
+        value,
+        taps,
+        coef,
+        rate,
+        skip,
+        out,
+        gain_two,
+        bias_two,
+        up,
+        down,
     )
 
 

time: 326 us -> 307 us (0.942)
  local copies, waits for them, and re-layouts: 33.5 us -> 0 us
  Pallas kernels: 290 us -> 305 us
    pallas_call x0 -> x1, Pallas kernels: none -> 23.4 us  [finish(): pl.pallas_call(functools.partial(finish_body, row_count, states, tap_coun...]
    unnamed x26 -> x0, local copies, waits for them, and re-layouts: 20.2 us -> none
    pallas_call x1, Pallas kernels: 244 us -> 235 us  [backward(): pl.pallas_call(functools.partial(backward_body, row_count, size, line, bi...]
    slice x3 -> x0, local copies, waits for them, and re-layouts: 4.86 us -> none  [the longest x1 1.94 us: on_device(): small[states:misc]]
    transpose x2 -> x0, local copies, waits for them, and re-layouts: 4.42 us -> none  [token_order(): values.reshape(width, CHUNKS, channels).swapaxes(0, 1)]
    another operation x5 -> x0, local copies, waits for them, and re-layouts: 3.45 us -> none  [on_device(): jnp.stack([ssm_skip, norm1_gain, norm1_bias, norm2_gain, norm2_bias])]
where the time goes in v5:
time: 307 us; the launch traced here: 306 us
  Pallas kernels  305 us (99%)
    pallas_call x1, Pallas kernels, backward(): pl.pallas_call(functools.partial(backward_body, row_count, size, line, bi...  235 us
    pallas_call x1, Pallas kernels, forward(): pl.pallas_call(functools.partial(forward_body, row_count, size, bits), ou...  46.5 us
    pallas_call x1, Pallas kernels, finish(): pl.pallas_call(functools.partial(finish_body, row_count, states, tap_coun...  23.4 us

profile of v5, /device:TPU:0, one launch (start us, length us, event | category | flops | bytes accessed | tf_op | source)
XLA Modules:
  0.0 306.1 jit_solution(934352147981997841)
XLA Ops:
  0.6 46.5 %shard_map.279 = (f32[512,768]{1,0:T(8,128)}, f32[6,1024,128]{2,1,0:T(8,128)}, f32[32,768]{1,0:T(8,128)}, f32[512,768]{1,0:T(8,128)}, f32[512,768]{1,0:T(8,128)}...) custom-call(bf16[512,768]{1,0:T(8,128)(2,1)} %bitcast.4, ...), custom_call_target="tpu_custom_call" | custom-call | tf_op jit(solution)/shard_map/pallas_call | solution.py:1047
  47.1 235.4 %shard_map.280 = (f32[3072,768]{1,0:T(8,128)}, f32[768,3072]{1,0:T(8,128)}, f32[768,768]{1,0:T(8,128)}, f32[768,768]{1,0:T(8,128)}, f32[768,768]{1,0:T(8,128)}, ...) custom-call(bf16[768,3072]{1,0:T(8,128)(2,1)} %refs_0_.1, ...), custom_call_target="tpu_custom_call" | custom-call | tf_op jit(solution)/shard_map/pallas_call | solution.py:1647
  282.6 23.4 %shard_map.281 = (f32[3072,768]{1,0:T(8,128)}, f32[768,3072]{1,0:T(8,128)}, f32[768,768]{1,0:T(8,128)}, f32[768,768]{1,0:T(8,128)}, f32[768,768]{1,0:T(8,128)}, ...) custom-call(f32[3072,768]{1,0:T(8,128)} %get-tuple-element.77.refs_0, ...), custom_call_target="tpu_custom_call" | custom-call | tf_op jit(solution)/shard_map/pallas_call | solution.py:1745

commit v6 on v5

--- a/solution.py
+++ b/solution.py
@@ -725,8 +725,8 @@
         return pltpu.make_async_remote_copy(
             src_ref=totals[level],
             dst_ref=arrivals[level],
-            send_sem=sends.at[level],
-            recv_sem=receives.at[level],
+            send_sem=sends[level],
+            recv_sem=receives[level],
             device_id=(me + bit * (1 - 2 * ((me // bit) % 2)), z),
             device_id_type=MESH,
         )
@@ -810,6 +810,7 @@
     results = ForwardOut(*refs[taken : taken + outs])
     own = ForwardOut(*refs[taken + outs : taken + 2 * outs])
     refs = refs[taken + 2 * outs :]
+    brought, refs = refs[:4], refs[4:]
     sums, taps, decay, entering, edge_out, edge_in = refs[:6]
     totals, arrivals = refs[6 : 6 + levels], refs[6 + levels : 6 + 2 * levels]
     sends, receives, keeps = refs[-3:]
@@ -838,16 +839,36 @@
         ]
     )
 
-    copy, arrive = state_exchange(
-        bits, row_count, rate, totals, arrivals, entering, sends, receives, True
-    )
+    def half_exchange(part):
+        size_of = channels // 2
+        here = pl.ds(part * size_of, size_of)
+        first = part * levels
+        return state_exchange(
+            bits,
+            row_count,
+            rate.at[:, here],
+            [total.at[:, here] for total in totals],
+            [arrival.at[:, here] for arrival in arrivals],
+            entering.at[:, here],
+            [sends.at[first + level] for level in range(levels)],
+            [receives.at[first + level] for level in range(levels)],
+            True,
+        )
+
+    halves = [half_exchange(0), half_exchange(1)]
+
+    def begin_half(part):
+        return halves[part][0](0).start
+
+    def arrive_half(part, level):
+        return functools.partial(halves[part][1], level)
 
     def edge(device):
         return pltpu.make_async_remote_copy(
             src_ref=edge_out,
             dst_ref=edge_in,
-            send_sem=sends.at[levels],
-            recv_sem=receives.at[levels],
+            send_sem=sends.at[2 * levels],
+            recv_sem=receives.at[2 * levels],
             device_id=(device, z),
             device_id_type=MESH,
         )
@@ -859,6 +880,14 @@
         chosen = lax.broadcasted_iota(jnp.int32, shape, 1) == token
         picks = jnp.where(chosen, 1.0, 0.0).astype(low)
         return jnp.dot(picks, rows[...], preferred_element_type=jnp.float32)
+
+    far = (given.key_weight, given.value_weight, given.query_weight, given.out_weight)
+    weights = [
+        pltpu.make_async_copy(far[i], brought[i], keeps.at[len(ForwardOut._fields) + i])
+        for i in range(4)
+    ]
+    for weight in weights:
+        weight.start()
 
     def norm_rows(i):
         rows = row_block(i, 128)
@@ -957,7 +986,7 @@
         gated = (own.queries[rows, :] * own.mixed[rows, :]).astype(low)
         own.gated[rows, :] = gated
         middle = own.middle[rows, :] + jnp.dot(
-            gated, given.out_weight[...], preferred_element_type=jnp.float32
+            gated, brought[3][...], preferred_element_type=jnp.float32
         )
         own.middle[rows, :] = middle
         standard, factor = standardize(middle)
@@ -982,29 +1011,44 @@
     keep_all(kept.vectors)
     loop(Loop(row_count // 128, norm_rows))
     keep_all(kept.standard_one, kept.factor_one, kept.normed_one)
-    loop(project_to(own.key_rows, given.key_weight, lead))
+    weights[0].wait()
+    loop(project_to(own.key_rows, brought[0], lead))
     send_edge()
-    loop(project_to(own.values, given.value_weight, 0))
+    weights[1].wait()
+    loop(project_to(own.values, brought[1], 0))
     keep_all(kept.values)
     take_edge()
-    loop(Loop(tiles, states_tile))
-    copy(0).start()
+    between = [[] for unused in range(tiles)]
+    between[tiles // 2 - 1].append(begin_half(0))
+    between[tiles - 2].append(arrive_half(0, 0))
+    loop(Loop(tiles, states_tile), between)
+    begin_half(1)()
     keep_all(kept.key_rows, kept.keys_mixed, kept.product)
-    loop(project_to(own.queries, given.query_weight, 0))
+    weights[2].wait()
+    loop(project_to(own.queries, brought[2], 0))
     keep_all(kept.queries)
+    arrive_half(1, 0)()
+    if levels > 1:
+        arrive_half(0, 1)()
     loop(Loop(row_count // 128, grad_rows))
     keep_all(kept.out_grad)
     between = [[] for unused in range(tiles)]
-    for level in range(levels):
-        between[level * tiles // levels].append(functools.partial(arrive, level))
+    for level in range(1, levels):
+        if level + 1 < levels:
+            between[max(0, level * tiles // levels - 1)].append(arrive_half(0, level + 1))
+            between[max(0, level * tiles // levels - 1)].insert(0, arrive_half(1, level))
+        else:
+            between[tiles - 1].append(arrive_half(1, level))
     loop(Loop(tiles, near_tile), between)
     keep_all(kept.kernel)
     loop(Loop(tiles, far_tile))
     keep_all(kept.mixed, kept.held)
+    weights[3].wait()
     loop(Loop(row_count // 128, out_rows))
     keep_all(kept.gated, kept.middle, kept.normed_two, kept.standard_two, kept.factor_two)
-    for level in range(levels):
-        copy(level).wait_send()
+    for copy, unused in halves:
+        for level in range(levels):
+            copy(level).wait_send()
     pl.when(me < size - 1)(edge(me + 1).wait_send)
     for one in kept:
         one.wait()
@@ -1041,13 +1085,18 @@
         out_grad=low_square,
         vectors=((8, channels), full),
     )
-    scratch = list(outs) + [held, thin, ((states, LANES), full), ((states, channels), full)]
+    square_low = (channels, channels)
+    weights = [(square_low, low)] * 4
+    scratch = list(outs) + weights + [held, thin, ((states, LANES), full), ((states, channels), full)]
     scratch += [((8, channels), full)] * 2 + [((states, channels), full)] * (2 * len(bits))
-    counts = [len(bits) + 1, len(bits) + 1, len(outs)]
+    counts = [2 * len(bits) + 1, 2 * len(bits) + 1, len(outs) + 4]
     found = pl.pallas_call(
         functools.partial(forward_body, row_count, size, bits),
         out_shape=[jax.ShapeDtypeStruct(*out) for out in outs],
-        in_specs=[pl.BlockSpec(memory_space=pltpu.VMEM)] * len(ForwardIn._fields),
+        in_specs=[
+            pl.BlockSpec(memory_space=pltpu.HBM if shape == square_low else pltpu.VMEM)
+            for shape in (getattr(arrays, name).shape for name in ForwardIn._fields)
+        ],
         out_specs=[pl.BlockSpec(memory_space=pltpu.HBM)] * len(outs),
         scratch_shapes=[pltpu.VMEM(*shape) for shape in scratch]
         + [pltpu.SemaphoreType.DMA((count,)) for count in counts],
@@ -1187,7 +1236,15 @@
         small[row : row + 1, :] += jnp.sum(value, axis=0, keepdims=True)
 
     exchange, arrive = state_exchange(
-        bits, row_count, rate, totals, arrivals, entering, swap_send, swap_recv, False
+        bits,
+        row_count,
+        rate,
+        totals,
+        arrivals,
+        entering,
+        [swap_send.at[level] for level in range(levels)],
+        [swap_recv.at[level] for level in range(levels)],
+        False,
     )
 
     def edge(device):
@@ -1683,16 +1740,16 @@
     stores = [pltpu.make_async_copy(*pair, store_sems.at[i]) for i, pair in enumerate(stores)]
     copies = [pltpu.make_async_copy(*pair, load_sems.at[i]) for i, pair in enumerate(pairs + loads)]
     first_large = len(pairs)
-    for copy in copies[first_large:] + copies[:first_large]:
+    for copy in copies:
         copy.start()
     moves = list(zip(copies[first_large:], stores))
 
-    def move(some):
-        for load, store in some:
+    def move(count):
+        for load, store in moves[:count]:
             load.wait()
             store.start()
-
-    move(moves[: len(moves) // 2])
+        del moves[:count]
+
     copies[0].wait()
     misc = 2 * states
     first = misc + tap_count
@@ -1704,15 +1761,14 @@
     for copy in copies[1:first_large]:
         copy.wait()
 
-    def body(chunk, unused):
-        rows = row_block(chunk, width)
+    for chunk in range(CHUNKS):
+        rows = slice(chunk * width, (chunk + 1) * width)
         for tile in range(tiles):
             tokens[rows, tile * LANES : (tile + 1) * LANES] = held_tokens.at[tile][
                 pl.ds(chunk, width, stride=CHUNKS), :
             ]
-        return unused
-
-    lax.fori_loop(0, CHUNKS, body, 0)
+        if chunk % 2:
+            move(1)
     token = lax.broadcasted_iota(jnp.int32, (128, row_count), 0)
     row = lax.broadcasted_iota(jnp.int32, (128, row_count), 1)
     for i in range(row_count // 128):
@@ -1722,7 +1778,8 @@
         mixed_out[i * 128 : (i + 1) * 128, :] = jnp.dot(
             picks, held_mixed[...], preferred_element_type=jnp.float32
         ).astype(jnp.bfloat16)
-    move(moves[len(moves) // 2 :])
+        move(2)
+    move(len(moves))
     for store in stores:
         store.wait()
 
@@ -1755,31 +1812,31 @@
 
 
 PLAN = [
-    [(True, False), (True, True), (True, True), (True, False), (True, False), (False, True), (True, False), (False, False)],
-    [(True, False), (True, True), (False, False), (False, False), (False, True), (True, True), (True, False), (False, False)],
+    [(True, False), (True, False), (True, True), (False, False), (False, False), (True, False), (True, False), (True, False)],
+    [(False, False), (True, True), (False, False), (False, True), (False, False), (True, True), (False, True), (False, False)],
+    [(True, False), (False, True)],
     [(False, True), (False, False)],
     [(True, False), (False, False)],
-    [(True, False), (True, False)],
-    [(False, True), (False, False)],
+    [(False, True), (True, False)],
     [(False, False)],
 ]
 ORDER = [
-    25, 25, 25, 25, 25, 25, 25, 25, 25, 25, 25, 25, 8, 25, 25, 25, 25, 0, 9, 1, 25, 25, 8, 25,
-    25, 25, 0, 25, 9, 1, 25, 25, 10, 25, 25, 25, 25, 3, 11, 25, 25, 8, 10, 25, 25, 3, 25, 25, 9,
-    11, 25, 25, 8, 12, 25, 0, 25, 25, 25, 4, 13, 5, 25, 12, 9, 25, 25, 25, 4, 10, 25, 1, 13, 3,
-    5, 25, 9, 25, 25, 14, 25, 25, 7, 1, 15, 11, 8, 6, 25, 4, 14, 0, 7, 25, 1, 8, 10, 3, 15, 9,
-    12, 6, 25, 4, 25, 8, 11, 25, 12, 25, 25, 16, 7, 25, 13, 1, 14, 12, 25, 16, 25, 15, 25, 9,
-    13, 6, 25, 8, 1, 5, 7, 25, 13, 25, 12, 15, 0, 9, 14, 5, 25, 25, 8, 1, 10, 6, 25, 0, 12, 13,
-    3, 5, 25, 25, 9, 25, 25, 18, 4, 19, 2, 17, 1, 10, 25, 12, 13, 5, 11, 0, 18, 3, 19, 2, 5, 17,
-    25, 12, 16, 13, 4, 18, 10, 5, 0, 7, 3, 11, 25, 25, 13, 15, 19, 25, 10, 25, 16, 4, 14, 25,
-    25, 11, 6, 25, 25, 0, 9, 7, 18, 25, 25, 16, 1, 19, 5, 25, 3, 25, 15, 11, 25, 25, 7, 25, 14,
-    25, 10, 25, 6, 25, 12, 4, 3, 25, 9, 16, 7, 25, 25, 13, 15, 25, 1, 25, 18, 14, 11, 25, 4, 25,
-    16, 25, 19, 6, 25, 25, 25, 21, 20, 2, 17, 15, 5, 12, 16, 7, 25, 25, 21, 25, 20, 9, 25, 18,
-    14, 25, 25, 25, 13, 25, 19, 6, 25, 25, 22, 23, 25, 1, 25, 25, 21, 25, 25, 22, 25, 23, 15,
-    25, 25, 25, 16, 25, 25, 12, 5, 20, 25, 25, 25, 21, 25, 25, 18, 25, 25, 22, 25, 25, 25, 25,
-    13, 25, 14, 25, 25, 25, 23, 22, 19, 24, 2, 17, 20, 24, 16, 6, 21, 18, 5, 23, 17, 24, 22, 19,
-    20, 21, 2, 22, 23, 17, 16, 18, 20, 24, 21, 19, 2, 22, 23, 24, 17, 22, 21, 2, 24, 16, 22, 17,
-    2, 20, 23, 24, 21, 2, 17, 22, 23, 20, 24, 2, 22, 2, 23, 20, 22, 24, 2,
+    25, 25, 25, 25, 25, 25, 25, 25, 25, 25, 25, 25, 8, 25, 25, 25, 25, 9, 1, 0, 25, 25, 8, 25,
+    25, 25, 9, 25, 1, 0, 25, 25, 10, 25, 25, 25, 25, 2, 11, 3, 25, 25, 10, 8, 25, 25, 2, 9, 25,
+    11, 1, 25, 3, 25, 25, 12, 25, 25, 25, 9, 25, 4, 5, 13, 25, 10, 12, 0, 25, 25, 2, 4, 1, 8,
+    25, 5, 9, 13, 25, 25, 10, 25, 25, 2, 14, 25, 25, 7, 6, 15, 3, 25, 14, 11, 2, 7, 5, 25, 9,
+    12, 6, 15, 25, 11, 1, 2, 0, 3, 25, 8, 25, 25, 25, 7, 17, 11, 1, 4, 25, 8, 5, 13, 25, 17, 9,
+    12, 25, 1, 25, 10, 13, 8, 25, 2, 6, 15, 25, 7, 4, 13, 14, 10, 25, 9, 11, 8, 25, 1, 15, 25,
+    2, 14, 10, 0, 13, 9, 25, 11, 6, 3, 25, 25, 25, 25, 18, 19, 16, 25, 14, 0, 5, 1, 18, 8, 13,
+    19, 2, 16, 17, 0, 3, 10, 25, 11, 14, 5, 13, 12, 3, 16, 7, 5, 17, 19, 25, 14, 4, 25, 17, 0,
+    13, 25, 12, 15, 25, 3, 25, 9, 25, 7, 19, 11, 10, 25, 14, 6, 4, 25, 12, 25, 25, 5, 25, 18,
+    17, 15, 0, 25, 7, 25, 12, 25, 9, 25, 2, 25, 4, 3, 25, 14, 25, 17, 6, 5, 13, 25, 7, 15, 25,
+    18, 19, 17, 4, 25, 9, 25, 11, 25, 12, 25, 2, 17, 25, 25, 25, 7, 25, 25, 21, 20, 16, 14, 6,
+    15, 25, 25, 21, 25, 20, 4, 25, 13, 25, 25, 19, 6, 25, 18, 25, 25, 25, 22, 23, 25, 11, 25,
+    25, 25, 25, 22, 20, 15, 25, 2, 23, 25, 25, 25, 25, 25, 17, 25, 25, 25, 21, 6, 25, 25, 25,
+    14, 25, 18, 22, 25, 25, 25, 25, 13, 25, 20, 25, 24, 25, 25, 23, 19, 22, 16, 24, 21, 20, 18,
+    11, 23, 19, 16, 17, 18, 21, 24, 20, 14, 23, 24, 21, 22, 19, 24, 23, 16, 18, 22, 17, 24, 22,
+    16, 20, 22, 21, 20, 23, 22, 16, 18, 21, 24, 23, 22, 20, 18, 24, 21, 22, 18, 24, 23, 22,
 ]
 
 

time: 307 us -> 296 us (0.964)
  Pallas kernels: 305 us -> 294 us
    pallas_call x1, Pallas kernels: 46.5 us -> 39.8 us  [forward(): pl.pallas_call(functools.partial(forward_body, row_count, size, bits), ou...]
where the time goes in v6:
time: 296 us; the launch traced here: 295 us
  Pallas kernels  294 us (99%)
    pallas_call x1, Pallas kernels, backward(): pl.pallas_call(functools.partial(backward_body, row_count, size, line, bi...  232 us
    pallas_call x1, Pallas kernels, forward(): pl.pallas_call(functools.partial(forward_body, row_count, size, bits), ou...  39.8 us
    pallas_call x1, Pallas kernels, finish(): pl.pallas_call(functools.partial(finish_body, row_count, states, tap_coun...  21.8 us

profile of v6, /device:TPU:0, one launch (start us, length us, event | category | flops | bytes accessed | tf_op | source)
XLA Modules:
  0.0 294.9 jit_solution(10271801606714062278)
XLA Ops:
  0.6 39.8 %shard_map.279 = (f32[512,768]{1,0:T(8,128)}, f32[6,1024,128]{2,1,0:T(8,128)}, f32[32,768]{1,0:T(8,128)}, f32[512,768]{1,0:T(8,128)}, f32[512,768]{1,0:T(8,128)}...) custom-call(bf16[512,768]{1,0:T(8,128)(2,1)} %bitcast.4, ...), custom_call_target="tpu_custom_call" | custom-call | tf_op jit(solution)/shard_map/pallas_call | solution.py:1093
  40.5 232.5 %shard_map.280 = (f32[3072,768]{1,0:T(8,128)}, f32[768,3072]{1,0:T(8,128)}, f32[768,768]{1,0:T(8,128)}, f32[768,768]{1,0:T(8,128)}, f32[768,768]{1,0:T(8,128)}, ...) custom-call(bf16[768,3072]{1,0:T(8,128)(2,1)} %refs_0_.1, ...), custom_call_target="tpu_custom_call" | custom-call | tf_op jit(solution)/shard_map/pallas_call | solution.py:1704
  272.9 21.8 %shard_map.281 = (f32[3072,768]{1,0:T(8,128)}, f32[768,3072]{1,0:T(8,128)}, f32[768,768]{1,0:T(8,128)}, f32[768,768]{1,0:T(8,128)}, f32[768,768]{1,0:T(8,128)}, ...) custom-call(f32[3072,768]{1,0:T(8,128)} %get-tuple-element.77.refs_0, ...), custom_call_target="tpu_custom_call" | custom-call | tf_op jit(solution)/shard_map/pallas_call | solution.py:1802

commit v7 on v6

--- a/solution.py
+++ b/solution.py
@@ -1235,24 +1235,30 @@
     def add_small(row, value):
         small[row : row + 1, :] += jnp.sum(value, axis=0, keepdims=True)
 
-    exchange, arrive = state_exchange(
-        bits,
-        row_count,
-        rate,
-        totals,
-        arrivals,
-        entering,
-        [swap_send.at[level] for level in range(levels)],
-        [swap_recv.at[level] for level in range(levels)],
-        False,
-    )
+    def half_exchange(part):
+        size_of = channels // 2
+        here = pl.ds(part * size_of, size_of)
+        first = part * levels
+        return state_exchange(
+            bits,
+            row_count,
+            rate.at[:, here],
+            [ref.at[:, here] for ref in totals],
+            [ref.at[:, here] for ref in arrivals],
+            entering.at[:, here],
+            [swap_send.at[first + level] for level in range(levels)],
+            [swap_recv.at[first + level] for level in range(levels)],
+            False,
+        )
+
+    halves = [half_exchange(0), half_exchange(1)]
 
     def edge(device):
         return pltpu.make_async_remote_copy(
             src_ref=edge_out,
             dst_ref=edge_in,
-            send_sem=swap_send.at[levels],
-            recv_sem=swap_recv.at[levels],
+            send_sem=swap_send.at[2 * levels],
+            recv_sem=swap_recv.at[2 * levels],
             device_id=(device, z),
             device_id_type=MESH,
         )
@@ -1411,14 +1417,16 @@
                 totals[0].at[:, here],
                 decay,
             )
+            pl.when(tile == tiles // 2 - 1)(halves[0][0](0).start)
 
         def start_tiles():
             for copy in tile_loads(0):
                 copy.start()
-            exchange(0).start()
+            halves[1][0](0).start()
 
         def near(tile):
             here, slot = lane_columns(tile), tile % 2
+            pl.when(tile == tiles // 2)(functools.partial(halves[1][1], levels - 1))
             for copy in tile_loads(tile):
                 copy.wait()
 
@@ -1553,7 +1561,9 @@
         work = [Loop(tiles, first_tile), start_tiles]
         work.append(weight_sum(grad_query, grad_queries))
         for level in range(levels):
-            work.append(functools.partial(arrive, level))
+            work.append(functools.partial(halves[0][1], level))
+            if level < levels - 1:
+                work.append(functools.partial(halves[1][1], level))
         work.append(Loop(tiles, near, far(0), far(1), end))
         work.append(send_edge)
         work.append(weight_sum(grad_value, values_low))
@@ -1587,7 +1597,7 @@
         source = (grad_query, grad_value, grad_key, small)[lane.array - 3]
         return source.at[:, cols], results[lane.array].at[:, cols]
 
-    pending = [exchange(level).wait_send for level in range(levels)]
+    pending = [copy(level).wait_send for copy, unused in halves for level in range(levels)]
     pending.append(lambda: pl.when(me > 0)(edge(me - 1).wait_send))
     programs = []
     start = 0
@@ -1659,7 +1669,7 @@
 def work_steps(row_count, channels, hidden, levels):
     tiles, weights = channels // LANES, channels // 256
     first = 2 + 4 * (hidden // HIDDEN_AT_ONCE) + 2 * (row_count // 128) + weights
-    second = 6 * tiles + 3 * weights + levels + 6 + 3 * (row_count // 128)
+    second = 6 * tiles + 3 * weights + 2 * levels + 5 + 3 * (row_count // 128)
     return first + second + row_count // ROWS_AT_ONCE + 3
 
 
@@ -1697,7 +1707,7 @@
     scratch = [pltpu.VMEM(*shape) for shape in scratch]
     scratch += [buffer for lane in lanes for buffer in lane.buffers(line)]
     copies = sum(lane.copies(line) for lane in lanes)
-    counts = [21 + STAGES, len(bits) + 1, len(bits) + 1]
+    counts = [21 + STAGES, 2 * len(bits) + 1, 2 * len(bits) + 1]
     outs = [((hidden, channels), full), ((channels, hidden), full)] + [square] * 4
     outs += [small, wide, low_wide]
     outs += [((parts, channels, channels), full)] * 2 + [((1, channels, channels), full)]
@@ -1812,31 +1822,31 @@
 
 
 PLAN = [
-    [(True, False), (True, False), (True, True), (False, False), (False, False), (True, False), (True, False), (True, False)],
-    [(False, False), (True, True), (False, False), (False, True), (False, False), (True, True), (False, True), (False, False)],
-    [(True, False), (False, True)],
-    [(False, True), (False, False)],
+    [(False, False), (True, False), (True, False), (True, True), (True, False), (True, True), (True, True), (True, False)],
+    [(True, False), (True, True), (False, True), (False, True), (False, False), (False, False), (True, False), (False, False)],
+    [(False, False), (False, True)],
+    [(False, False), (True, True)],
     [(True, False), (False, False)],
-    [(False, True), (True, False)],
+    [(True, False), (False, False)],
     [(False, False)],
 ]
 ORDER = [
     25, 25, 25, 25, 25, 25, 25, 25, 25, 25, 25, 25, 8, 25, 25, 25, 25, 9, 1, 0, 25, 25, 8, 25,
-    25, 25, 9, 25, 1, 0, 25, 25, 10, 25, 25, 25, 25, 2, 11, 3, 25, 25, 10, 8, 25, 25, 2, 9, 25,
-    11, 1, 25, 3, 25, 25, 12, 25, 25, 25, 9, 25, 4, 5, 13, 25, 10, 12, 0, 25, 25, 2, 4, 1, 8,
-    25, 5, 9, 13, 25, 25, 10, 25, 25, 2, 14, 25, 25, 7, 6, 15, 3, 25, 14, 11, 2, 7, 5, 25, 9,
-    12, 6, 15, 25, 11, 1, 2, 0, 3, 25, 8, 25, 25, 25, 7, 17, 11, 1, 4, 25, 8, 5, 13, 25, 17, 9,
-    12, 25, 1, 25, 10, 13, 8, 25, 2, 6, 15, 25, 7, 4, 13, 14, 10, 25, 9, 11, 8, 25, 1, 15, 25,
-    2, 14, 10, 0, 13, 9, 25, 11, 6, 3, 25, 25, 25, 25, 18, 19, 16, 25, 14, 0, 5, 1, 18, 8, 13,
-    19, 2, 16, 17, 0, 3, 10, 25, 11, 14, 5, 13, 12, 3, 16, 7, 5, 17, 19, 25, 14, 4, 25, 17, 0,
-    13, 25, 12, 15, 25, 3, 25, 9, 25, 7, 19, 11, 10, 25, 14, 6, 4, 25, 12, 25, 25, 5, 25, 18,
-    17, 15, 0, 25, 7, 25, 12, 25, 9, 25, 2, 25, 4, 3, 25, 14, 25, 17, 6, 5, 13, 25, 7, 15, 25,
-    18, 19, 17, 4, 25, 9, 25, 11, 25, 12, 25, 2, 17, 25, 25, 25, 7, 25, 25, 21, 20, 16, 14, 6,
-    15, 25, 25, 21, 25, 20, 4, 25, 13, 25, 25, 19, 6, 25, 18, 25, 25, 25, 22, 23, 25, 11, 25,
-    25, 25, 25, 22, 20, 15, 25, 2, 23, 25, 25, 25, 25, 25, 17, 25, 25, 25, 21, 6, 25, 25, 25,
-    14, 25, 18, 22, 25, 25, 25, 25, 13, 25, 20, 25, 24, 25, 25, 23, 19, 22, 16, 24, 21, 20, 18,
-    11, 23, 19, 16, 17, 18, 21, 24, 20, 14, 23, 24, 21, 22, 19, 24, 23, 16, 18, 22, 17, 24, 22,
-    16, 20, 22, 21, 20, 23, 22, 16, 18, 21, 24, 23, 22, 20, 18, 24, 21, 22, 18, 24, 23, 22,
+    25, 25, 9, 25, 1, 0, 25, 25, 25, 25, 25, 25, 3, 2, 11, 25, 25, 8, 25, 25, 25, 9, 3, 25, 2,
+    11, 0, 25, 25, 12, 25, 1, 25, 9, 8, 25, 25, 13, 4, 5, 25, 12, 25, 25, 25, 1, 13, 3, 2, 9, 4,
+    25, 5, 25, 25, 0, 25, 14, 25, 25, 9, 15, 12, 3, 6, 7, 25, 11, 14, 25, 15, 4, 13, 3, 6, 7,
+    25, 8, 12, 2, 11, 25, 9, 25, 1, 25, 14, 8, 25, 15, 16, 11, 17, 25, 1, 13, 5, 25, 9, 8, 4, 3,
+    16, 17, 25, 14, 25, 1, 11, 0, 5, 25, 7, 8, 25, 15, 9, 3, 25, 6, 11, 0, 5, 25, 16, 25, 8, 12,
+    11, 25, 1, 6, 2, 0, 5, 25, 25, 25, 7, 25, 18, 19, 3, 25, 16, 25, 13, 10, 11, 5, 12, 18, 6,
+    4, 19, 25, 10, 2, 25, 1, 5, 13, 12, 0, 17, 3, 2, 6, 18, 4, 25, 25, 13, 14, 25, 17, 5, 25,
+    15, 0, 25, 25, 9, 12, 4, 2, 25, 18, 6, 17, 25, 7, 25, 14, 25, 13, 16, 25, 25, 12, 11, 25,
+    25, 15, 4, 6, 2, 14, 25, 9, 17, 25, 19, 25, 25, 15, 7, 25, 13, 16, 25, 9, 4, 25, 25, 6, 11,
+    7, 17, 14, 25, 25, 15, 19, 16, 17, 25, 25, 25, 25, 25, 21, 20, 10, 7, 3, 21, 11, 14, 20, 5,
+    10, 15, 19, 16, 18, 25, 25, 17, 25, 25, 25, 6, 25, 25, 3, 25, 25, 25, 22, 23, 25, 21, 7, 5,
+    25, 25, 25, 25, 22, 25, 18, 23, 25, 25, 20, 16, 25, 25, 25, 19, 17, 25, 25, 25, 25, 25, 25,
+    21, 6, 25, 25, 3, 25, 25, 25, 23, 25, 25, 24, 5, 25, 25, 21, 20, 10, 22, 19, 24, 18, 23, 10,
+    17, 20, 21, 18, 22, 10, 6, 19, 23, 20, 10, 17, 24, 19, 22, 23, 21, 24, 20, 18, 24, 10, 21,
+    22, 19, 24, 20, 23, 10, 21, 22, 20, 19, 23, 24, 22, 10, 24, 19, 23, 10, 22, 24,
 ]
 
 

time: 296 us -> 292 us (0.986)
  Pallas kernels: 294 us -> 290 us
    pallas_call x1, Pallas kernels: 232 us -> 229 us  [backward(): pl.pallas_call(functools.partial(backward_body, row_count, size, line, bi...]
where the time goes in v7:
time: 292 us; the launch traced here: 291 us
  Pallas kernels  290 us (99%)
    pallas_call x1, Pallas kernels, backward(): pl.pallas_call(functools.partial(backward_body, row_count, size, line, bi...  229 us
    pallas_call x1, Pallas kernels, forward(): pl.pallas_call(functools.partial(forward_body, row_count, size, bits), ou...  39.8 us
    pallas_call x1, Pallas kernels, finish(): pl.pallas_call(functools.partial(finish_body, row_count, states, tap_coun...  21.8 us

profile of v7, /device:TPU:0, one launch (start us, length us, event | category | flops | bytes accessed | tf_op | source)
XLA Modules:
  0.0 291.2 jit_solution(10154883870230924617)
XLA Ops:
  0.6 39.8 %shard_map.279 = (f32[512,768]{1,0:T(8,128)}, f32[6,1024,128]{2,1,0:T(8,128)}, f32[32,768]{1,0:T(8,128)}, f32[512,768]{1,0:T(8,128)}, f32[512,768]{1,0:T(8,128)}...) custom-call(bf16[512,768]{1,0:T(8,128)(2,1)} %bitcast.4, ...), custom_call_target="tpu_custom_call" | custom-call | tf_op jit(solution)/shard_map/pallas_call | solution.py:1093
  40.5 228.8 %shard_map.280 = (f32[3072,768]{1,0:T(8,128)}, f32[768,3072]{1,0:T(8,128)}, f32[768,768]{1,0:T(8,128)}, f32[768,768]{1,0:T(8,128)}, f32[768,768]{1,0:T(8,128)}, ...) custom-call(bf16[768,3072]{1,0:T(8,128)(2,1)} %refs_0_.1, ...), custom_call_target="tpu_custom_call" | custom-call | tf_op jit(solution)/shard_map/pallas_call | solution.py:1714
  269.3 21.8 %shard_map.281 = (f32[3072,768]{1,0:T(8,128)}, f32[768,3072]{1,0:T(8,128)}, f32[768,768]{1,0:T(8,128)}, f32[768,768]{1,0:T(8,128)}, f32[768,768]{1,0:T(8,128)}, ...) custom-call(f32[3072,768]{1,0:T(8,128)} %get-tuple-element.77.refs_0, ...), custom_call_target="tpu_custom_call" | custom-call | tf_op jit(solution)/shard_map/pallas_call | solution.py:1812
